TPU v7x, 32 devices: a whole 2x2x4 slice. The times are simulated.
32 devices in a mesh: gy: 4 (over y, x), gz: 8 (over z, core).
Axes of the slice: x: 2, y: 2, z: 4, core: 2. Of those that a mesh axis runs over, the one named last changes fastest.
Arguments:
- density: float32 [1024, 128, 256], P('gy', 'gz'), may hold values from 0.5 to 2
- momentum: float32 [3, 1024, 128, 256], P(None, 'gy', 'gz'), may hold values from -3 to 3
- energy: float32 [1024, 128, 256], P('gy', 'gz'), may hold values from 2 to 4
- wall_operator: float32 [1024, 1024], replicated, may hold values from -0.1875 to 0.1875
- span_operator: float32 [128, 128], replicated, may hold values from -0.5 to 0.5
- damping: float32 [1024], replicated, may hold values from 0.1 to 1
Outputs:
- new_density: float32 [1024, 128, 256], P('gy', 'gz')
- new_momentum: float32 [3, 1024, 128, 256], P(None, 'gy', 'gz')
- new_energy: float32 [1024, 128, 256], P('gy', 'gz')
All inputs are finite; a program needn't handle non-finite values.
Results may differ from a plain program's by a relative error of at most 0.00009.
Values sent between devices are 32-bit elements; how exact they have to be, the bound alone decides.
No kernel may reach another device: no remote copies, remote signals or barrier semaphores. Data moves between devices by JAX's collectives and lax.ppermute only.
A program may use at most 320 MiB of HBM per device.

v0:
```python
import jax
import jax.numpy as jnp
from jax import lax
from jax.sharding import PartitionSpec as P

gamma_less = 0.4
time_step = 0.1


def flux_along(conserved, direction):
    velocity = conserved[1 + direction] / conserved[0]
    kinetic = (
        0.5
        * (conserved[1] * conserved[1] + conserved[2] * conserved[2] + conserved[3] * conserved[3])
        / conserved[0]
    )
    pressure = gamma_less * (conserved[4] - kinetic)
    components = [conserved[1 + direction]]
    for column in range(3):
        product = conserved[1 + column] * velocity
        if column == direction:
            product = product + pressure
        components.append(product)
    components.append((conserved[4] + pressure) * velocity)
    return jnp.stack(components)


def x_derivative(flux_field):
    widths = [(0, 0)] * (flux_field.ndim - 1) + [(2, 2)]
    padded = jnp.pad(flux_field, widths, mode="edge")
    return (
        8.0 * (padded[..., 3:-1] - padded[..., 1:-3]) - (padded[..., 4:] - padded[..., :-4])
    ) / 12.0


def fourth_difference(padded, along_axis, length_out):

    def shifted(offset):
        return lax.slice_in_dim(padded, offset, offset + length_out, axis=along_axis)

    return shifted(0) - 4.0 * shifted(1) + 6.0 * shifted(2) - 4.0 * shifted(3) + shifted(4)


def local(density, momentum, energy, wall_operator, span_operator, damping):
    conserved = jnp.concatenate([density[None], momentum, energy[None]], axis=0)
    rows_here = conserved.shape[1]
    first_row = lax.axis_index("gy") * rows_here
    local_damping = lax.dynamic_slice_in_dim(damping, first_row, rows_here)
    along_x = x_derivative(flux_along(conserved, 0))
    count_gz = lax.axis_size("gz")
    row_weights = jnp.broadcast_to(local_damping[None, :, None, None], (1, rows_here, 1, count_gz))
    pencil = lax.all_to_all(conserved, "gy", split_axis=3, concat_axis=1, tiled=True)
    upward = flux_along(pencil, 1)
    derivative = jnp.einsum("ij,fjzx->fizx", wall_operator, upward, precision=lax.Precision.HIGHEST)
    padded = jnp.pad(pencil, ((0, 0), (2, 2), (0, 0), (0, 0)))
    contrib = derivative + damping[None, :, None, None] * fourth_difference(
        padded, 1, pencil.shape[1]
    )
    wall_terms = lax.all_to_all(contrib, "gy", split_axis=1, concat_axis=3, tiled=True)
    pencil = lax.all_to_all(conserved, "gz", split_axis=3, concat_axis=2, tiled=True)
    weights = lax.all_to_all(row_weights, "gz", split_axis=3, concat_axis=2, tiled=True)
    sideways = flux_along(pencil, 2)
    derivative = jnp.einsum(
        "ij,fyjx->fyix", span_operator, sideways, precision=lax.Precision.HIGHEST
    )
    padded = jnp.concatenate([pencil[:, :, -2:], pencil, pencil[:, :, :2]], axis=2)
    pencil_damping = weights[0, :, 0, 0]
    contrib = derivative + pencil_damping[None, :, None, None] * fourth_difference(
        padded, 2, pencil.shape[2]
    )
    span_terms = lax.all_to_all(contrib, "gz", split_axis=2, concat_axis=3, tiled=True)
    tendency = -along_x - wall_terms - span_terms
    advanced = conserved + time_step * tendency
    return (advanced[0], advanced[1:4], advanced[4])


def solution(mesh):
    in_specs = (P("gy", "gz", None), P(None, "gy", "gz", None), P("gy", "gz", None), P(), P(), P())
    out_specs = (P("gy", "gz", None), P(None, "gy", "gz", None), P("gy", "gz", None))
    return jax.shard_map(local, mesh=mesh, in_specs=in_specs, out_specs=out_specs, check_vma=False)
```

profile of v0, /device:TPU:15, one launch (start us, length us, event | category | flops | bytes accessed | tf_op | source)
XLA Modules:
  0.0 1605.4 jit_solution(7403438118843490097)
XLA Ops:
  2.0 5.6 all-to-all-start.3
  7.7 12.8 copy.122
  20.4 5.5 copy.121
  26.0 5.5 copy.120
  31.5 9.3 pad_maximum_fusion.4
  40.8 7.8 copy.130
  48.7 238.7 %all_to_all.84 = f32[5,256,16,256]{1,2,0,3:T(8,128)} all-to-all(f32[5,256,16,256]{1,2,0,3:T(8,128)} %copy.130), channel_id=1, replica_groups=mesh['gy'=4,'gz'=8] {'gy'}, dimensions={3} | all-to-all | bytes 41943040 | tf_op jit(solution)/shard_map/all_to_all | solution.py:52
  287.4 7.8 all-to-all-start.2
  295.2 21.4 %copy.131 = f32[5,256,16,256]{1,3,2,0:T(8,128)} copy(f32[5,256,16,256]{1,2,0,3:T(8,128)} %all_to_all.84) | data formatting | bytes 41943040 | tf_op jit(solution)/shard_map/all_to_all | solution.py:52
  316.6 11.8 slice_bitcast_fusion.2
  347.8 23.0 %copy.137 = f32[5,4,256,16,64]{2,1,4,3,0:T(4,128)} copy(f32[5,4,256,16,64]{2,3,0,4,1:T(8,128)S(1)} %bitcast.117) | data formatting | bytes 41943040 | tf_op jit(solution)/shard_map/all_to_all | solution.py:52
  370.8 25.6 %all_to_all.64 = f32[5,1024,16,64]{1,3,2,0:T(8,128)} reshape(f32[5,4,256,16,64]{2,1,4,3,0:T(4,128)} %copy.137) | data formatting | bytes 41943040 | tf_op jit(solution)/shard_map/all_to_all | solution.py:52
  401.5 9.4 multiply_dynamic-update-slice_fusion.5
  422.6 79.7 %fusion.16 = f32[5,1024,16,64]{1,3,2,0:T(8,128)} fusion(f32[5,1024,16,64]{1,3,2,0:T(8,128)} %all_to_all.64, f32[1024]{0:T(1024)S(1)} %copy-done.13, f32[5,1024,16,64]{1,3,2,0:T(8,128)} %multiply_dynamic-update-slice_fusion.3, f32[1024,1024]{1,0:T(8,128)} %param.9), kind=kOutput, calls=%fused_computation.28 | convolution fusion | flops 64471695360 | bytes 67112960 | tf_op jit(solution)/shard_map/ij,fjzx->fizx/dot_general | solution.py:54
  502.2 33.9 %copy.138 = f32[5,1024,16,64]{3,2,0,1:T(8,128)} copy(f32[5,1024,16,64]{1,3,2,0:T(8,128)} %fusion.16) | data formatting | bytes 41943040 | tf_op jit(solution)/shard_map/add | solution.py:56
  536.2 58.1 %reshape.373 = f32[4,1,1310720]{2,1,0:T(1,128)} reshape(f32[1024,5,16,64]{3,2,1,0:T(8,128)} %bitcast.120) | data formatting | bytes 41943040
  594.2 150.9 %all-to-all-done.2 = f32[5,256,16,256]{1,2,0,3:T(8,128)} async-done(((f32[5,256,16,256]{1,2,0,3:T(8,128)}), f32[5,256,16,256]{1,2,0,3:T(8,128)}, u32[]{:S(2)}, u32[]{:S(2)}) %all-to-all-start.2) | async-done | bytes 20971552 | tf_op jit(solution)/shard_map/all_to_all | solution.py:60
  745.1 9.9 all-to-all-start.1
  755.6 21.4 %copy.143 = f32[5,256,16,256]{1,3,2,0:T(8,128)} copy(f32[5,256,16,256]{1,2,0,3:T(8,128)} %all-to-all-done.2) | data formatting | bytes 41943040 | tf_op jit(solution)/shard_map/all_to_all | solution.py:60
  777.0 14.5 fusion.40
  793.8 5.3 copy.163
  803.9 5.3 copy.148
  813.9 5.3 copy.149
  824.1 5.3 copy.151
  834.1 5.3 copy.161
  839.5 22.2 %copy.164 = f32[5,256,8,16,32]{1,4,3,2,0:T(8,128)} copy(f32[5,256,8,16,32]{1,3,0,4,2:T(8,128)} %bitcast.35) | data formatting | bytes 41943040 | tf_op jit(solution)/shard_map/all_to_all | solution.py:60
  861.7 21.8 %copy.165 = f32[5,256,128,32]{2,1,3,0:T(8,128)} copy(f32[5,256,128,32]{1,3,2,0:T(8,128)} %bitcast.135) | data formatting | bytes 41943040 | tf_op jit(solution)/shard_map/all_to_all | solution.py:60
  888.5 8.8 multiply_dynamic-update-slice_fusion.2
  900.3 7.3 add_dynamic-update-slice_fusion
  908.9 7.9 multiply_dynamic-update-slice_fusion
  920.4 14.9 fusion.41
  935.3 73.5 %fusion.24 = f32[5,256,128,32]{2,1,3,0:T(8,128)} fusion(f32[5,256,128,32]{2,1,3,0:T(8,128)} %copy.165, f32[5,256,2,32]{2,1,3,0:T(8,128)} %get-tuple-element.23, f32[5,256,2,32]{2,1,3,0:T(8,128)} %get-tuple-element.22, f32[256]{0:T(256)S(1)} %bitcast.155, f32[5,256,128,32]{2,1,3,0:T(8,128)} %multiply_dynamic-update-slice_fusion, f32[128,128]{1,0:T(8,128)S(1)} %copy-done), kind=kOutput, calls=%fused_computation.36 | convolution fusion | flops 8121221120 | bytes 63636480 | tf_op jit(solution)/shard_map/ij,fyjx->fyix/dot_general | solution.py:63
  1008.8 21.7 %copy.170 = f32[5,256,128,32]{1,3,0,2:T(8,128)} copy(f32[5,256,128,32]{2,1,3,0:T(8,128)} %fusion.24) | data formatting | bytes 41943040 | tf_op jit(solution)/shard_map/add | solution.py:68
  1030.5 10.2 all-to-all-start.4
  1045.5 11.9 bitcast_dynamic-update-slice_fusion.3
  1063.5 5.8 bitcast_dynamic-update-slice_fusion
  1070.7 64.6 %reduce = f32[4,1310720]{1,0:T(4,128)} reduce(f32[4,1,1310720]{2,1,0:T(1,128)} %all-to-all-done.1, f32[]{:T(128)} %broadcast.64), dimensions={1}, to_apply=%all_to_all.65.reduce_sub_computation | reduce | bytes 41943044 | tf_op jit(solution)/shard_map/all_to_all | solution.py:59
  1135.3 68.1 %reshape.374 = f32[1024,5,16,64]{3,2,1,0:T(8,128)} reshape(f32[4,1310720]{1,0:T(4,128)} %reduce) | data formatting | bytes 41943040
  1203.5 31.0 %copy.180 = f32[5,4,256,16,64]{2,1,4,3,0:T(4,128)} copy(f32[5,4,256,16,64]{4,3,0,2,1:T(8,128)} %bitcast.121) | data formatting | bytes 41943040 | tf_op jit(solution)/shard_map/all_to_all | solution.py:59
  1234.5 21.3 %copy.181 = f32[5,256,16,4,64]{1,2,4,3,0:T(8,128)} copy(f32[5,256,16,4,64]{1,3,4,2,0:T(4,128)} %bitcast.138) | data formatting | bytes 41943040 | tf_op jit(solution)/shard_map/all_to_all | solution.py:59
  1255.8 234.8 %all-to-all-done.4 = f32[5,256,128,32]{1,3,0,2:T(8,128)} async-done(((f32[5,256,128,32]{1,3,0,2:T(8,128)}), f32[5,256,128,32]{1,3,0,2:T(8,128)}, u32[]{:S(2)}, u32[]{:S(2)}) %all-to-all-start.4) | async-done | bytes 20971552 | tf_op jit(solution)/shard_map/all_to_all | solution.py:71
  1490.6 16.4 %copy.172 = f32[5,256,16,8,32]{1,4,3,2,0:T(8,128)} copy(f32[5,256,16,8,32]{1,4,0,2,3:T(8,128)} %bitcast.39) | data formatting | bytes 41943040 | tf_op jit(solution)/shard_map/all_to_all | solution.py:71
  1507.0 55.8 %fusion.9 = f32[5,256,16,256]{1,2,3,0:T(8,128)} fusion(f32[5,256,16,256]{1,2,3,0:T(8,128)} %bitcast.136, f32[5,256,16,2]{1,2,3,0:T(8,128)S(1)} %reshape.370, f32[5,256,16,256]{1,2,3,0:T(8,128)} %bitcast_dynamic-update-slice_fusion, f32[5,256,16,2]{1,2,3,0:T(8,128)S(1)} %reshape.369, f32[5,256,16,256]{1,3,2,0:T(8,128)} %bitcast.137, ...), kind=kLoop, calls=%fused_computation.21 | loop fusion | flops 83886080 | bytes 105185280 | tf_op jit(solution)/shard_map/add | solution.py:73
  1562.8 10.7 slice.220
  1573.4 7.8 slice_bitcast_fusion
  1581.2 12.8 copy.175
  1594.0 5.5 copy.174
  1599.6 5.5 copy.176
  (85 shorter events, 84.5 us)
Async XLA Ops:
  0.6 934.6 %copy-start = (f32[128,128]{1,0:T(8,128)S(1)}, f32[128,128]{1,0:T(8,128)}, u32[]{:S(2)}) copy-start(f32[128,128]{1,0:T(8,128)} %param.10) | copy-start | bytes 196612
  2.0 46.6 %all-to-all-start.3 = ((f32[1,256,1,8]{1,0,2,3:T(1,128)}), f32[1,256,1,8]{1,0,2,3:T(1,128)S(1)}, u32[]{:S(2)}, u32[]{:S(2)}) async-start(f32[1,256,1,8]{1,0,2,3:T(1,128)} %broadcast_in_dim.19), calls=%async_computation.3 | async-start | bytes 16384 | tf_op jit(solution)/shard_map/all_to_all | solution.py:61
  48.7 238.7 %copy-start.12 = (f32[1,256,1,8]{1,0,2,3:T(1,128)}, f32[1,256,1,8]{1,0,2,3:T(1,128)S(1)}, u32[]{:S(2)}) copy-start(f32[1,256,1,8]{1,0,2,3:T(1,128)S(1)} %all-to-all-done.3) | copy-start | bytes 24580
  287.4 457.7 %all-to-all-start.2 = ((f32[5,256,16,256]{1,2,0,3:T(8,128)}), f32[5,256,16,256]{1,2,0,3:T(8,128)}, u32[]{:S(2)}, u32[]{:S(2)}) async-start(f32[5,256,16,256]{1,2,0,3:T(8,128)} %copy.130), calls=%async_computation.2 | async-start | bytes 41943040 | tf_op jit(solution)/shard_map/all_to_all | solution.py:60
  328.5 18.3 %slice-start.3 = ((s8[20971520]{0:T(1024)(128)(4,1)}), s8[4194304]{0:T(1024)(128)(4,1)S(1)}, s32[]{:S(2)}) async-start(s8[20971520]{0:T(1024)(128)(4,1)} %bitcast.115), calls=%async_computation.8 | async-start | bytes 8388608
  333.5 13.3 slice-start.4
  338.5 8.2 slice-start.5
  341.3 5.4 slice-start.6
  344.0 3.8 slice-start.7
  396.4 14.5 copy-start.3
  396.4 14.5 copy-start.7
  396.4 14.5 copy-start.9
  396.4 14.5 copy-start.10
  396.4 14.5 copy-start.11
  418.6 4.0 copy-start.13
  745.1 285.4 %all-to-all-start.1 = ((f32[4,1,1310720]{2,1,0:T(1,128)}), f32[4,1,1310720]{2,1,0:T(1,128)}, u32[]{:S(2)}, u32[]{:S(2)}) async-start(f32[4,1,1310720]{2,1,0:T(1,128)} %reshape.373), calls=%async_computation.1 | async-start | bytes 41943040 | tf_op jit(solution)/shard_map/all_to_all | solution.py:59
  883.5 13.8 copy-start.1
  883.5 13.8 copy-start.5
  883.5 13.8 copy-start.8
  900.3 7.4 copy-start.2
  900.3 8.6 copy-start.6
  900.3 16.6 %slice-start.8 = ((s8[20971520]{0:T(1024)(128)(4,1)}), s8[4194304]{0:T(1024)(128)(4,1)S(1)}, s32[]{:S(2)}) async-start(s8[20971520]{0:T(1024)(128)(4,1)} %bitcast.118), calls=%async_computation.13 | async-start | bytes 8388608
  900.3 16.6 %slice-start.9 = ((s8[20971520]{0:T(1024)(128)(4,1)}), s8[4194304]{0:T(1024)(128)(4,1)S(1)}, s32[]{:S(2)}) async-start(s8[20971520]{0:T(1024)(128)(4,1)} %bitcast.118), calls=%async_computation.14 | async-start | bytes 8388608
  900.3 17.4 %slice-start.10 = ((s8[20971520]{0:T(1024)(128)(4,1)}), s8[4194304]{0:T(1024)(128)(4,1)S(1)}, s32[]{:S(2)}) async-start(s8[20971520]{0:T(1024)(128)(4,1)} %bitcast.118), calls=%async_computation.15 | async-start | bytes 8388608
  908.9 10.2 slice-start.11
  908.9 11.4 slice-start.12
  1030.5 460.1 %all-to-all-start.4 = ((f32[5,256,128,32]{1,3,0,2:T(8,128)}), f32[5,256,128,32]{1,3,0,2:T(8,128)}, u32[]{:S(2)}, u32[]{:S(2)}) async-start(f32[5,256,128,32]{1,3,0,2:T(8,128)} %copy.170), calls=%async_computation.4 | async-start | bytes 41943040 | tf_op jit(solution)/shard_map/all_to_all | solution.py:71
  1040.6 16.8 %slice-start = ((s8[12582912]{0:T(1024)(128)(4,1)}), s8[4194304]{0:T(1024)(128)(4,1)S(1)}, s32[]{:S(2)}) async-start(s8[12582912]{0:T(1024)(128)(4,1)} %bitcast.113), calls=%async_computation.5 | async-start | bytes 8388608
  1045.5 11.9 slice-start.1
  1045.5 11.9 slice-start.2
  1057.4 6.1 copy-start.4
where the time goes:
time: 1620 us; the launch traced here: 1610 us
  local copies, waits for them, and re-layouts  592 us (37%)
  waiting for transfers between devices  386 us (24%)
  blocking collectives  239 us (15%)
  other arithmetic  202 us (12%)
  matrix products  153 us (9%)
  starting transfers between devices  33.5 us (2%)
    all_to_all x1, blocking collectives, local(): lax.all_to_all(conserved, 'gy', split_axis=3, concat_axis=1, tiled=True)  239 us
    all_to_all x1, waiting for transfers between devices, local(): lax.all_to_all(contrib, 'gz', split_axis=2, concat_axis=3, tiled=True)  235 us
    unnamed x66, local copies, waits for them, and re-layouts  206 us
    all_to_all x1, waiting for transfers between devices, local(): lax.all_to_all(conserved, 'gz', split_axis=3, concat_axis=2, tiled=True)  151 us
    dot_general x1, matrix products, local(): jnp.einsum('ij,fjzx->fizx', wall_operator, upward, precision=lax.Precisio...  79.7 us
    dot_general x1, matrix products, local(): jnp.einsum('ij,fyjx->fyix', span_operator, sideways, precision=lax.Precis...  73.5 us
    all_to_all x3, local copies, waits for them, and re-layouts, local(): lax.all_to_all(conserved, 'gy', split_axis=3, concat_axis=1, tiled=True)  70.1 us
    all_to_all x3, local copies, waits for them, and re-layouts, local(): lax.all_to_all(conserved, 'gz', split_axis=3, concat_axis=2, tiled=True)  65.5 us
  transfers between devices with their start and end apart: 4, of which 2 were waited for; matrix products, arithmetic and copies ran while one was open for 50% of the time, Pallas kernels for 0%

commit v1 on v0

v1 whole, which is shorter than its diff:
```python
import functools

import jax
import jax.numpy as jnp
from jax import lax
from jax.experimental import pallas as pl
from jax.experimental.pallas import tpu as pltpu
from jax.sharding import PartitionSpec as P

gamma_less = 0.4
time_step = 0.1
vmem_bytes = 56 * 1024 * 1024


def divisor_up_to(number, limit):
    return max(d for d in range(1, limit + 1) if number % d == 0)


def hop(index, step, size, sign):
    if size & (size - 1) == 0:
        return index ^ step
    return (index + sign * step) % size


def fluxes(fields, direction):
    density, momentum, energy = fields[0], fields[1:4], fields[4]
    inverse = 1.0 / density
    velocity = momentum[direction] * inverse
    square = momentum[0] * momentum[0] + momentum[1] * momentum[1] + momentum[2] * momentum[2]
    pressure = gamma_less * (energy - 0.5 * square * inverse)
    out = [momentum[direction]]
    for column in range(3):
        product = momentum[column] * velocity
        if column == direction:
            product = product + pressure
        out.append(product)
    out.append((energy + pressure) * velocity)
    return out


def halves(value):
    high = value.astype(jnp.bfloat16)
    low = (value - high.astype(jnp.float32)).astype(jnp.bfloat16)
    return high, low


def split_outside(value):
    high = lax.reduce_precision(value, exponent_bits=8, mantissa_bits=7)
    return high.astype(jnp.bfloat16), (value - high).astype(jnp.bfloat16)


def dot(a, b):
    return jnp.dot(a, b, preferred_element_type=jnp.float32)


def call(body, name, order, operands, grid, in_specs, out_specs, out_shape, scratch=(), aliases=None, flops=0):
    scalars = tuple(order)
    moved = sum(4 * o.size for o in operands) + sum(4 * o.size for o in out_shape)
    return pl.pallas_call(
        body,
        name=name,
        grid_spec=pltpu.PrefetchScalarGridSpec(
            num_scalar_prefetch=len(scalars),
            grid=grid,
            in_specs=in_specs,
            out_specs=out_specs,
            scratch_shapes=list(scratch),
        ),
        out_shape=out_shape,
        input_output_aliases={} if aliases is None else aliases,
        compiler_params=pltpu.CompilerParams(vmem_limit_bytes=vmem_bytes),
        cost_estimate=pl.CostEstimate(flops=flops, bytes_accessed=moved, transcendentals=0),
    )(*scalars, *operands)


def pack_span_kernel(order, density, momentum, energy, *pieces):
    for k, piece in enumerate(pieces):
        block = order[k]
        piece[0] = density[block]
        for column in range(3):
            piece[1 + column] = momentum[column, block]
        piece[4] = energy[block]


def pack_span(blocks, chunk, chunks, density, momentum, energy):
    n, share, zl, nx = density.shape
    rows = share // chunks
    r = divisor_up_to(rows, 2)
    first = chunk * (rows // r)
    flat = pl.BlockSpec((n, r, zl, nx), lambda i, s: (0, first + i, 0, 0))
    return call(
        pack_span_kernel,
        f"pack_span_{chunk}",
        (blocks,),
        (density, momentum, energy),
        (rows // r,),
        [flat, pl.BlockSpec((3, n, r, zl, nx), lambda i, s: (0, 0, first + i, 0, 0)), flat],
        [pl.BlockSpec((5, r, zl, nx), lambda i, s: (0, i, 0, 0))] * n,
        [jax.ShapeDtypeStruct((5, rows, zl, nx), jnp.float32)] * n,
    )


def span_kernel(n, weights, both, *refs):
    pieces, outs = refs[:n], refs[n:]
    _, r, zl, nx = pieces[0].shape
    nz = n * zl

    @pl.loop(0, r)
    def _(row):
        weight = weights[pl.program_id(0) * r + row]
        fields = [jnp.concatenate([p[f, row] for p in pieces], axis=0) for f in range(5)]
        for f, flux in enumerate(fluxes(fields, 2)):
            high, low = halves(jnp.concatenate([flux, weight * fields[f]], axis=0))
            total = dot(both[...], high)
            total = total[:nz] + total[nz:] + dot(both[:nz], low)
            for k, out in enumerate(outs):
                out[f, row] = total[k * zl : (k + 1) * zl]


def span_terms(chunk, weights, both, pieces):
    n = len(pieces)
    _, rows, zl, nx = pieces[0].shape
    r = divisor_up_to(rows, 2)
    nz = n * zl
    spec = pl.BlockSpec((5, r, zl, nx), lambda i, s: (0, i, 0, 0))
    return call(
        functools.partial(span_kernel, n),
        f"span_terms_{chunk}",
        (weights,),
        (both, *pieces),
        (rows // r,),
        [pl.BlockSpec(both.shape, lambda i, s: (0, 0))] + [spec] * n,
        [spec] * n,
        [jax.ShapeDtypeStruct(p.shape, jnp.float32) for p in pieces],
        flops=5 * rows * 6 * nz * 2 * nz * nx,
    )


def pack_wall_kernel(zl, order, density, momentum, energy, *refs):
    pieces, narrow = refs[:-1], refs[-1]
    _, zz, rows, nx = pieces[0].shape
    lane = narrow.shape[-1]
    for half in range(nx // lane):
        lanes = slice(half * lane, (half + 1) * lane)
        narrow[half, 0] = density[:, lanes]
        for column in range(3):
            narrow[half, 1 + column] = momentum[column, :, lanes]
        narrow[half, 4] = energy[:, lanes]
    for k, piece in enumerate(pieces):
        for z in range(zz):
            lines = pl.ds(order[k] * zz + z, rows, stride=zl)
            for half in range(nx // lane):
                lanes = slice(half * lane, (half + 1) * lane)
                for f in range(5):
                    piece[f, z, :, lanes] = narrow[half, f, lines, :]


def pack_wall(blocks, density, momentum, energy):
    m = blocks.shape[0]
    jl, zl, nx = density.shape
    zz = zl // m
    lane = divisor_up_to(nx, 128)
    rows = divisor_up_to(jl, 32)
    flat = pl.BlockSpec((rows * zl, nx), lambda i, s: (i, 0))
    return call(
        functools.partial(pack_wall_kernel, zl),
        "pack_wall",
        (blocks,),
        (density.reshape(jl * zl, nx), momentum.reshape(3, jl * zl, nx), energy.reshape(jl * zl, nx)),
        (jl // rows,),
        [flat, pl.BlockSpec((3, rows * zl, nx), lambda i, s: (0, i, 0)), flat],
        [pl.BlockSpec((5, zz, rows, nx), lambda i, s: (0, 0, i, 0))] * m,
        [jax.ShapeDtypeStruct((5, zz, jl, nx), jnp.float32)] * m,
        scratch=[pltpu.VMEM((nx // lane, 5, rows * zl, lane), jnp.float32)],
    )


def wall_kernel(m, order, high, low, damping, *refs):
    pieces, outs = refs[:m], refs[m : 2 * m]
    kept, flux_high, flux_low = refs[2 * m :]
    jl, nx = pieces[0].shape[2:]
    ny = m * jl
    step = divisor_up_to(jl, 32)
    for f in range(5):
        kept[f, 0:8] = jnp.zeros((8, nx), jnp.float32)
        kept[f, 8 + ny : 16 + ny] = jnp.zeros((8, nx), jnp.float32)
    for k in range(m):

        @pl.loop(0, jl // step)
        def _(i):
            here = pl.ds(pl.multiple_of(i * step, step), step)
            there = pl.multiple_of(order[k] * jl + i * step, step)
            fields = [pieces[k][f, 0, here, :] for f in range(5)]
            for f, flux in enumerate(fluxes(fields, 1)):
                kept[f, pl.ds(there + 8, step), :] = fields[f]
                flux_high[f, pl.ds(there, step), :], flux_low[f, pl.ds(there, step), :] = halves(flux)

    for k in range(m):
        first = pl.multiple_of(order[k] * jl, jl)
        rows = pl.ds(first, jl)

        @pl.loop(0, 5)
        def _(f):
            total = dot(high[rows, :], flux_high[f]) + dot(low[rows, :], flux_high[f])
            outs[k][f, 0] = total + dot(high[rows, :], flux_low[f])
            part = divisor_up_to(jl, 64)

            @pl.loop(0, jl // part)
            def _(i):
                at = pl.multiple_of(i * part, part)
                c = kept[f, pl.ds(first + at, part + 16), :]

                def shifted(offset):
                    return c[8 + offset : 8 + offset + part]

                fourth = (
                    shifted(-2) - 4.0 * shifted(-1) + 6.0 * shifted(0) - 4.0 * shifted(1) + shifted(2)
                )
                weight = damping[pl.ds(first + at, part), :]
                outs[k][f, 0, pl.ds(at, part), :] += weight * fourth


def wall_terms(blocks, operator, damping, pieces):
    m = len(pieces)
    _, zz, jl, nx = pieces[0].shape
    ny = m * jl
    high, low = split_outside(operator)
    spec = pl.BlockSpec((5, 1, jl, nx), lambda i, s: (0, i, 0, 0))
    whole = pl.BlockSpec((ny, ny), lambda i, s: (0, 0))
    return call(
        functools.partial(wall_kernel, m),
        "wall_terms",
        (blocks,),
        (high, low, damping.reshape(ny, 1), *pieces),
        (zz,),
        [whole, whole, pl.BlockSpec((ny, 1), lambda i, s: (0, 0))] + [spec] * m,
        [spec] * m,
        [jax.ShapeDtypeStruct(p.shape, jnp.float32) for p in pieces],
        scratch=[
            pltpu.VMEM((5, ny + 16, nx), jnp.float32),
            pltpu.VMEM((5, ny, nx), jnp.bfloat16),
            pltpu.VMEM((5, ny, nx), jnp.bfloat16),
        ],
        flops=6 * 5 * zz * ny * ny * nx,
    )


def base_kernel(m, zl, order, density, momentum, energy, *refs):
    pieces, outs, wall = refs[:m], refs[m : m + 3], refs[m + 3]
    _, zz, rows, nx = pieces[0].shape
    lane = wall.shape[-1]
    for k, piece in enumerate(pieces):
        for z in range(zz):
            lines = pl.ds(order[k] * zz + z, rows, stride=zl)
            for half in range(nx // lane):
                lanes = slice(half * lane, (half + 1) * lane)
                for f in range(5):
                    wall[half, f, lines, :] = piece[f, z, :, lanes]
    part = 16

    @pl.loop(0, rows * zl // part)
    def _(i):
        here = pl.ds(pl.multiple_of(i * part, part), part)
        fields = [density[here, :]] + [momentum[column, here, :] for column in range(3)] + [energy[here, :]]
        column = lax.broadcasted_iota(jnp.int32, (part, nx), 1)
        for f, flux in enumerate(fluxes(fields, 0)):
            first, last = flux[:, :1], flux[:, nx - 1 :]
            above1 = jnp.where(column >= nx - 1, last, pltpu.roll(flux, nx - 1, 1))
            above2 = jnp.where(column >= nx - 2, last, pltpu.roll(flux, nx - 2, 1))
            below1 = jnp.where(column < 1, first, pltpu.roll(flux, 1, 1))
            below2 = jnp.where(column < 2, first, pltpu.roll(flux, 2, 1))
            along = (8.0 * (above1 - below1) - (above2 - below2)) * (1.0 / 12.0)
            across = jnp.concatenate([wall[half, f, here, :] for half in range(wall.shape[0])], axis=1)
            value = fields[f] - time_step * (along + across)
            if f == 0:
                outs[0][here, :] = value
            elif f == 4:
                outs[2][here, :] = value
            else:
                outs[1][f - 1, here, :] = value


def base_fields(blocks, density, momentum, energy, pieces):
    m = len(pieces)
    jl, zl, nx = density.shape
    zz = zl // m
    lane = divisor_up_to(nx, 128)
    rows = divisor_up_to(jl, 16)
    flat = pl.BlockSpec((rows * zl, nx), lambda i, s: (i, 0))
    three = pl.BlockSpec((3, rows * zl, nx), lambda i, s: (0, i, 0))
    shape = jax.ShapeDtypeStruct((jl * zl, nx), jnp.float32)
    outs = call(
        functools.partial(base_kernel, m, zl),
        "base_fields",
        (blocks,),
        (density.reshape(jl * zl, nx), momentum.reshape(3, jl * zl, nx), energy.reshape(jl * zl, nx), *pieces),
        (jl // rows,),
        [flat, three, flat] + [pl.BlockSpec((5, zz, rows, nx), lambda i, s: (0, 0, i, 0))] * m,
        [flat, three, flat],
        [shape, jax.ShapeDtypeStruct((3, jl * zl, nx), jnp.float32), shape],
        scratch=[pltpu.VMEM((nx // lane, 5, rows * zl, lane), jnp.float32)],
    )
    return outs


def add_span_kernel(n, order, density, momentum, energy, *refs):
    pieces, outs = refs[:n], refs[n:]
    for k, piece in enumerate(pieces):
        block = order[k]
        outs[0][block] = density[block] - time_step * piece[0]
        for column in range(3):
            outs[1][column, block] = momentum[column, block] - time_step * piece[1 + column]
        outs[2][block] = energy[block] - time_step * piece[4]


def add_span(blocks, chunk, chunks, fields, pieces):
    n = len(pieces)
    share, zl, nx = fields[0].shape[1:]
    rows = share // chunks
    r = divisor_up_to(rows, 2)
    first = chunk * (rows // r)
    flat = pl.BlockSpec((n, r, zl, nx), lambda i, s: (0, first + i, 0, 0))
    three = pl.BlockSpec((3, n, r, zl, nx), lambda i, s: (0, 0, first + i, 0, 0))
    return call(
        functools.partial(add_span_kernel, n),
        f"add_span_{chunk}",
        (blocks,),
        (*fields, *pieces),
        (rows // r,),
        [flat, three, flat] + [pl.BlockSpec((5, r, zl, nx), lambda i, s: (0, i, 0, 0))] * n,
        [flat, three, flat],
        [jax.ShapeDtypeStruct(f.shape, f.dtype) for f in fields],
        aliases={1: 0, 2: 1, 3: 2},
    )


def exchange(pieces, axis, sign, sequence):
    size = len(pieces)
    out = list(pieces)
    for k in sequence:
        pairs = [(i, hop(i, k, size, sign)) for i in range(size)]
        out[k] = lax.ppermute(pieces[k], axis, pairs)
    return out


def local(density, momentum, energy, wall_operator, span_operator, damping, *, chunks):
    jl, zl, nx = density.shape
    nz = span_operator.shape[0]
    m, n = lax.axis_size("gy"), lax.axis_size("gz")
    gy, gz = lax.axis_index("gy"), lax.axis_index("gz")
    share = jl // n
    chunks = divisor_up_to(share, chunks)
    rows = share // chunks

    span_to = jnp.stack([jnp.asarray(hop(gz, k, n, 1), jnp.int32) for k in range(n)])
    span_from = jnp.stack([jnp.asarray(hop(gz, k, n, -1), jnp.int32) for k in range(n)])
    wall_to = jnp.stack([jnp.asarray(hop(gy, k, m, 1), jnp.int32) for k in range(m)])
    wall_from = jnp.stack([jnp.asarray(hop(gy, k, m, -1), jnp.int32) for k in range(m)])

    by_share = (
        density.reshape(n, share, zl, nx),
        momentum.reshape(3, n, share, zl, nx),
        energy.reshape(n, share, zl, nx),
    )
    far_first = range(n - 1, 0, -1)
    span_out = [
        exchange(pack_span(span_to, c, chunks, *by_share), "gz", 1, far_first) for c in range(chunks)
    ]
    wall_out = exchange(pack_wall(wall_to, density, momentum, energy), "gy", 1, range(m - 1, 0, -1))

    identity = jnp.eye(nz, dtype=jnp.float32)
    fourth = 6.0 * identity
    for offset, factor in ((1, -4.0), (-1, -4.0), (2, 1.0), (-2, 1.0)):
        fourth = fourth + factor * jnp.roll(identity, offset, 1)

    def in_order_of_arrival(matrix):
        blocks = matrix.reshape(n, zl, n, zl)
        blocks = jnp.take(jnp.take(blocks, span_from, axis=0), span_from, axis=2)
        return blocks.reshape(nz, nz)

    both = jnp.concatenate([in_order_of_arrival(span_operator), in_order_of_arrival(fourth)], axis=1)
    both = jnp.concatenate(split_outside(both), axis=0)

    wall_back = exchange(wall_terms(wall_from, wall_operator, damping, wall_out), "gy", -1, range(m - 1, 0, -1))
    span_back = []
    for c in range(chunks):
        weights = lax.dynamic_slice_in_dim(damping, gy * jl + gz * share + c * rows, rows)
        span_back.append(exchange(span_terms(c, weights, both, span_out[c]), "gz", -1, far_first))

    fields = base_fields(wall_to, density, momentum, energy, wall_back)
    fields = (
        fields[0].reshape(n, share, zl, nx),
        fields[1].reshape(3, n, share, zl, nx),
        fields[2].reshape(n, share, zl, nx),
    )
    for c in range(chunks):
        fields = add_span(span_to, c, chunks, fields, span_back[c])
    return (
        fields[0].reshape(jl, zl, nx),
        fields[1].reshape(3, jl, zl, nx),
        fields[2].reshape(jl, zl, nx),
    )


def solution(mesh):
    in_specs = (P("gy", "gz", None), P(None, "gy", "gz", None), P("gy", "gz", None), P(), P(), P())
    out_specs = (P("gy", "gz", None), P(None, "gy", "gz", None), P("gy", "gz", None))
    return jax.shard_map(
        functools.partial(local, chunks=2), mesh=mesh, in_specs=in_specs, out_specs=out_specs, check_vma=False
    )
```

time: 1620 us -> 1010 us (0.62)
  local copies, waits for them, and re-layouts: 592 us -> 9.33 us
  waiting for transfers between devices: 386 us -> 705 us
  Pallas kernels: 0 us -> 246 us
  blocking collectives: 239 us -> 0 us
  other arithmetic: 202 us -> 7.17 us
  matrix products: 153 us -> 0 us
    ppermute x0 -> x34, waiting for transfers between devices: none -> 705 us  [exchange(): out[k] = lax.ppermute(pieces[k], axis, pairs)]
    all_to_all x4 -> x0, waiting for transfers between devices: 386 us -> none  [the longest x1 235 us: local(): lax.all_to_all(contrib, 'gz', split_axis=2, concat_axis=3, tiled=True)]
    pallas_call x0 -> x9, Pallas kernels: none -> 246 us  [call(): pl.pallas_call(body, name=name, grid_spec=pltpu.PrefetchScalarGridSpec(nu...]
    all_to_all x1 -> x0, blocking collectives: 239 us -> none  [local(): lax.all_to_all(conserved, 'gy', split_axis=3, concat_axis=1, tiled=True)]
    all_to_all x10 -> x0, local copies, waits for them, and re-layouts: 205 us -> none  [the longest x3 70.1 us: local(): lax.all_to_all(conserved, 'gy', split_axis=3, concat_axis=1, tiled=True)]
    unnamed x66 -> x33, local copies, waits for them, and re-layouts: 206 us -> 2.22 us
    dot_general x2 -> x0, matrix products: 153 us -> none  [the longest x1 79.7 us: local(): jnp.einsum('ij,fjzx->fizx', wall_operator, upward, precision=lax.Precisio...]
    slice x12 -> x4, local copies, waits for them, and re-layouts: 73.3 us -> 0.32 us  [local(): fourth = fourth + factor * jnp.roll(identity, offset, 1)]
  transfers between devices with their start and end apart: 4 -> 34, of which waited for: 2 -> 17; matrix products, arithmetic and copies ran while one was open for 50% -> 1% of each run, Pallas kernels for 0% -> 22%
where the time goes in v1:
time: 1010 us
  waiting for transfers between devices  705 us (70%)
  Pallas kernels  246 us (24%)
  starting transfers between devices  40.5 us (4%)
    ppermute x34, waiting for transfers between devices, exchange(): out[k] = lax.ppermute(pieces[k], axis, pairs)  705 us
    pallas_call x9, Pallas kernels, call(): pl.pallas_call(body, name=name, grid_spec=pltpu.PrefetchScalarGridSpec(nu...  246 us
    ppermute x34, starting transfers between devices, exchange(): out[k] = lax.ppermute(pieces[k], axis, pairs)  40.5 us
  transfers between devices with their start and end apart: 34, of which 17 were waited for; matrix products, arithmetic and copies ran while one was open for 1% of the time, Pallas kernels for 22%

profile of v1, /device:TPU:15, one launch (start us, length us, event | category | flops | bytes accessed | tf_op | source)
XLA Modules:
  0.0 1009.3 jit_solution(11670486015928676792)
XLA Ops:
  1.3 10.6 %pack_span_0.1 = (f32[5,16,16,256]{3,2,1,0:T(8,128)}, f32[5,16,16,256]{3,2,1,0:T(8,128)}, f32[5,16,16,256]{3,2,1,0:T(8,128)}, f32[5,16,16,256]{3,2,1,0:T(8,128)}...) custom-call(s32[8]{0:T(128)} %stack.64.order, ...), custom_call_target="tpu_custom_call" | custom-call | bytes 31457280 | tf_op jit(solution)/shard_map/pack_span_0/pallas_call | solution.py:59
  11.9 0.7 collective-permute-start.6
  12.8 1.5 collective-permute-start.8
  14.4 2.3 collective-permute-start.9
  17.1 1.3 collective-permute-start.11
  19.0 20.8 %pack_wall.1 = (f32[5,4,256,256]{3,2,1,0:T(8,128)}, f32[5,4,256,256]{3,2,1,0:T(8,128)}, f32[5,4,256,256]{3,2,1,0:T(8,128)}, f32[5,4,256,256]{3,2,1,0:T(8,128)}) custom-call(s32[4]{0:T(128)} %pad_add_fusion.order, f32[4096,256]{1,0:T(8,128)} %bitcast.38, f32[3,4096,256]{2,1,0:T(8,128)} %bitcast.34, f32[4096,256]{1,0:T(8,128)} %bitcast.42), custom_call_target="tpu_custom_call" | custom-call | bytes 41943040 | tf_op jit(solution)/shard_map/pack_wall/pallas_call | solution.py:59
  39.8 57.2 %collective-permute-done.7.refs_2_ = f32[5,16,16,256]{3,2,1,0:T(8,128)S(1)} collective-permute-done((f32[5,16,16,256]{3,2,1,0:T(8,128)}, f32[5,16,16,256]{3,2,1,0:T(8,128)S(1)}, u32[]{:S(2)}, u32[]{:S(2)}) %collective-permute-start.7) | collective-permute-done | bytes 1310752 | tf_op jit(solution)/shard_map/ppermute | solution.py:342
  97.2 27.8 %collective-permute-done.8.refs_3_ = f32[5,16,16,256]{3,2,1,0:T(8,128)S(1)} collective-permute-done((f32[5,16,16,256]{3,2,1,0:T(8,128)}, f32[5,16,16,256]{3,2,1,0:T(8,128)S(1)}, u32[]{:S(2)}, u32[]{:S(2)}) %collective-permute-start.8) | collective-permute-done | bytes 1310752 | tf_op jit(solution)/shard_map/ppermute | solution.py:342
  125.2 1.2 collective-permute-start.2
  126.5 10.6 %pack_span_1.1 = (f32[5,16,16,256]{3,2,1,0:T(8,128)}, f32[5,16,16,256]{3,2,1,0:T(8,128)}, f32[5,16,16,256]{3,2,1,0:T(8,128)}, f32[5,16,16,256]{3,2,1,0:T(8,128)}...) custom-call(s32[8]{0:T(128)} %stack.64.order, ...), custom_call_target="tpu_custom_call" | custom-call | bytes 31457280 | tf_op jit(solution)/shard_map/pack_span_1/pallas_call | solution.py:59
  137.1 20.3 %collective-permute-done.10.refs_5_ = f32[5,16,16,256]{3,2,1,0:T(8,128)} collective-permute-done((f32[5,16,16,256]{3,2,1,0:T(8,128)}, f32[5,16,16,256]{3,2,1,0:T(8,128)}, u32[]{:S(2)}, u32[]{:S(2)}) %collective-permute-start.10) | collective-permute-done | bytes 1310752 | tf_op jit(solution)/shard_map/ppermute | solution.py:342
  157.9 55.7 %collective-permute-done.11.refs_6_ = f32[5,16,16,256]{3,2,1,0:T(8,128)} collective-permute-done((f32[5,16,16,256]{3,2,1,0:T(8,128)}, f32[5,16,16,256]{3,2,1,0:T(8,128)}, u32[]{:S(2)}, u32[]{:S(2)}) %collective-permute-start.11) | collective-permute-done | bytes 1310752 | tf_op jit(solution)/shard_map/ppermute | solution.py:342
  213.6 1.5 collective-permute-start.20
  215.7 26.3 %collective-permute-done.12.refs_7_ = f32[5,16,16,256]{3,2,1,0:T(8,128)S(1)} collective-permute-done((f32[5,16,16,256]{3,2,1,0:T(8,128)S(1)}, f32[5,16,16,256]{3,2,1,0:T(8,128)S(1)}, u32[]{:S(2)}, u32[]{:S(2)}) %collective-permute-start.12) | collective-permute-done | bytes 1310752 | tf_op jit(solution)/shard_map/ppermute | solution.py:342
  242.0 1.1 copy-done.8
  243.2 2.1 collective-permute-start.22
  249.9 22.3 %collective-permute-done.21.refs_2_ = f32[5,16,16,256]{3,2,1,0:T(8,128)} collective-permute-done((f32[5,16,16,256]{3,2,1,0:T(8,128)}, f32[5,16,16,256]{3,2,1,0:T(8,128)}, u32[]{:S(2)}, u32[]{:S(2)}) %collective-permute-start.21) | collective-permute-done | bytes 1310752 | tf_op jit(solution)/shard_map/ppermute | solution.py:342
  272.2 3.1 collective-permute-start.23
  275.3 49.6 %collective-permute-done.22.refs_3_ = f32[5,16,16,256]{3,2,1,0:T(8,128)} collective-permute-done((f32[5,16,16,256]{3,2,1,0:T(8,128)}, f32[5,16,16,256]{3,2,1,0:T(8,128)}, u32[]{:S(2)}, u32[]{:S(2)}) %collective-permute-start.22) | collective-permute-done | bytes 1310752 | tf_op jit(solution)/shard_map/ppermute | solution.py:342
  324.9 2.9 collective-permute-start.24
  328.4 1.0 copy.18.damping
  330.6 5.1 fusion
  335.8 14.0 %span_terms_0.1 = (f32[5,16,16,256]{3,2,1,0:T(8,128)}, f32[5,16,16,256]{3,2,1,0:T(8,128)}, f32[5,16,16,256]{3,2,1,0:T(8,128)}, f32[5,16,16,256]{3,2,1,0:T(8,128)...) custom-call(f32[16]{0:T(128)} %get-tuple-element.116.weights, ...), custom_call_target="tpu_custom_call" | custom-call | flops 4026531840 | bytes 21233664 | tf_op jit(solution)/shard_map/span_terms_0/pallas_call | solution.py:59
  349.8 10.0 collective-permute-done.23.refs_4_
  359.8 56.1 %collective-permute-done.24.refs_5_ = f32[5,16,16,256]{3,2,1,0:T(8,128)} collective-permute-done((f32[5,16,16,256]{3,2,1,0:T(8,128)S(1)}, f32[5,16,16,256]{3,2,1,0:T(8,128)}, u32[]{:S(2)}, u32[]{:S(2)}) %collective-permute-start.24) | collective-permute-done | bytes 1310752 | tf_op jit(solution)/shard_map/ppermute | solution.py:342
  415.9 1.9 collective-permute-start.26
  417.8 3.8 collective-permute-start.14
  421.6 84.5 %wall_terms.1 = (f32[5,4,256,256]{3,2,1,0:T(8,128)}, f32[5,4,256,256]{3,2,1,0:T(8,128)}, f32[5,4,256,256]{3,2,1,0:T(8,128)}, f32[5,4,256,256]{3,2,1,0:T(8,128)}) custom-call(s32[4]{0:T(128)} %pad_add_fusion.order, bf16[1024,1024]{1,0:T(8,128)(2,1)} %get-tuple-element.104.high, bf16[1024,1024]{1,0:T(8,128)(2,1)} %get-tuple-element.103.low, ...), custom_call_target="tpu_custom_call" | custom-call | flops 32212254720 | bytes 50335744 | tf_op jit(solution)/shard_map/wall_terms/pallas_call | solution.py:59
  506.1 1.0 copy-done.15
  507.6 2.2 collective-permute-start.5
  509.8 1.8 collective-permute-start.16
  511.6 2.0 collective-permute-start.17
  513.6 82.6 %collective-permute-done.16.refs_4_ = f32[5,16,16,256]{3,2,1,0:T(8,128)} collective-permute-done((f32[5,16,16,256]{3,2,1,0:T(8,128)}, f32[5,16,16,256]{3,2,1,0:T(8,128)}, u32[]{:S(2)}, u32[]{:S(2)}) %collective-permute-start.16) | collective-permute-done | bytes 1310752 | tf_op jit(solution)/shard_map/ppermute | solution.py:342
  596.2 1.0 collective-permute-start.18
  597.2 55.2 %collective-permute-done.17.refs_5_ = f32[5,16,16,256]{3,2,1,0:T(8,128)} collective-permute-done((f32[5,16,16,256]{3,2,1,0:T(8,128)}, f32[5,16,16,256]{3,2,1,0:T(8,128)}, u32[]{:S(2)}, u32[]{:S(2)}) %collective-permute-start.17) | collective-permute-done | bytes 1310752 | tf_op jit(solution)/shard_map/ppermute | solution.py:342
  652.4 1.5 collective-permute-start.19
  653.8 13.8 %span_terms_1.1 = (f32[5,16,16,256]{3,2,1,0:T(8,128)}, f32[5,16,16,256]{3,2,1,0:T(8,128)}, f32[5,16,16,256]{3,2,1,0:T(8,128)}, f32[5,16,16,256]{3,2,1,0:T(8,128)...) custom-call(f32[16]{0:T(128)} %get-tuple-element.115.weights, ...), custom_call_target="tpu_custom_call" | custom-call | flops 4026531840 | bytes 21233664 | tf_op jit(solution)/shard_map/span_terms_1/pallas_call | solution.py:59
  667.6 42.6 %collective-permute-done.18.refs_6_ = f32[5,16,16,256]{3,2,1,0:T(8,128)} collective-permute-done((f32[5,16,16,256]{3,2,1,0:T(8,128)}, f32[5,16,16,256]{3,2,1,0:T(8,128)}, u32[]{:S(2)}, u32[]{:S(2)}) %collective-permute-start.18) | collective-permute-done | bytes 1310752 | tf_op jit(solution)/shard_map/ppermute | solution.py:342
  710.8 27.5 %collective-permute-done.19.refs_7_ = f32[5,16,16,256]{3,2,1,0:T(8,128)} collective-permute-done((f32[5,16,16,256]{3,2,1,0:T(8,128)}, f32[5,16,16,256]{3,2,1,0:T(8,128)}, u32[]{:S(2)}, u32[]{:S(2)}) %collective-permute-start.19) | collective-permute-done | bytes 1310752 | tf_op jit(solution)/shard_map/ppermute | solution.py:342
  738.4 2.0 collective-permute-start.29
  740.4 28.1 %collective-permute-done.28.refs_2_ = f32[5,16,16,256]{3,2,1,0:T(8,128)S(1)} collective-permute-done((f32[5,16,16,256]{3,2,1,0:T(8,128)}, f32[5,16,16,256]{3,2,1,0:T(8,128)S(1)}, u32[]{:S(2)}, u32[]{:S(2)}) %collective-permute-start.28) | collective-permute-done | bytes 1310752 | tf_op jit(solution)/shard_map/ppermute | solution.py:342
  769.0 4.1 collective-permute-start.31
  773.6 65.5 %base_fields.1 = (f32[4096,256]{1,0:T(8,128)}, f32[3,4096,256]{2,1,0:T(8,128)}, f32[4096,256]{1,0:T(8,128)}) custom-call(s32[4]{0:T(128)} %pad_add_fusion.order, f32[4096,256]{1,0:T(8,128)} %bitcast.40, f32[3,4096,256]{2,1,0:T(8,128)} %bitcast.36, f32[4096,256]{1,0:T(8,128)} %bitcast.44, f32[5,4,256,256]{3,2,1,0:T(8,128)} %get-tuple-element.58.refs_0_, ...), custom_call_target="tpu_custom_call" | custom-call | bytes 62914560 | tf_op jit(solution)/shard_map/base_fields/pallas_call | solution.py:59
  839.2 13.3 %add_span_0.1 = (f32[8,32,16,256]{3,2,1,0:T(8,128)}, f32[3,8,32,16,256]{4,3,2,1,0:T(8,128)}, f32[8,32,16,256]{3,2,1,0:T(8,128)}) custom-call(s32[8]{0:T(128)} %stack.64.order, f32[8,32,16,256]{3,2,1,0:T(8,128)} %bitcast.47, f32[3,8,32,16,256]{4,3,2,1,0:T(8,128)} %bitcast.45, ...), custom_call_target="tpu_custom_call", output_to_operand_aliasing={{0}: (1, {}), {1}: (2, {}), {2}: (3, {})} | custom-call | bytes 52428800 | tf_op jit(solution)/shard_map/add_span_0/pallas_call | solution.py:59
  852.5 84.0 %collective-permute-done.31.refs_5_ = f32[5,16,16,256]{3,2,1,0:T(8,128)} collective-permute-done((f32[5,16,16,256]{3,2,1,0:T(8,128)}, f32[5,16,16,256]{3,2,1,0:T(8,128)}, u32[]{:S(2)}, u32[]{:S(2)}) %collective-permute-start.31) | collective-permute-done | bytes 1310752 | tf_op jit(solution)/shard_map/ppermute | solution.py:342
  936.5 29.8 %collective-permute-done.32.refs_6_ = f32[5,16,16,256]{3,2,1,0:T(8,128)} collective-permute-done((f32[5,16,16,256]{3,2,1,0:T(8,128)}, f32[5,16,16,256]{3,2,1,0:T(8,128)}, u32[]{:S(2)}, u32[]{:S(2)}) %collective-permute-start.32) | collective-permute-done | bytes 1310752 | tf_op jit(solution)/shard_map/ppermute | solution.py:342
  966.4 29.7 %collective-permute-done.33.refs_7_ = f32[5,16,16,256]{3,2,1,0:T(8,128)} collective-permute-done((f32[5,16,16,256]{3,2,1,0:T(8,128)}, f32[5,16,16,256]{3,2,1,0:T(8,128)}, u32[]{:S(2)}, u32[]{:S(2)}) %collective-permute-start.33) | collective-permute-done | bytes 1310752 | tf_op jit(solution)/shard_map/ppermute | solution.py:342
  996.0 13.3 %add_span_1.1 = (f32[8,32,16,256]{3,2,1,0:T(8,128)}, f32[3,8,32,16,256]{4,3,2,1,0:T(8,128)}, f32[8,32,16,256]{3,2,1,0:T(8,128)}) custom-call(s32[8]{0:T(128)} %stack.64.order, f32[8,32,16,256]{3,2,1,0:T(8,128)} %get-tuple-element.81.density, ...), custom_call_target="tpu_custom_call", output_to_operand_aliasing={{0}: (1, {}), {1}: (2, {}), {2}: (3, {})} | custom-call | bytes 52428800 | tf_op jit(solution)/shard_map/add_span_1/pallas_call | solution.py:59
  (99 shorter events, 11.8 us)
Async XLA Ops:
  11.9 5.1 collective-permute-start.6
  12.7 84.3 %collective-permute-start.7 = (f32[5,16,16,256]{3,2,1,0:T(8,128)}, f32[5,16,16,256]{3,2,1,0:T(8,128)S(1)}, u32[]{:S(2)}, u32[]{:S(2)}) collective-permute-start(f32[5,16,16,256]{3,2,1,0:T(8,128)} %get-tuple-element.67), channel_id=1, source_target_pairs={{0,2},{1,3},{2,0},{3,1},{4,6},{5,7},{6,4},{7,5},{8,10},{9,11},{10,... | collective-permute-start | bytes 3932168 | tf_op jit(solution)/shard_map/ppermute | solution.py:342
  12.8 112.2 %collective-permute-start.8 = (f32[5,16,16,256]{3,2,1,0:T(8,128)}, f32[5,16,16,256]{3,2,1,0:T(8,128)S(1)}, u32[]{:S(2)}, u32[]{:S(2)}) collective-permute-start(f32[5,16,16,256]{3,2,1,0:T(8,128)} %get-tuple-element.68), channel_id=1, source_target_pairs={{0,3},{1,2},{2,1},{3,0},{4,7},{5,6},{6,5},{7,4},{8,11},{9,10},{10,... | collective-permute-start | bytes 3932168 | tf_op jit(solution)/shard_map/ppermute | solution.py:342
  14.4 110.9 %collective-permute-start.9 = (f32[5,16,16,256]{3,2,1,0:T(8,128)}, f32[5,16,16,256]{3,2,1,0:T(8,128)}, u32[]{:S(2)}, u32[]{:S(2)}) collective-permute-start(f32[5,16,16,256]{3,2,1,0:T(8,128)} %get-tuple-element.69), channel_id=1, source_target_pairs={{0,4},{1,5},{2,6},{3,7},{4,0},{5,1},{6,2},{7,3},{8,12},{9,13},{10,... | collective-permute-start | bytes 3932168 | tf_op jit(solution)/shard_map/ppermute | solution.py:342
  16.7 140.7 %collective-permute-start.10 = (f32[5,16,16,256]{3,2,1,0:T(8,128)}, f32[5,16,16,256]{3,2,1,0:T(8,128)}, u32[]{:S(2)}, u32[]{:S(2)}) collective-permute-start(f32[5,16,16,256]{3,2,1,0:T(8,128)} %get-tuple-element.70), channel_id=1, source_target_pairs={{0,5},{1,4},{2,7},{3,6},{4,1},{5,0},{6,3},{7,2},{8,13},{9,12},{10,... | collective-permute-start | bytes 3932168 | tf_op jit(solution)/shard_map/ppermute | solution.py:342
  17.1 196.5 %collective-permute-start.11 = (f32[5,16,16,256]{3,2,1,0:T(8,128)}, f32[5,16,16,256]{3,2,1,0:T(8,128)}, u32[]{:S(2)}, u32[]{:S(2)}) collective-permute-start(f32[5,16,16,256]{3,2,1,0:T(8,128)} %get-tuple-element.71), channel_id=1, source_target_pairs={{0,6},{1,7},{2,4},{3,5},{4,2},{5,3},{6,0},{7,1},{8,14},{9,15},{10,... | collective-permute-start | bytes 3932168 | tf_op jit(solution)/shard_map/ppermute | solution.py:342
  96.9 29.5 %copy-start.9 = (f32[5,16,16,256]{3,2,1,0:T(8,128)}, f32[5,16,16,256]{3,2,1,0:T(8,128)S(1)}, u32[]{:S(2)}) copy-start(f32[5,16,16,256]{3,2,1,0:T(8,128)S(1)} %collective-permute-done.7.refs_2_) | copy-start | bytes 3932164
  96.9 320.9 %collective-permute-start = (f32[5,4,256,256]{3,2,1,0:T(8,128)}, f32[5,4,256,256]{3,2,1,0:T(8,128)}, u32[]{:S(2)}, u32[]{:S(2)}) collective-permute-start(f32[5,4,256,256]{3,2,1,0:T(8,128)} %get-tuple-element.55), channel_id=1, source_target_pairs={{0,8},{8,0},{16,24},{24,16},{1,9},{9,1},{17,25},{25,17},{2,10},{10... | collective-permute-start | bytes 15728648 | tf_op jit(solution)/shard_map/ppermute | solution.py:342
  125.0 12.1 %copy-start.10 = (f32[5,16,16,256]{3,2,1,0:T(8,128)}, f32[5,16,16,256]{3,2,1,0:T(8,128)S(1)}, u32[]{:S(2)}) copy-start(f32[5,16,16,256]{3,2,1,0:T(8,128)S(1)} %collective-permute-done.8.refs_3_) | copy-start | bytes 3932164
  125.0 292.8 %collective-permute-start.1 = (f32[5,4,256,256]{3,2,1,0:T(8,128)}, f32[5,4,256,256]{3,2,1,0:T(8,128)}, u32[]{:S(2)}, u32[]{:S(2)}) collective-permute-start(f32[5,4,256,256]{3,2,1,0:T(8,128)} %get-tuple-element.56), channel_id=1, source_target_pairs={{0,16},{8,24},{16,0},{24,8},{1,17},{9,25},{17,1},{25,9},{2,18},{10... | collective-permute-start | bytes 15728648 | tf_op jit(solution)/shard_map/ppermute | solution.py:342
  125.2 32.2 %copy-start.14 = (f32[5,16,16,256]{3,2,1,0:T(8,128)S(1)}, f32[5,16,16,256]{3,2,1,0:T(8,128)}, u32[]{:S(2)}) copy-start(f32[5,16,16,256]{3,2,1,0:T(8,128)} %get-tuple-element.72) | copy-start | bytes 3932164
  125.2 296.3 %collective-permute-start.2 = (f32[5,4,256,256]{3,2,1,0:T(8,128)}, f32[5,4,256,256]{3,2,1,0:T(8,128)}, u32[]{:S(2)}, u32[]{:S(2)}) collective-permute-start(f32[5,4,256,256]{3,2,1,0:T(8,128)} %get-tuple-element.57), channel_id=1, source_target_pairs={{0,24},{8,16},{16,8},{24,0},{1,25},{9,17},{17,9},{25,1},{2,26},{10... | collective-permute-start | bytes 15728648 | tf_op jit(solution)/shard_map/ppermute | solution.py:342
  137.1 78.6 %copy-start.6 = (s32[8]{0:T(128)S(1)}, s32[8]{0:T(128)}, u32[]{:S(2)}) copy-start(s32[8]{0:T(128)} %stack.64.order) | copy-start | bytes 100
  157.4 84.6 %collective-permute-start.12 = (f32[5,16,16,256]{3,2,1,0:T(8,128)S(1)}, f32[5,16,16,256]{3,2,1,0:T(8,128)S(1)}, u32[]{:S(2)}, u32[]{:S(2)}) collective-permute-start(f32[5,16,16,256]{3,2,1,0:T(8,128)S(1)} %copy-done.14), channel_id=1, source_target_pairs={{0,7},{1,6},{2,5},{3,4},{4,3},{5,2},{6,1},{7,0},{8,15},{9,14},{10,... | collective-permute-start | bytes 3932168 | tf_op jit(solution)/shard_map/ppermute | solution.py:342
  213.6 28.4 %collective-permute-start.20 = (f32[5,16,16,256]{3,2,1,0:T(8,128)}, f32[5,16,16,256]{3,2,1,0:T(8,128)S(1)}, u32[]{:S(2)}, u32[]{:S(2)}) collective-permute-start(f32[5,16,16,256]{3,2,1,0:T(8,128)} %get-tuple-element.85), channel_id=1, source_target_pairs={{0,1},{1,0},{2,3},{3,2},{4,5},{5,4},{6,7},{7,6},{8,9},{9,8},{10,11... | collective-permute-start | bytes 3932168 | tf_op jit(solution)/shard_map/ppermute | solution.py:342
  215.6 30.5 %copy-start.5 = (f32[128,128]{1,0:T(8,128)S(1)}, f32[128,128]{1,0:T(8,128)}, u32[]{:S(2)}) copy-start(f32[128,128]{1,0:T(8,128)} %param.14) | copy-start | bytes 196612
  242.0 3.2 copy-start.13
  242.0 30.1 %collective-permute-start.21 = (f32[5,16,16,256]{3,2,1,0:T(8,128)}, f32[5,16,16,256]{3,2,1,0:T(8,128)}, u32[]{:S(2)}, u32[]{:S(2)}) collective-permute-start(f32[5,16,16,256]{3,2,1,0:T(8,128)} %get-tuple-element.86), channel_id=1, source_target_pairs={{0,2},{1,3},{2,0},{3,1},{4,6},{5,7},{6,4},{7,5},{8,10},{9,11},{10,... | collective-permute-start | bytes 3932168 | tf_op jit(solution)/shard_map/ppermute | solution.py:342
  243.2 81.7 %collective-permute-start.22 = (f32[5,16,16,256]{3,2,1,0:T(8,128)}, f32[5,16,16,256]{3,2,1,0:T(8,128)}, u32[]{:S(2)}, u32[]{:S(2)}) collective-permute-start(f32[5,16,16,256]{3,2,1,0:T(8,128)} %get-tuple-element.87), channel_id=1, source_target_pairs={{0,3},{1,2},{2,1},{3,0},{4,7},{5,6},{6,5},{7,4},{8,11},{9,10},{10,... | collective-permute-start | bytes 3932168 | tf_op jit(solution)/shard_map/ppermute | solution.py:342
  249.4 75.5 %copy-start.12 = (f32[5,16,16,256]{3,2,1,0:T(8,128)S(1)}, f32[5,16,16,256]{3,2,1,0:T(8,128)}, u32[]{:S(2)}) copy-start(f32[5,16,16,256]{3,2,1,0:T(8,128)} %get-tuple-element.89) | copy-start | bytes 3932164
  249.4 78.4 %copy-start.7 = (f32[1024]{0:T(1024)S(1)}, f32[1024]{0:T(1024)}, u32[]{:S(2)}) copy-start(f32[1024]{0:T(1024)} %param.15) | copy-start | bytes 12292
  272.2 87.6 %collective-permute-start.23 = (f32[5,16,16,256]{3,2,1,0:T(8,128)}, f32[5,16,16,256]{3,2,1,0:T(8,128)}, u32[]{:S(2)}, u32[]{:S(2)}) collective-permute-start(f32[5,16,16,256]{3,2,1,0:T(8,128)} %get-tuple-element.88), channel_id=1, source_target_pairs={{0,4},{1,5},{2,6},{3,7},{4,0},{5,1},{6,2},{7,3},{8,12},{9,13},{10,... | collective-permute-start | bytes 3932168 | tf_op jit(solution)/shard_map/ppermute | solution.py:342
  324.9 91.0 %collective-permute-start.24 = (f32[5,16,16,256]{3,2,1,0:T(8,128)S(1)}, f32[5,16,16,256]{3,2,1,0:T(8,128)}, u32[]{:S(2)}, u32[]{:S(2)}) collective-permute-start(f32[5,16,16,256]{3,2,1,0:T(8,128)S(1)} %copy-done.12), channel_id=1, source_target_pairs={{0,5},{1,4},{2,7},{3,6},{4,1},{5,0},{6,3},{7,2},{8,13},{9,12},{10,... | collective-permute-start | bytes 3932168 | tf_op jit(solution)/shard_map/ppermute | solution.py:342
  335.8 24.1 %copy-start.11 = (f32[5,16,16,256]{3,2,1,0:T(8,128)S(1)}, f32[5,16,16,256]{3,2,1,0:T(8,128)}, u32[]{:S(2)}) copy-start(f32[5,16,16,256]{3,2,1,0:T(8,128)} %get-tuple-element.90) | copy-start | bytes 3932164
  359.8 146.3 %collective-permute-start.25 = (f32[5,16,16,256]{3,2,1,0:T(8,128)S(1)}, f32[5,16,16,256]{3,2,1,0:T(8,128)S(1)}, u32[]{:S(2)}, u32[]{:S(2)}) collective-permute-start(f32[5,16,16,256]{3,2,1,0:T(8,128)S(1)} %copy-done.11), channel_id=1, source_target_pairs={{0,6},{1,7},{2,4},{3,5},{4,2},{5,3},{6,0},{7,1},{8,14},{9,15},{10,... | collective-permute-start | bytes 3932168 | tf_op jit(solution)/shard_map/ppermute | solution.py:342
  415.9 91.5 %collective-permute-start.26 = (f32[5,16,16,256]{3,2,1,0:T(8,128)}, f32[5,16,16,256]{3,2,1,0:T(8,128)}, u32[]{:S(2)}, u32[]{:S(2)}) collective-permute-start(f32[5,16,16,256]{3,2,1,0:T(8,128)} %get-tuple-element.91), channel_id=1, source_target_pairs={{0,7},{1,6},{2,5},{3,4},{4,3},{5,2},{6,1},{7,0},{8,15},{9,14},{10,... | collective-permute-start | bytes 3932168 | tf_op jit(solution)/shard_map/ppermute | solution.py:342
  417.8 89.8 %collective-permute-start.13 = (f32[5,16,16,256]{3,2,1,0:T(8,128)}, f32[5,16,16,256]{3,2,1,0:T(8,128)S(1)}, u32[]{:S(2)}, u32[]{:S(2)}) collective-permute-start(f32[5,16,16,256]{3,2,1,0:T(8,128)} %get-tuple-element.74), channel_id=1, source_target_pairs={{0,1},{1,0},{2,3},{3,2},{4,5},{5,4},{6,7},{7,6},{8,9},{9,8},{10,11... | collective-permute-start | bytes 3932168 | tf_op jit(solution)/shard_map/ppermute | solution.py:342
  417.8 92.0 %collective-permute-start.14 = (f32[5,16,16,256]{3,2,1,0:T(8,128)}, f32[5,16,16,256]{3,2,1,0:T(8,128)S(1)}, u32[]{:S(2)}, u32[]{:S(2)}) collective-permute-start(f32[5,16,16,256]{3,2,1,0:T(8,128)} %get-tuple-element.75), channel_id=1, source_target_pairs={{0,2},{1,3},{2,0},{3,1},{4,6},{5,7},{6,4},{7,5},{8,10},{9,11},{10,... | collective-permute-start | bytes 3932168 | tf_op jit(solution)/shard_map/ppermute | solution.py:342
  421.6 90.0 %collective-permute-start.15 = (f32[5,16,16,256]{3,2,1,0:T(8,128)}, f32[5,16,16,256]{3,2,1,0:T(8,128)}, u32[]{:S(2)}, u32[]{:S(2)}) collective-permute-start(f32[5,16,16,256]{3,2,1,0:T(8,128)} %get-tuple-element.76), channel_id=1, source_target_pairs={{0,3},{1,2},{2,1},{3,0},{4,7},{5,6},{6,5},{7,4},{8,11},{9,10},{10,... | collective-permute-start | bytes 3932168 | tf_op jit(solution)/shard_map/ppermute | solution.py:342
  507.2 261.9 %collective-permute-start.3 = (f32[5,4,256,256]{3,2,1,0:T(8,128)}, f32[5,4,256,256]{3,2,1,0:T(8,128)S(1)}, u32[]{:S(2)}, u32[]{:S(2)}) collective-permute-start(f32[5,4,256,256]{3,2,1,0:T(8,128)} %get-tuple-element.59), channel_id=1, source_target_pairs={{0,8},{8,0},{16,24},{24,16},{1,9},{9,1},{17,25},{25,17},{2,10},{10... | collective-permute-start | bytes 15728648 | tf_op jit(solution)/shard_map/ppermute | solution.py:342
  507.4 265.7 %collective-permute-start.4 = (f32[5,4,256,256]{3,2,1,0:T(8,128)}, f32[5,4,256,256]{3,2,1,0:T(8,128)}, u32[]{:S(2)}, u32[]{:S(2)}) collective-permute-start(f32[5,4,256,256]{3,2,1,0:T(8,128)} %get-tuple-element.60), channel_id=1, source_target_pairs={{0,16},{8,24},{16,0},{24,8},{1,17},{9,25},{17,1},{25,9},{2,18},{10... | collective-permute-start | bytes 15728648 | tf_op jit(solution)/shard_map/ppermute | solution.py:342
  507.6 160.0 %copy-start.1 = (f32[5,16,16,256]{3,2,1,0:T(8,128)}, f32[5,16,16,256]{3,2,1,0:T(8,128)S(1)}, u32[]{:S(2)}) copy-start(f32[5,16,16,256]{3,2,1,0:T(8,128)S(1)} %collective-permute-done.13.refs_1_) | copy-start | bytes 3932164
  507.6 266.0 %collective-permute-start.5 = (f32[5,4,256,256]{3,2,1,0:T(8,128)}, f32[5,4,256,256]{3,2,1,0:T(8,128)}, u32[]{:S(2)}, u32[]{:S(2)}) collective-permute-start(f32[5,4,256,256]{3,2,1,0:T(8,128)} %get-tuple-element.61), channel_id=1, source_target_pairs={{0,24},{8,16},{16,8},{24,0},{1,25},{9,17},{17,9},{25,1},{2,26},{10... | collective-permute-start | bytes 15728648 | tf_op jit(solution)/shard_map/ppermute | solution.py:342
  509.8 157.8 %copy-start.2 = (f32[5,16,16,256]{3,2,1,0:T(8,128)}, f32[5,16,16,256]{3,2,1,0:T(8,128)S(1)}, u32[]{:S(2)}) copy-start(f32[5,16,16,256]{3,2,1,0:T(8,128)S(1)} %collective-permute-done.14.refs_2_) | copy-start | bytes 3932164
  509.8 86.4 %collective-permute-start.16 = (f32[5,16,16,256]{3,2,1,0:T(8,128)}, f32[5,16,16,256]{3,2,1,0:T(8,128)}, u32[]{:S(2)}, u32[]{:S(2)}) collective-permute-start(f32[5,16,16,256]{3,2,1,0:T(8,128)} %get-tuple-element.77), channel_id=1, source_target_pairs={{0,4},{1,5},{2,6},{3,7},{4,0},{5,1},{6,2},{7,3},{8,12},{9,13},{10,... | collective-permute-start | bytes 3932168 | tf_op jit(solution)/shard_map/ppermute | solution.py:342
  511.6 140.7 %collective-permute-start.17 = (f32[5,16,16,256]{3,2,1,0:T(8,128)}, f32[5,16,16,256]{3,2,1,0:T(8,128)}, u32[]{:S(2)}, u32[]{:S(2)}) collective-permute-start(f32[5,16,16,256]{3,2,1,0:T(8,128)} %get-tuple-element.78), channel_id=1, source_target_pairs={{0,5},{1,4},{2,7},{3,6},{4,1},{5,0},{6,3},{7,2},{8,13},{9,12},{10,... | collective-permute-start | bytes 3932168 | tf_op jit(solution)/shard_map/ppermute | solution.py:342
  596.2 114.1 %collective-permute-start.18 = (f32[5,16,16,256]{3,2,1,0:T(8,128)}, f32[5,16,16,256]{3,2,1,0:T(8,128)}, u32[]{:S(2)}, u32[]{:S(2)}) collective-permute-start(f32[5,16,16,256]{3,2,1,0:T(8,128)} %get-tuple-element.79), channel_id=1, source_target_pairs={{0,6},{1,7},{2,4},{3,5},{4,2},{5,3},{6,0},{7,1},{8,14},{9,15},{10,... | collective-permute-start | bytes 3932168 | tf_op jit(solution)/shard_map/ppermute | solution.py:342
  652.4 86.0 %collective-permute-start.19 = (f32[5,16,16,256]{3,2,1,0:T(8,128)}, f32[5,16,16,256]{3,2,1,0:T(8,128)}, u32[]{:S(2)}, u32[]{:S(2)}) collective-permute-start(f32[5,16,16,256]{3,2,1,0:T(8,128)} %get-tuple-element.80), channel_id=1, source_target_pairs={{0,7},{1,6},{2,5},{3,4},{4,3},{5,2},{6,1},{7,0},{8,15},{9,14},{10,... | collective-permute-start | bytes 3932168 | tf_op jit(solution)/shard_map/ppermute | solution.py:342
  710.3 28.1 %collective-permute-start.27 = (f32[5,16,16,256]{3,2,1,0:T(8,128)}, f32[5,16,16,256]{3,2,1,0:T(8,128)S(1)}, u32[]{:S(2)}, u32[]{:S(2)}) collective-permute-start(f32[5,16,16,256]{3,2,1,0:T(8,128)} %get-tuple-element.93), channel_id=1, source_target_pairs={{0,1},{1,0},{2,3},{3,2},{4,5},{5,4},{6,7},{7,6},{8,9},{9,8},{10,11... | collective-permute-start | bytes 3932168 | tf_op jit(solution)/shard_map/ppermute | solution.py:342
  738.4 30.2 %collective-permute-start.28 = (f32[5,16,16,256]{3,2,1,0:T(8,128)}, f32[5,16,16,256]{3,2,1,0:T(8,128)S(1)}, u32[]{:S(2)}, u32[]{:S(2)}) collective-permute-start(f32[5,16,16,256]{3,2,1,0:T(8,128)} %get-tuple-element.94), channel_id=1, source_target_pairs={{0,2},{1,3},{2,0},{3,1},{4,6},{5,7},{6,4},{7,5},{8,10},{9,11},{10,... | collective-permute-start | bytes 3932168 | tf_op jit(solution)/shard_map/ppermute | solution.py:342
  738.4 100.8 %copy-start.3 = (f32[5,16,16,256]{3,2,1,0:T(8,128)}, f32[5,16,16,256]{3,2,1,0:T(8,128)S(1)}, u32[]{:S(2)}) copy-start(f32[5,16,16,256]{3,2,1,0:T(8,128)S(1)} %collective-permute-done.27.refs_1_) | copy-start | bytes 3932164
  738.4 114.1 %collective-permute-start.29 = (f32[5,16,16,256]{3,2,1,0:T(8,128)}, f32[5,16,16,256]{3,2,1,0:T(8,128)}, u32[]{:S(2)}, u32[]{:S(2)}) collective-permute-start(f32[5,16,16,256]{3,2,1,0:T(8,128)} %get-tuple-element.95), channel_id=1, source_target_pairs={{0,3},{1,2},{2,1},{3,0},{4,7},{5,6},{6,5},{7,4},{8,11},{9,10},{10,... | collective-permute-start | bytes 3932168 | tf_op jit(solution)/shard_map/ppermute | solution.py:342
  768.5 70.6 %copy-start.4 = (f32[5,16,16,256]{3,2,1,0:T(8,128)}, f32[5,16,16,256]{3,2,1,0:T(8,128)S(1)}, u32[]{:S(2)}) copy-start(f32[5,16,16,256]{3,2,1,0:T(8,128)S(1)} %collective-permute-done.28.refs_2_) | copy-start | bytes 3932164
  768.5 84.0 %collective-permute-start.30 = (f32[5,16,16,256]{3,2,1,0:T(8,128)}, f32[5,16,16,256]{3,2,1,0:T(8,128)}, u32[]{:S(2)}, u32[]{:S(2)}) collective-permute-start(f32[5,16,16,256]{3,2,1,0:T(8,128)} %get-tuple-element.96), channel_id=1, source_target_pairs={{0,4},{1,5},{2,6},{3,7},{4,0},{5,1},{6,2},{7,3},{8,12},{9,13},{10,... | collective-permute-start | bytes 3932168 | tf_op jit(solution)/shard_map/ppermute | solution.py:342
  769.0 4.6 copy-start
  769.0 167.5 %collective-permute-start.31 = (f32[5,16,16,256]{3,2,1,0:T(8,128)}, f32[5,16,16,256]{3,2,1,0:T(8,128)}, u32[]{:S(2)}, u32[]{:S(2)}) collective-permute-start(f32[5,16,16,256]{3,2,1,0:T(8,128)} %get-tuple-element.97), channel_id=1, source_target_pairs={{0,5},{1,4},{2,7},{3,6},{4,1},{5,0},{6,3},{7,2},{8,13},{9,12},{10,... | collective-permute-start | bytes 3932168 | tf_op jit(solution)/shard_map/ppermute | solution.py:342
  773.1 193.2 %collective-permute-start.32 = (f32[5,16,16,256]{3,2,1,0:T(8,128)}, f32[5,16,16,256]{3,2,1,0:T(8,128)}, u32[]{:S(2)}, u32[]{:S(2)}) collective-permute-start(f32[5,16,16,256]{3,2,1,0:T(8,128)} %get-tuple-element.98), channel_id=1, source_target_pairs={{0,6},{1,7},{2,4},{3,5},{4,2},{5,3},{6,0},{7,1},{8,14},{9,15},{10,... | collective-permute-start | bytes 3932168 | tf_op jit(solution)/shard_map/ppermute | solution.py:342
  773.6 222.4 %collective-permute-start.33 = (f32[5,16,16,256]{3,2,1,0:T(8,128)}, f32[5,16,16,256]{3,2,1,0:T(8,128)}, u32[]{:S(2)}, u32[]{:S(2)}) collective-permute-start(f32[5,16,16,256]{3,2,1,0:T(8,128)} %get-tuple-element.99), channel_id=1, source_target_pairs={{0,7},{1,6},{2,5},{3,4},{4,3},{5,2},{6,1},{7,0},{8,15},{9,14},{10,... | collective-permute-start | bytes 3932168 | tf_op jit(solution)/shard_map/ppermute | solution.py:342
  (2 other events, 2.2 us)

commit v2 on v1

v2 whole, which is shorter than its diff:
```python
import functools

import jax
import jax.numpy as jnp
from jax import lax
from jax.experimental import pallas as pl
from jax.experimental.pallas import tpu as pltpu
from jax.sharding import PartitionSpec as P

gamma_less = 0.4
time_step = 0.1
vmem_bytes = 56 * 1024 * 1024


def divisor_up_to(number, limit):
    return max(d for d in range(1, limit + 1) if number % d == 0)


def hop(index, step, size, sign):
    if size & (size - 1) == 0:
        return index ^ step
    return (index + sign * step) % size


def fluxes(fields, direction):
    density, momentum, energy = fields[0], fields[1:4], fields[4]
    inverse = 1.0 / density
    velocity = momentum[direction] * inverse
    square = momentum[0] * momentum[0] + momentum[1] * momentum[1] + momentum[2] * momentum[2]
    pressure = gamma_less * (energy - 0.5 * square * inverse)
    out = [momentum[direction]]
    for column in range(3):
        product = momentum[column] * velocity
        if column == direction:
            product = product + pressure
        out.append(product)
    out.append((energy + pressure) * velocity)
    return out


def halves(value):
    high = value.astype(jnp.bfloat16)
    low = (value - high.astype(jnp.float32)).astype(jnp.bfloat16)
    return high, low


def split_outside(value):
    high = lax.reduce_precision(value, exponent_bits=8, mantissa_bits=7)
    return high.astype(jnp.bfloat16), (value - high).astype(jnp.bfloat16)


def dot(a, b):
    return jnp.dot(a, b, preferred_element_type=jnp.float32)


def call(body, name, order, operands, grid, in_specs, out_specs, out_shape, scratch=(), aliases=None, flops=0):
    scalars = tuple(order)
    moved = sum(4 * o.size for o in operands) + sum(4 * o.size for o in jax.tree.leaves(out_shape))
    return pl.pallas_call(
        body,
        name=name,
        grid_spec=pltpu.PrefetchScalarGridSpec(
            num_scalar_prefetch=len(scalars),
            grid=grid,
            in_specs=in_specs,
            out_specs=out_specs,
            scratch_shapes=list(scratch),
        ),
        out_shape=out_shape,
        input_output_aliases={} if aliases is None else aliases,
        compiler_params=pltpu.CompilerParams(vmem_limit_bytes=vmem_bytes),
        cost_estimate=pl.CostEstimate(flops=flops, bytes_accessed=moved, transcendentals=0),
    )(*scalars, *operands)


def pack_span_kernel(order, density, momentum, energy, piece):
    piece[0] = density[0]
    for column in range(3):
        piece[1 + column] = momentum[column, 0]
    piece[4] = energy[0]


def pack_span(order, chunk, chunks, density, momentum, energy):
    _, share, zl, nx = density.shape
    rows = share // chunks
    r = divisor_up_to(rows, 8)
    first = chunk * (rows // r)
    flat = pl.BlockSpec((1, r, zl, nx), lambda i, s: (s[0], first + i, 0, 0))
    return call(
        pack_span_kernel,
        f"pack_span_{chunk}",
        (order,),
        (density, momentum, energy),
        (rows // r,),
        [flat, pl.BlockSpec((3, 1, r, zl, nx), lambda i, s: (0, s[0], first + i, 0, 0)), flat],
        pl.BlockSpec((5, r, zl, nx), lambda i, s: (0, i, 0, 0)),
        jax.ShapeDtypeStruct((5, rows, zl, nx), jnp.float32),
    )


def span_kernel(n, weights, both, *refs):
    pieces, outs = refs[:n], refs[n:]
    _, r, zl, nx = pieces[0].shape
    nz = n * zl

    @pl.loop(0, r)
    def _(row):
        weight = weights[pl.program_id(0) * r + row]
        fields = [jnp.concatenate([p[f, row] for p in pieces], axis=0) for f in range(5)]
        for f, flux in enumerate(fluxes(fields, 2)):
            high, low = halves(jnp.concatenate([flux, weight * fields[f]], axis=0))
            total = dot(both[...], high)
            total = total[:nz] + total[nz:] + dot(both[:nz], low)
            for k, out in enumerate(outs):
                out[f, row] = total[k * zl : (k + 1) * zl]


def span_terms(chunk, weights, both, pieces):
    n = len(pieces)
    _, rows, zl, nx = pieces[0].shape
    r = divisor_up_to(rows, 2)
    nz = n * zl
    spec = pl.BlockSpec((5, r, zl, nx), lambda i, s: (0, i, 0, 0))
    return call(
        functools.partial(span_kernel, n),
        f"span_terms_{chunk}",
        (weights,),
        (both, *pieces),
        (rows // r,),
        [pl.BlockSpec(both.shape, lambda i, s: (0, 0))] + [spec] * n,
        [spec] * n,
        [jax.ShapeDtypeStruct(p.shape, jnp.float32) for p in pieces],
        flops=5 * rows * 6 * nz * 2 * nz * nx,
    )


def pack_wall_kernel(zl, density, momentum, energy, pieces, narrow):
    m, _, zz, rows, nx = pieces.shape
    lane = narrow.shape[-1]
    for half in range(nx // lane):
        lanes = slice(half * lane, (half + 1) * lane)
        narrow[half, 0] = density[:, lanes]
        for column in range(3):
            narrow[half, 1 + column] = momentum[column, :, lanes]
        narrow[half, 4] = energy[:, lanes]
    for z in range(zl):
        lines = pl.ds(z, rows, stride=zl)
        for half in range(nx // lane):
            lanes = slice(half * lane, (half + 1) * lane)
            for f in range(5):
                pieces[z // zz, f, z % zz, :, lanes] = narrow[half, f, lines, :]


def pack_wall(m, density, momentum, energy):
    jl, zl, nx = density.shape
    zz = zl // m
    lane = divisor_up_to(nx, 128)
    rows = divisor_up_to(jl, 32)
    flat = pl.BlockSpec((rows * zl, nx), lambda i: (i, 0))
    return call(
        functools.partial(pack_wall_kernel, zl),
        "pack_wall",
        (),
        (density.reshape(jl * zl, nx), momentum.reshape(3, jl * zl, nx), energy.reshape(jl * zl, nx)),
        (jl // rows,),
        [flat, pl.BlockSpec((3, rows * zl, nx), lambda i: (0, i, 0)), flat],
        pl.BlockSpec((m, 5, zz, rows, nx), lambda i: (0, 0, 0, i, 0)),
        jax.ShapeDtypeStruct((m, 5, zz, jl, nx), jnp.float32),
        scratch=[pltpu.VMEM((nx // lane, 5, rows * zl, lane), jnp.float32)],
    )


def wall_kernel(high, low, damping, pieces, outs, kept, flux_high, flux_low):
    m, _, _, jl, nx = pieces.shape
    ny = m * jl
    step = divisor_up_to(jl, 32)
    for f in range(5):
        kept[f, 0:8] = jnp.zeros((8, nx), jnp.float32)
        kept[f, 8 + ny : 16 + ny] = jnp.zeros((8, nx), jnp.float32)
    for k in range(m):

        @pl.loop(0, jl // step)
        def _(i):
            here = pl.ds(pl.multiple_of(i * step, step), step)
            there = pl.multiple_of(k * jl + i * step, step)
            fields = [pieces[k, f, 0, here, :] for f in range(5)]
            for f, flux in enumerate(fluxes(fields, 1)):
                kept[f, pl.ds(there + 8, step), :] = fields[f]
                flux_high[f, pl.ds(there, step), :], flux_low[f, pl.ds(there, step), :] = halves(flux)

    for k in range(m):
        first = k * jl
        rows = pl.ds(first, jl)

        @pl.loop(0, 5)
        def _(f):
            total = dot(high[rows, :], flux_high[f]) + dot(low[rows, :], flux_high[f])
            outs[k, f, 0] = total + dot(high[rows, :], flux_low[f])
            part = divisor_up_to(jl, 64)

            @pl.loop(0, jl // part)
            def _(i):
                at = pl.multiple_of(i * part, part)
                c = kept[f, pl.ds(first + at, part + 16), :]

                def shifted(offset):
                    return c[8 + offset : 8 + offset + part]

                fourth = (
                    shifted(-2) - 4.0 * shifted(-1) + 6.0 * shifted(0) - 4.0 * shifted(1) + shifted(2)
                )
                weight = damping[pl.ds(first + at, part), :]
                outs[k, f, 0, pl.ds(at, part), :] += weight * fourth


def wall_terms(operator, damping, pieces):
    m, _, zz, jl, nx = pieces.shape
    ny = m * jl
    high, low = split_outside(operator)
    spec = pl.BlockSpec((m, 5, 1, jl, nx), lambda i: (0, 0, i, 0, 0))
    whole = pl.BlockSpec((ny, ny), lambda i: (0, 0))
    return call(
        wall_kernel,
        "wall_terms",
        (),
        (high, low, damping.reshape(ny, 1), pieces),
        (zz,),
        [whole, whole, pl.BlockSpec((ny, 1), lambda i: (0, 0)), spec],
        spec,
        jax.ShapeDtypeStruct(pieces.shape, jnp.float32),
        scratch=[
            pltpu.VMEM((5, ny + 16, nx), jnp.float32),
            pltpu.VMEM((5, ny, nx), jnp.bfloat16),
            pltpu.VMEM((5, ny, nx), jnp.bfloat16),
        ],
        flops=6 * 5 * zz * ny * ny * nx,
    )


def base_kernel(zl, density, momentum, energy, pieces, *refs):
    outs, wall = refs[:3], refs[3]
    _, _, zz, rows, nx = pieces.shape
    lane = wall.shape[-1]
    for z in range(zl):
        lines = pl.ds(z, rows, stride=zl)
        for half in range(nx // lane):
            lanes = slice(half * lane, (half + 1) * lane)
            for f in range(5):
                wall[half, f, lines, :] = pieces[z // zz, f, z % zz, :, lanes]
    part = 16

    @pl.loop(0, rows * zl // part)
    def _(i):
        here = pl.ds(pl.multiple_of(i * part, part), part)
        fields = [density[here, :]] + [momentum[column, here, :] for column in range(3)] + [energy[here, :]]
        column = lax.broadcasted_iota(jnp.int32, (part, nx), 1)
        for f, flux in enumerate(fluxes(fields, 0)):
            first, last = flux[:, :1], flux[:, nx - 1 :]
            above1 = jnp.where(column >= nx - 1, last, pltpu.roll(flux, nx - 1, 1))
            above2 = jnp.where(column >= nx - 2, last, pltpu.roll(flux, nx - 2, 1))
            below1 = jnp.where(column < 1, first, pltpu.roll(flux, 1, 1))
            below2 = jnp.where(column < 2, first, pltpu.roll(flux, 2, 1))
            along = (8.0 * (above1 - below1) - (above2 - below2)) * (1.0 / 12.0)
            across = jnp.concatenate([wall[half, f, here, :] for half in range(wall.shape[0])], axis=1)
            value = fields[f] - time_step * (along + across)
            if f == 0:
                outs[0][here, :] = value
            elif f == 4:
                outs[2][here, :] = value
            else:
                outs[1][f - 1, here, :] = value


def base_fields(density, momentum, energy, pieces):
    m = pieces.shape[0]
    jl, zl, nx = density.shape
    zz = zl // m
    lane = divisor_up_to(nx, 128)
    rows = divisor_up_to(jl, 16)
    flat = pl.BlockSpec((rows * zl, nx), lambda i: (i, 0))
    three = pl.BlockSpec((3, rows * zl, nx), lambda i: (0, i, 0))
    shape = jax.ShapeDtypeStruct((jl * zl, nx), jnp.float32)
    outs = call(
        functools.partial(base_kernel, zl),
        "base_fields",
        (),
        (density.reshape(jl * zl, nx), momentum.reshape(3, jl * zl, nx), energy.reshape(jl * zl, nx), pieces),
        (jl // rows,),
        [flat, three, flat, pl.BlockSpec((m, 5, zz, rows, nx), lambda i: (0, 0, 0, i, 0))],
        [flat, three, flat],
        [shape, jax.ShapeDtypeStruct((3, jl * zl, nx), jnp.float32), shape],
        scratch=[pltpu.VMEM((nx // lane, 5, rows * zl, lane), jnp.float32)],
    )
    return outs


def add_span_kernel(order, density, momentum, energy, *refs):
    pieces, outs = refs[:-3], refs[-3:]
    for k, piece in enumerate(pieces):

        @pl.when(pl.program_id(0) == k)
        def _():
            outs[0][0] = density[0] - time_step * piece[0]
            for column in range(3):
                outs[1][column, 0] = momentum[column, 0] - time_step * piece[1 + column]
            outs[2][0] = energy[0] - time_step * piece[4]


def add_span(order, chunk, chunks, fields, pieces):
    share, zl, nx = fields[0].shape[1:]
    rows = share // chunks
    r = divisor_up_to(rows, 8)
    steps = rows // r
    first = chunk * steps
    flat = pl.BlockSpec((1, r, zl, nx), lambda p, i, s: (s[p], first + i, 0, 0))
    three = pl.BlockSpec((3, 1, r, zl, nx), lambda p, i, s: (0, s[p], first + i, 0, 0))

    def own(k):
        def index(p, i, s):
            return 0, jnp.where(p == k, i, jnp.where(p < k, 0, steps - 1)), 0, 0

        return pl.BlockSpec((5, r, zl, nx), index)

    return call(
        add_span_kernel,
        f"add_span_{chunk}",
        (order,),
        (*fields, *pieces),
        (len(pieces), steps),
        [flat, three, flat] + [own(k) for k in range(len(pieces))],
        [flat, three, flat],
        [jax.ShapeDtypeStruct(f.shape, f.dtype) for f in fields],
        aliases={1: 0, 2: 1, 3: 2},
    )


def after(value, earlier):
    if len(earlier) == 0:
        return value
    return lax.optimization_barrier((value, *earlier))[0]


class Sender:
    def __init__(self, axis, size, width):
        self.axis, self.size, self.width, self.far = axis, size, width, []

    def permute(self, piece, step, sign, earlier):
        pairs = [(i, hop(i, step, self.size, sign)) for i in range(self.size)]
        return lax.ppermute(after(piece, earlier), self.axis, pairs)

    def exchange(self, pieces, sign, earlier=()):
        pieces = list(pieces)
        first = self.size // 2
        sent = []
        for k in range(self.size - 1, first - 1, -1):
            held = [self.far[-self.width]] if len(self.far) >= self.width else []
            pieces[k] = self.permute(pieces[k], k, sign, [*held, *earlier])
            self.far.append(pieces[k])
            sent.append(pieces[k])
        for j, k in enumerate(range(1, first)):
            pieces[k] = self.permute(pieces[k], k, sign, [sent[j]])
        return pieces


def local(density, momentum, energy, wall_operator, span_operator, damping, *, chunks):
    jl, zl, nx = density.shape
    nz = span_operator.shape[0]
    m, n = lax.axis_size("gy"), lax.axis_size("gz")
    gy, gz = lax.axis_index("gy"), lax.axis_index("gz")
    share = jl // n
    chunks = divisor_up_to(share, chunks)
    rows = share // chunks

    span_to = [jnp.asarray(hop(gz, k, n, 1), jnp.int32).reshape(1) for k in range(n)]
    span_from = jnp.concatenate([jnp.asarray(hop(gz, k, n, -1), jnp.int32).reshape(1) for k in range(n)])
    by_share = (
        density.reshape(n, share, zl, nx),
        momentum.reshape(3, n, share, zl, nx),
        energy.reshape(n, share, zl, nx),
    )
    far, near = list(range(n // 2, n))[::-1], list(range(1, n // 2))
    sender = Sender("gz", n, 4)

    packs = [[pack_span(span_to[k], c, chunks, *by_share) for k in range(n)] for c in range(chunks)]
    packed = pack_wall(m, after(density, packs[0]), momentum, energy)
    wall_out = lax.all_to_all(packed, "gy", split_axis=0, concat_axis=0, tiled=True)
    span_out = [sender.exchange(packs[c], 1, [] if c == 0 else [packed]) for c in range(chunks)]

    identity = jnp.eye(nz, dtype=jnp.float32)
    fourth = 6.0 * identity
    for offset, factor in ((1, -4.0), (-1, -4.0), (2, 1.0), (-2, 1.0)):
        fourth = fourth + factor * jnp.roll(identity, offset, 1)

    def in_order_of_arrival(matrix):
        blocks = matrix.reshape(n, zl, n, zl)
        blocks = jnp.take(jnp.take(blocks, span_from, axis=0), span_from, axis=2)
        return blocks.reshape(nz, nz)

    both = jnp.concatenate([in_order_of_arrival(span_operator), in_order_of_arrival(fourth)], axis=1)
    both = jnp.concatenate(split_outside(both), axis=0)

    def weights(c):
        return lax.dynamic_slice_in_dim(damping, gy * jl + gz * share + c * rows, rows)

    span_back = [sender.exchange(span_terms(0, weights(0), both, span_out[0]), -1)]
    begun = span_out[-1][far[0]] if chunks > 1 else wall_out
    wall_back = wall_terms(wall_operator, damping, after(wall_out, [begun]))
    wall_back = lax.all_to_all(wall_back, "gy", split_axis=0, concat_axis=0, tiled=True)
    for c in range(1, chunks):
        span_back.append(sender.exchange(span_terms(c, weights(c), both, span_out[c]), -1))

    middle = span_back[0][far[n // 4]]
    fields = base_fields(density, momentum, energy, after(wall_back, [middle]))
    fields = (
        fields[0].reshape(n, share, zl, nx),
        fields[1].reshape(3, n, share, zl, nx),
        fields[2].reshape(n, share, zl, nx),
    )
    groups = [(c, [0, *near, *far]) for c in range(chunks - 1)]
    groups += [(chunks - 1, g) for g in ([0, *near], far[: n // 4], far[n // 4 :]) if g]
    for c, group in groups:
        order = jnp.concatenate([span_to[k] for k in group])
        fields = add_span(order, c, chunks, fields, [span_back[c][k] for k in group])
    return (
        fields[0].reshape(jl, zl, nx),
        fields[1].reshape(3, jl, zl, nx),
        fields[2].reshape(jl, zl, nx),
    )


def solution(mesh):
    in_specs = (P("gy", "gz", None), P(None, "gy", "gz", None), P("gy", "gz", None), P(), P(), P())
    out_specs = (P("gy", "gz", None), P(None, "gy", "gz", None), P("gy", "gz", None))
    return jax.shard_map(
        functools.partial(local, chunks=2), mesh=mesh, in_specs=in_specs, out_specs=out_specs, check_vma=False
    )
```

time: 1010 us -> 1210 us (1.20)
  waiting for transfers between devices: 705 us -> 845 us
  starting transfers between devices: 40.5 us -> 74.2 us
  Pallas kernels: 246 us -> 270 us
    all_to_all x0 -> x2, waiting for transfers between devices: none -> 106 us  [the longest x1 106 us: local(): lax.all_to_all(packed, 'gy', split_axis=0, concat_axis=0, tiled=True)]
    ppermute x34 -> x28, waiting for transfers between devices: 705 us -> 739 us  [permute(): return lax.ppermute(after(piece, earlier), self.axis, pairs)]
    pallas_call x9 -> x25, Pallas kernels: 246 us -> 270 us  [call(): pl.pallas_call(body, name=name, grid_spec=pltpu.PrefetchScalarGridSpec(nu...]
    all_to_all x0 -> x2, starting transfers between devices: none -> 16.9 us  [the longest x1 8.91 us: local(): lax.all_to_all(wall_back, 'gy', split_axis=0, concat_axis=0, tiled=True)]
    ppermute x34 -> x28, starting transfers between devices: 40.5 us -> 57.3 us  [permute(): return lax.ppermute(after(piece, earlier), self.axis, pairs)]
  transfers between devices with their start and end apart: 34 -> 30, of which waited for: 17 -> 16; matrix products, arithmetic and copies ran while one was open for 1% -> 1% of each run, Pallas kernels for 22% -> 12%
where the time goes in v2:
time: 1210 us
  waiting for transfers between devices  845 us (70%)
  Pallas kernels  270 us (22%)
  starting transfers between devices  74.2 us (6%)
    ppermute x28, waiting for transfers between devices, permute(): return lax.ppermute(after(piece, earlier), self.axis, pairs)  739 us
    pallas_call x25, Pallas kernels, call(): pl.pallas_call(body, name=name, grid_spec=pltpu.PrefetchScalarGridSpec(nu...  270 us
    all_to_all x1, waiting for transfers between devices, local(): lax.all_to_all(packed, 'gy', split_axis=0, concat_axis=0, tiled=True)  106 us
    ppermute x28, starting transfers between devices, permute(): return lax.ppermute(after(piece, earlier), self.axis, pairs)  57.3 us
  transfers between devices with their start and end apart: 30, of which 16 were waited for; matrix products, arithmetic and copies ran while one was open for 1% of the time, Pallas kernels for 12%

profile of v2, /device:TPU:15, one launch (start us, length us, event | category | flops | bytes accessed | tf_op | source)
XLA Modules:
  0.0 1206.2 jit_solution(11734108278386370529)
XLA Ops:
  0.7 2.3 pack_span_0.9
  5.2 2.3 pack_span_0.11
  7.4 2.2 pack_span_0.12
  9.6 2.2 pack_span_0.13
  18.4 20.3 %pack_wall.1 = f32[4,5,4,256,256]{4,3,2,1,0:T(8,128)} custom-call(f32[4096,256]{1,0:T(8,128)} %bitcast.56, f32[3,4096,256]{2,1,0:T(8,128)} %bitcast.38, f32[4096,256]{1,0:T(8,128)} %bitcast.74), custom_call_target="tpu_custom_call" | custom-call | bytes 41943040 | tf_op jit(solution)/shard_map/pack_wall/pallas_call | solution.py:59
  38.8 8.0 all-to-all-start
  48.9 2.3 pack_span_1.8
  51.2 83.5 %collective-permute-done.refs_7_ = f32[5,16,16,256]{3,2,1,0:T(8,128)S(1)} collective-permute-done((f32[5,16,16,256]{3,2,1,0:T(8,128)S(1)}, f32[5,16,16,256]{3,2,1,0:T(8,128)S(1)}, u32[]{:S(2)}, u32[]{:S(2)}) %collective-permute-start) | collective-permute-done | bytes 1310752 | tf_op jit(solution)/shard_map/ppermute | solution.py:349
  137.0 5.1 fusion
  142.1 23.8 %collective-permute-done.1.refs_7_ = f32[5,16,16,256]{3,2,1,0:T(8,128)S(1)} collective-permute-done((f32[5,16,16,256]{3,2,1,0:T(8,128)}, f32[5,16,16,256]{3,2,1,0:T(8,128)S(1)}, u32[]{:S(2)}, u32[]{:S(2)}) %collective-permute-start.1) | collective-permute-done | bytes 1310752 | tf_op jit(solution)/shard_map/ppermute | solution.py:349
  165.9 106.4 %all-to-all-done.pieces = f32[4,5,4,256,256]{4,3,2,1,0:T(8,128)} async-done(((f32[4,5,4,256,256]{4,3,2,1,0:T(8,128)}), f32[4,5,4,256,256]{4,3,2,1,0:T(8,128)}, u32[]{:S(2)}, u32[]{:S(2)}) %all-to-all-start) | async-done | bytes 20971552 | tf_op jit(solution)/shard_map/all_to_all | solution.py:386
  272.3 83.3 %wall_terms.1 = f32[4,5,4,256,256]{4,3,2,1,0:T(8,128)} custom-call(bf16[1024,1024]{1,0:T(8,128)(2,1)} %get-tuple-element.122.high, bf16[1024,1024]{1,0:T(8,128)(2,1)} %get-tuple-element.121.low, f32[1024,1]{1,0:T(8,128)} %copy.24.damping, f32[4,5,4,256,256]{4,3,2,1,0:T(8,128)} %all-to-all-done.pieces), custom_call_target="tpu_custom_call" | custom-call | flops 32212254720 | bytes 50335744 | tf_op jit(solution)/shard_map/wall_terms/pallas_call | solution.py:59
  355.6 8.9 all-to-all-start.1
  365.8 2.7 collective-permute-start.5
  370.1 2.3 pack_span_1.13
  372.4 2.2 pack_span_1.10
  381.3 2.2 pack_span_1.11
  385.3 121.6 %collective-permute-done.3.refs_6_ = f32[5,16,16,256]{3,2,1,0:T(8,128)} collective-permute-done((f32[5,16,16,256]{3,2,1,0:T(8,128)}, f32[5,16,16,256]{3,2,1,0:T(8,128)}, u32[]{:S(2)}, u32[]{:S(2)}) %collective-permute-start.3) | collective-permute-done | bytes 1310752 | tf_op jit(solution)/shard_map/ppermute | solution.py:349
  507.2 25.9 %collective-permute-done.5.refs_5_ = f32[5,16,16,256]{3,2,1,0:T(8,128)} collective-permute-done((f32[5,16,16,256]{3,2,1,0:T(8,128)}, f32[5,16,16,256]{3,2,1,0:T(8,128)}, u32[]{:S(2)}, u32[]{:S(2)}) %collective-permute-start.5) | collective-permute-done | bytes 1310752 | tf_op jit(solution)/shard_map/ppermute | solution.py:349
  533.1 3.4 collective-permute-start.8
  536.5 4.3 collective-permute-start.2
  540.7 48.6 %collective-permute-done.7.refs_4_ = f32[5,16,16,256]{3,2,1,0:T(8,128)} collective-permute-done((f32[5,16,16,256]{3,2,1,0:T(8,128)}, f32[5,16,16,256]{3,2,1,0:T(8,128)}, u32[]{:S(2)}, u32[]{:S(2)}) %collective-permute-start.7) | collective-permute-done | bytes 1310752 | tf_op jit(solution)/shard_map/ppermute | solution.py:349
  589.3 5.5 collective-permute-start.6
  600.0 19.3 %collective-permute-done.12.refs_6_ = f32[5,16,16,256]{3,2,1,0:T(8,128)} collective-permute-done((f32[5,16,16,256]{3,2,1,0:T(8,128)}, f32[5,16,16,256]{3,2,1,0:T(8,128)}, u32[]{:S(2)}, u32[]{:S(2)}) %collective-permute-start.12) | collective-permute-done | bytes 1310752 | tf_op jit(solution)/shard_map/ppermute | solution.py:349
  619.4 54.2 %collective-permute-done.8.refs_5_ = f32[5,16,16,256]{3,2,1,0:T(8,128)} collective-permute-done((f32[5,16,16,256]{3,2,1,0:T(8,128)}, f32[5,16,16,256]{3,2,1,0:T(8,128)}, u32[]{:S(2)}, u32[]{:S(2)}) %collective-permute-start.8) | collective-permute-done | bytes 1310752 | tf_op jit(solution)/shard_map/ppermute | solution.py:349
  673.6 4.5 collective-permute-start.18
  679.8 13.8 %span_terms_0.1 = (f32[5,16,16,256]{3,2,1,0:T(8,128)}, f32[5,16,16,256]{3,2,1,0:T(8,128)}, f32[5,16,16,256]{3,2,1,0:T(8,128)}, f32[5,16,16,256]{3,2,1,0:T(8,128)...) custom-call(f32[16]{0:T(128)} %get-tuple-element.134.weights, ...), custom_call_target="tpu_custom_call" | custom-call | flops 4026531840 | bytes 21233664 | tf_op jit(solution)/shard_map/span_terms_0/pallas_call | solution.py:59
  693.6 2.6 collective-permute-start.9
  698.4 3.4 collective-permute-done.16.refs_4_
  703.0 4.9 collective-permute-start.10
  707.9 51.8 %collective-permute-done.19.refs_2_ = f32[5,16,16,256]{3,2,1,0:T(8,128)S(1)} collective-permute-done((f32[5,16,16,256]{3,2,1,0:T(8,128)}, f32[5,16,16,256]{3,2,1,0:T(8,128)S(1)}, u32[]{:S(2)}, u32[]{:S(2)}) %collective-permute-start.19) | collective-permute-done | bytes 1310752 | tf_op jit(solution)/shard_map/ppermute | solution.py:349
  759.7 84.2 %collective-permute-done.20.refs_3_ = f32[5,16,16,256]{3,2,1,0:T(8,128)} collective-permute-done((f32[5,16,16,256]{3,2,1,0:T(8,128)S(1)}, f32[5,16,16,256]{3,2,1,0:T(8,128)}, u32[]{:S(2)}, u32[]{:S(2)}) %collective-permute-start.20) | collective-permute-done | bytes 1310752 | tf_op jit(solution)/shard_map/ppermute | solution.py:349
  843.9 14.0 %span_terms_1.1 = (f32[5,16,16,256]{3,2,1,0:T(8,128)}, f32[5,16,16,256]{3,2,1,0:T(8,128)}, f32[5,16,16,256]{3,2,1,0:T(8,128)}, f32[5,16,16,256]{3,2,1,0:T(8,128)...) custom-call(f32[16]{0:T(128)} %get-tuple-element.133.weights, ...), custom_call_target="tpu_custom_call" | custom-call | flops 4026531840 | bytes 21233664 | tf_op jit(solution)/shard_map/span_terms_1/pallas_call | solution.py:59
  857.9 3.7 collective-permute-start.25
  861.7 96.4 %collective-permute-done.10.refs_4_ = f32[5,16,16,256]{3,2,1,0:T(8,128)S(1)} collective-permute-done((f32[5,16,16,256]{3,2,1,0:T(8,128)}, f32[5,16,16,256]{3,2,1,0:T(8,128)S(1)}, u32[]{:S(2)}, u32[]{:S(2)}) %collective-permute-start.10) | collective-permute-done | bytes 1310752 | tf_op jit(solution)/shard_map/ppermute | solution.py:349
  958.1 3.2 collective-permute-start.15
  961.3 49.4 %collective-permute-done.25.refs_0_ = f32[5,16,16,256]{3,2,1,0:T(8,128)S(1)} collective-permute-done((f32[5,16,16,256]{3,2,1,0:T(8,128)}, f32[5,16,16,256]{3,2,1,0:T(8,128)S(1)}, u32[]{:S(2)}, u32[]{:S(2)}) %collective-permute-start.25) | collective-permute-done | bytes 1310752 | tf_op jit(solution)/shard_map/ppermute | solution.py:349
  1010.7 4.9 collective-permute-start.14
  1015.6 25.2 %collective-permute-done.23.refs_1_ = f32[5,16,16,256]{3,2,1,0:T(8,128)} collective-permute-done((f32[5,16,16,256]{3,2,1,0:T(8,128)}, f32[5,16,16,256]{3,2,1,0:T(8,128)}, u32[]{:S(2)}, u32[]{:S(2)}) %collective-permute-start.23) | collective-permute-done | bytes 1310752 | tf_op jit(solution)/shard_map/ppermute | solution.py:349
  1040.8 2.5 collective-permute-start.11
  1043.3 27.3 %collective-permute-done.21.refs_0_ = f32[5,16,16,256]{3,2,1,0:T(8,128)} collective-permute-done((f32[5,16,16,256]{3,2,1,0:T(8,128)}, f32[5,16,16,256]{3,2,1,0:T(8,128)}, u32[]{:S(2)}, u32[]{:S(2)}) %collective-permute-start.21) | collective-permute-done | bytes 1310752 | tf_op jit(solution)/shard_map/ppermute | solution.py:349
  1070.6 24.4 %collective-permute-done.17.refs_7_ = f32[5,16,16,256]{3,2,1,0:T(8,128)} collective-permute-done((f32[5,16,16,256]{3,2,1,0:T(8,128)}, f32[5,16,16,256]{3,2,1,0:T(8,128)}, u32[]{:S(2)}, u32[]{:S(2)}) %collective-permute-start.17) | collective-permute-done | bytes 1310752 | tf_op jit(solution)/shard_map/ppermute | solution.py:349
  1095.0 3.2 collective-permute-start.24
  1103.2 64.7 %base_fields.1 = (f32[4096,256]{1,0:T(8,128)}, f32[3,4096,256]{2,1,0:T(8,128)}, f32[4096,256]{1,0:T(8,128)}) custom-call(f32[4096,256]{1,0:T(8,128)} %bitcast.65, f32[3,4096,256]{2,1,0:T(8,128)} %bitcast.47, f32[4096,256]{1,0:T(8,128)} %bitcast.83, f32[4,5,4,256,256]{4,3,2,1,0:T(8,128)} %all-to-all-done.1.pieces), custom_call_target="tpu_custom_call" | custom-call | bytes 62914560 | tf_op jit(solution)/shard_map/base_fields/pallas_call | solution.py:59
  1167.9 18.0 %add_span_0.1 = (f32[8,32,16,256]{3,2,1,0:T(8,128)}, f32[3,8,32,16,256]{4,3,2,1,0:T(8,128)}, f32[8,32,16,256]{3,2,1,0:T(8,128)}) custom-call(s32[8]{0:T(128)} %concatenate.44.order, f32[8,32,16,256]{3,2,1,0:T(8,128)} %bitcast.86, f32[3,8,32,16,256]{4,3,2,1,0:T(8,128)} %bitcast.84, ...), custom_call_target="tpu_custom_call", output_to_operand_aliasing={{0}: (1, {}), {1}: (2, {}), {2}: (3, {})} | custom-call | bytes 52428800 | tf_op jit(solution)/shard_map/add_span_0/pallas_call | solution.py:59
  1185.9 9.5 add_span_1.3
  1195.3 5.4 add_span_1.4
  1200.8 5.4 add_span_1.5
  (102 shorter events, 40.1 us)
Async XLA Ops:
  38.8 8.0 copy-start.5
  38.8 233.5 %all-to-all-start = ((f32[4,5,4,256,256]{4,3,2,1,0:T(8,128)}), f32[4,5,4,256,256]{4,3,2,1,0:T(8,128)}, u32[]{:S(2)}, u32[]{:S(2)}) async-start(f32[4,5,4,256,256]{4,3,2,1,0:T(8,128)} %pack_wall.1), calls=%async_computation | async-start | bytes 41943040 | tf_op jit(solution)/shard_map/all_to_all | solution.py:386
  46.8 89.1 %copy-start.7 = (f32[1024]{0:T(1024)S(1)}, f32[1024]{0:T(1024)}, u32[]{:S(2)}) copy-start(f32[1024]{0:T(1024)} %param.15) | copy-start | bytes 12292
  46.8 87.9 %collective-permute-start = (f32[5,16,16,256]{3,2,1,0:T(8,128)S(1)}, f32[5,16,16,256]{3,2,1,0:T(8,128)S(1)}, u32[]{:S(2)}, u32[]{:S(2)}) collective-permute-start(f32[5,16,16,256]{3,2,1,0:T(8,128)S(1)} %copy-done.5), channel_id=1, source_target_pairs={{0,7},{1,6},{2,5},{3,4},{4,3},{5,2},{6,1},{7,0},{8,15},{9,14},{10,... | collective-permute-start | bytes 3932168 | tf_op jit(solution)/shard_map/ppermute | solution.py:349
  134.7 7.4 copy-start.9
  134.7 31.2 %collective-permute-start.1 = (f32[5,16,16,256]{3,2,1,0:T(8,128)}, f32[5,16,16,256]{3,2,1,0:T(8,128)S(1)}, u32[]{:S(2)}, u32[]{:S(2)}) collective-permute-start(f32[5,16,16,256]{3,2,1,0:T(8,128)} %pack_span_1.8), channel_id=1, source_target_pairs={{0,7},{1,6},{2,5},{3,4},{4,3},{5,2},{6,1},{7,0},{8,15},{9,14},{10,... | collective-permute-start | bytes 3932168 | tf_op jit(solution)/shard_map/ppermute | solution.py:349
  165.9 189.7 %copy-start.8 = (f32[5,16,16,256]{3,2,1,0:T(8,128)}, f32[5,16,16,256]{3,2,1,0:T(8,128)S(1)}, u32[]{:S(2)}) copy-start(f32[5,16,16,256]{3,2,1,0:T(8,128)S(1)} %collective-permute-done.1.refs_7_) | copy-start | bytes 3932164
  355.6 747.6 %all-to-all-start.1 = ((f32[4,5,4,256,256]{4,3,2,1,0:T(8,128)}), f32[4,5,4,256,256]{4,3,2,1,0:T(8,128)}, u32[]{:S(2)}, u32[]{:S(2)}) async-start(f32[4,5,4,256,256]{4,3,2,1,0:T(8,128)} %wall_terms.1), calls=%async_computation.1 | async-start | bytes 41943040 | tf_op jit(solution)/shard_map/all_to_all | solution.py:408
  364.5 142.5 %collective-permute-start.3 = (f32[5,16,16,256]{3,2,1,0:T(8,128)}, f32[5,16,16,256]{3,2,1,0:T(8,128)}, u32[]{:S(2)}, u32[]{:S(2)}) collective-permute-start(f32[5,16,16,256]{3,2,1,0:T(8,128)} %pack_span_0.14), channel_id=1, source_target_pairs={{0,6},{1,7},{2,4},{3,5},{4,2},{5,3},{6,0},{7,1},{8,14},{9,15},{10,... | collective-permute-start | bytes 3932168 | tf_op jit(solution)/shard_map/ppermute | solution.py:349
  365.8 167.3 %collective-permute-start.5 = (f32[5,16,16,256]{3,2,1,0:T(8,128)}, f32[5,16,16,256]{3,2,1,0:T(8,128)}, u32[]{:S(2)}, u32[]{:S(2)}) collective-permute-start(f32[5,16,16,256]{3,2,1,0:T(8,128)} %pack_span_0.13), channel_id=1, source_target_pairs={{0,5},{1,4},{2,7},{3,6},{4,1},{5,0},{6,3},{7,2},{8,13},{9,12},{10,... | collective-permute-start | bytes 3932168 | tf_op jit(solution)/shard_map/ppermute | solution.py:349
  368.5 220.8 %collective-permute-start.7 = (f32[5,16,16,256]{3,2,1,0:T(8,128)}, f32[5,16,16,256]{3,2,1,0:T(8,128)}, u32[]{:S(2)}, u32[]{:S(2)}) collective-permute-start(f32[5,16,16,256]{3,2,1,0:T(8,128)} %pack_span_0.12), channel_id=1, source_target_pairs={{0,4},{1,5},{2,6},{3,7},{4,0},{5,1},{6,2},{7,3},{8,12},{9,13},{10,... | collective-permute-start | bytes 3932168 | tf_op jit(solution)/shard_map/ppermute | solution.py:349
  384.0 0.8 copy-start.6
  507.0 112.4 %collective-permute-start.12 = (f32[5,16,16,256]{3,2,1,0:T(8,128)}, f32[5,16,16,256]{3,2,1,0:T(8,128)}, u32[]{:S(2)}, u32[]{:S(2)}) collective-permute-start(f32[5,16,16,256]{3,2,1,0:T(8,128)} %pack_span_1.10), channel_id=1, source_target_pairs={{0,6},{1,7},{2,4},{3,5},{4,2},{5,3},{6,0},{7,1},{8,14},{9,15},{10,... | collective-permute-start | bytes 3932168 | tf_op jit(solution)/shard_map/ppermute | solution.py:349
  533.1 140.5 %collective-permute-start.8 = (f32[5,16,16,256]{3,2,1,0:T(8,128)}, f32[5,16,16,256]{3,2,1,0:T(8,128)}, u32[]{:S(2)}, u32[]{:S(2)}) collective-permute-start(f32[5,16,16,256]{3,2,1,0:T(8,128)} %pack_span_1.9), channel_id=1, source_target_pairs={{0,5},{1,4},{2,7},{3,6},{4,1},{5,0},{6,3},{7,2},{8,13},{9,12},{10,... | collective-permute-start | bytes 3932168 | tf_op jit(solution)/shard_map/ppermute | solution.py:349
  536.5 141.7 %collective-permute-start.2 = (f32[5,16,16,256]{3,2,1,0:T(8,128)}, f32[5,16,16,256]{3,2,1,0:T(8,128)}, u32[]{:S(2)}, u32[]{:S(2)}) collective-permute-start(f32[5,16,16,256]{3,2,1,0:T(8,128)} %pack_span_0.9), channel_id=1, source_target_pairs={{0,1},{1,0},{2,3},{3,2},{4,5},{5,4},{6,7},{7,6},{8,9},{9,8},{10,11... | collective-permute-start | bytes 3932168 | tf_op jit(solution)/shard_map/ppermute | solution.py:349
  540.7 137.8 %collective-permute-start.4 = (f32[5,16,16,256]{3,2,1,0:T(8,128)}, f32[5,16,16,256]{3,2,1,0:T(8,128)}, u32[]{:S(2)}, u32[]{:S(2)}) collective-permute-start(f32[5,16,16,256]{3,2,1,0:T(8,128)} %pack_span_0.10), channel_id=1, source_target_pairs={{0,2},{1,3},{2,0},{3,1},{4,6},{5,7},{6,4},{7,5},{8,10},{9,11},{10,... | collective-permute-start | bytes 3932168 | tf_op jit(solution)/shard_map/ppermute | solution.py:349
  589.3 90.5 %collective-permute-start.6 = (f32[5,16,16,256]{3,2,1,0:T(8,128)}, f32[5,16,16,256]{3,2,1,0:T(8,128)}, u32[]{:S(2)}, u32[]{:S(2)}) collective-permute-start(f32[5,16,16,256]{3,2,1,0:T(8,128)} %pack_span_0.11), channel_id=1, source_target_pairs={{0,3},{1,2},{2,1},{3,0},{4,7},{5,6},{6,5},{7,4},{8,11},{9,10},{10,... | collective-permute-start | bytes 3932168 | tf_op jit(solution)/shard_map/ppermute | solution.py:349
  598.2 80.3 %copy-start = (f32[5,16,16,256]{3,2,1,0:T(8,128)S(1)}, f32[5,16,16,256]{3,2,1,0:T(8,128)}, u32[]{:S(2)}) copy-start(f32[5,16,16,256]{3,2,1,0:T(8,128)} %pack_span_1.15) | copy-start | bytes 3932164
  619.4 82.4 %collective-permute-start.16 = (f32[5,16,16,256]{3,2,1,0:T(8,128)}, f32[5,16,16,256]{3,2,1,0:T(8,128)}, u32[]{:S(2)}, u32[]{:S(2)}) collective-permute-start(f32[5,16,16,256]{3,2,1,0:T(8,128)} %pack_span_1.11), channel_id=1, source_target_pairs={{0,4},{1,5},{2,6},{3,7},{4,0},{5,1},{6,2},{7,3},{8,12},{9,13},{10,... | collective-permute-start | bytes 3932168 | tf_op jit(solution)/shard_map/ppermute | solution.py:349
  673.6 29.4 %collective-permute-start.18 = (f32[5,16,16,256]{3,2,1,0:T(8,128)}, f32[5,16,16,256]{3,2,1,0:T(8,128)}, u32[]{:S(2)}, u32[]{:S(2)}) collective-permute-start(f32[5,16,16,256]{3,2,1,0:T(8,128)} %pack_span_1.13), channel_id=1, source_target_pairs={{0,1},{1,0},{2,3},{3,2},{4,5},{5,4},{6,7},{7,6},{8,9},{9,8},{10,11... | collective-permute-start | bytes 3932168 | tf_op jit(solution)/shard_map/ppermute | solution.py:349
  678.2 81.6 %collective-permute-start.19 = (f32[5,16,16,256]{3,2,1,0:T(8,128)}, f32[5,16,16,256]{3,2,1,0:T(8,128)S(1)}, u32[]{:S(2)}, u32[]{:S(2)}) collective-permute-start(f32[5,16,16,256]{3,2,1,0:T(8,128)} %pack_span_1.14), channel_id=1, source_target_pairs={{0,2},{1,3},{2,0},{3,1},{4,6},{5,7},{6,4},{7,5},{8,10},{9,11},{10,... | collective-permute-start | bytes 3932168 | tf_op jit(solution)/shard_map/ppermute | solution.py:349
  678.5 165.4 %collective-permute-start.20 = (f32[5,16,16,256]{3,2,1,0:T(8,128)S(1)}, f32[5,16,16,256]{3,2,1,0:T(8,128)}, u32[]{:S(2)}, u32[]{:S(2)}) collective-permute-start(f32[5,16,16,256]{3,2,1,0:T(8,128)S(1)} %copy-done), channel_id=1, source_target_pairs={{0,3},{1,2},{2,1},{3,0},{4,7},{5,6},{6,5},{7,4},{8,11},{9,10},{10,... | collective-permute-start | bytes 3932168 | tf_op jit(solution)/shard_map/ppermute | solution.py:349
  693.6 164.3 %collective-permute-start.9 = (f32[5,16,16,256]{3,2,1,0:T(8,128)}, f32[5,16,16,256]{3,2,1,0:T(8,128)S(1)}, u32[]{:S(2)}, u32[]{:S(2)}) collective-permute-start(f32[5,16,16,256]{3,2,1,0:T(8,128)} %get-tuple-element.71), channel_id=1, source_target_pairs={{0,5},{1,4},{2,7},{3,6},{4,1},{5,0},{6,3},{7,2},{8,13},{9,12},{10,... | collective-permute-start | bytes 3932168 | tf_op jit(solution)/shard_map/ppermute | solution.py:349
  701.7 159.8 %collective-permute-start.13 = (f32[5,16,16,256]{3,2,1,0:T(8,128)}, f32[5,16,16,256]{3,2,1,0:T(8,128)S(1)}, u32[]{:S(2)}, u32[]{:S(2)}) collective-permute-start(f32[5,16,16,256]{3,2,1,0:T(8,128)} %get-tuple-element.84), channel_id=1, source_target_pairs={{0,6},{1,7},{2,4},{3,5},{4,2},{5,3},{6,0},{7,1},{8,14},{9,15},{10,... | collective-permute-start | bytes 3932168 | tf_op jit(solution)/shard_map/ppermute | solution.py:349
  703.0 255.2 %collective-permute-start.10 = (f32[5,16,16,256]{3,2,1,0:T(8,128)}, f32[5,16,16,256]{3,2,1,0:T(8,128)S(1)}, u32[]{:S(2)}, u32[]{:S(2)}) collective-permute-start(f32[5,16,16,256]{3,2,1,0:T(8,128)} %get-tuple-element.79), channel_id=1, source_target_pairs={{0,7},{1,6},{2,5},{3,4},{4,3},{5,2},{6,1},{7,0},{8,15},{9,14},{10,... | collective-permute-start | bytes 3932168 | tf_op jit(solution)/shard_map/ppermute | solution.py:349
  759.7 84.2 %copy-start.11 = (f32[5,16,16,256]{3,2,1,0:T(8,128)}, f32[5,16,16,256]{3,2,1,0:T(8,128)S(1)}, u32[]{:S(2)}) copy-start(f32[5,16,16,256]{3,2,1,0:T(8,128)S(1)} %collective-permute-done.19.refs_2_) | copy-start | bytes 3932164
  843.9 166.8 %copy-start.10 = (f32[5,16,16,256]{3,2,1,0:T(8,128)S(1)}, f32[5,16,16,256]{3,2,1,0:T(8,128)}, u32[]{:S(2)}) copy-start(f32[5,16,16,256]{3,2,1,0:T(8,128)} %get-tuple-element.85) | copy-start | bytes 3932164
  857.9 309.9 %copy-start.2 = (f32[5,16,16,256]{3,2,1,0:T(8,128)}, f32[5,16,16,256]{3,2,1,0:T(8,128)S(1)}, u32[]{:S(2)}) copy-start(f32[5,16,16,256]{3,2,1,0:T(8,128)S(1)} %collective-permute-done.9.refs_6_) | copy-start | bytes 3932164
  857.9 152.8 %collective-permute-start.25 = (f32[5,16,16,256]{3,2,1,0:T(8,128)}, f32[5,16,16,256]{3,2,1,0:T(8,128)S(1)}, u32[]{:S(2)}, u32[]{:S(2)}) collective-permute-start(f32[5,16,16,256]{3,2,1,0:T(8,128)} %get-tuple-element.108), channel_id=1, source_target_pairs={{0,5},{1,4},{2,7},{3,6},{4,1},{5,0},{6,3},{7,2},{8,13},{9,12},{10,... | collective-permute-start | bytes 3932168 | tf_op jit(solution)/shard_map/ppermute | solution.py:349
  861.6 149.1 %copy-start.3 = (f32[5,16,16,256]{3,2,1,0:T(8,128)}, f32[5,16,16,256]{3,2,1,0:T(8,128)S(1)}, u32[]{:S(2)}) copy-start(f32[5,16,16,256]{3,2,1,0:T(8,128)S(1)} %collective-permute-done.13.refs_5_) | copy-start | bytes 3932164
  861.6 179.2 %collective-permute-start.23 = (f32[5,16,16,256]{3,2,1,0:T(8,128)}, f32[5,16,16,256]{3,2,1,0:T(8,128)}, u32[]{:S(2)}, u32[]{:S(2)}) collective-permute-start(f32[5,16,16,256]{3,2,1,0:T(8,128)} %get-tuple-element.104), channel_id=1, source_target_pairs={{0,6},{1,7},{2,4},{3,5},{4,2},{5,3},{6,0},{7,1},{8,14},{9,15},{10,... | collective-permute-start | bytes 3932168 | tf_op jit(solution)/shard_map/ppermute | solution.py:349
  958.1 57.5 %copy-start.4 = (f32[5,16,16,256]{3,2,1,0:T(8,128)}, f32[5,16,16,256]{3,2,1,0:T(8,128)S(1)}, u32[]{:S(2)}) copy-start(f32[5,16,16,256]{3,2,1,0:T(8,128)S(1)} %collective-permute-done.10.refs_4_) | copy-start | bytes 3932164
  958.1 112.5 %collective-permute-start.21 = (f32[5,16,16,256]{3,2,1,0:T(8,128)}, f32[5,16,16,256]{3,2,1,0:T(8,128)}, u32[]{:S(2)}, u32[]{:S(2)}) collective-permute-start(f32[5,16,16,256]{3,2,1,0:T(8,128)} %get-tuple-element.100), channel_id=1, source_target_pairs={{0,7},{1,6},{2,5},{3,4},{4,3},{5,2},{6,1},{7,0},{8,15},{9,14},{10,... | collective-permute-start | bytes 3932168 | tf_op jit(solution)/shard_map/ppermute | solution.py:349
  958.1 136.9 %collective-permute-start.17 = (f32[5,16,16,256]{3,2,1,0:T(8,128)}, f32[5,16,16,256]{3,2,1,0:T(8,128)}, u32[]{:S(2)}, u32[]{:S(2)}) collective-permute-start(f32[5,16,16,256]{3,2,1,0:T(8,128)} %get-tuple-element.90), channel_id=1, source_target_pairs={{0,4},{1,5},{2,6},{3,7},{4,0},{5,1},{6,2},{7,3},{8,12},{9,13},{10,... | collective-permute-start | bytes 3932168 | tf_op jit(solution)/shard_map/ppermute | solution.py:349
  958.1 140.1 %collective-permute-start.15 = (f32[5,16,16,256]{3,2,1,0:T(8,128)}, f32[5,16,16,256]{3,2,1,0:T(8,128)}, u32[]{:S(2)}, u32[]{:S(2)}) collective-permute-start(f32[5,16,16,256]{3,2,1,0:T(8,128)} %get-tuple-element.87), channel_id=1, source_target_pairs={{0,3},{1,2},{2,1},{3,0},{4,7},{5,6},{6,5},{7,4},{8,11},{9,10},{10,... | collective-permute-start | bytes 3932168 | tf_op jit(solution)/shard_map/ppermute | solution.py:349
  1010.7 157.1 %copy-start.1 = (f32[5,16,16,256]{3,2,1,0:T(8,128)}, f32[5,16,16,256]{3,2,1,0:T(8,128)S(1)}, u32[]{:S(2)}) copy-start(f32[5,16,16,256]{3,2,1,0:T(8,128)S(1)} %collective-permute-done.25.refs_0_) | copy-start | bytes 3932164
  1010.7 89.3 %collective-permute-start.14 = (f32[5,16,16,256]{3,2,1,0:T(8,128)S(1)}, f32[5,16,16,256]{3,2,1,0:T(8,128)}, u32[]{:S(2)}, u32[]{:S(2)}) collective-permute-start(f32[5,16,16,256]{3,2,1,0:T(8,128)S(1)} %copy-done.10), channel_id=1, source_target_pairs={{0,2},{1,3},{2,0},{3,1},{4,6},{5,7},{6,4},{7,5},{8,10},{9,11},{10,... | collective-permute-start | bytes 3932168 | tf_op jit(solution)/shard_map/ppermute | solution.py:349
  1040.8 127.0 %collective-permute-start.11 = (f32[5,16,16,256]{3,2,1,0:T(8,128)}, f32[5,16,16,256]{3,2,1,0:T(8,128)}, u32[]{:S(2)}, u32[]{:S(2)}) collective-permute-start(f32[5,16,16,256]{3,2,1,0:T(8,128)} %get-tuple-element.80), channel_id=1, source_target_pairs={{0,1},{1,0},{2,3},{3,2},{4,5},{5,4},{6,7},{7,6},{8,9},{9,8},{10,11... | collective-permute-start | bytes 3932168 | tf_op jit(solution)/shard_map/ppermute | solution.py:349
  1070.6 115.2 %collective-permute-start.26 = (f32[5,16,16,256]{3,2,1,0:T(8,128)}, f32[5,16,16,256]{3,2,1,0:T(8,128)}, u32[]{:S(2)}, u32[]{:S(2)}) collective-permute-start(f32[5,16,16,256]{3,2,1,0:T(8,128)} %get-tuple-element.109), channel_id=1, source_target_pairs={{0,3},{1,2},{2,1},{3,0},{4,7},{5,6},{6,5},{7,4},{8,11},{9,10},{10,... | collective-permute-start | bytes 3932168 | tf_op jit(solution)/shard_map/ppermute | solution.py:349
  1095.0 90.8 %collective-permute-start.24 = (f32[5,16,16,256]{3,2,1,0:T(8,128)}, f32[5,16,16,256]{3,2,1,0:T(8,128)}, u32[]{:S(2)}, u32[]{:S(2)}) collective-permute-start(f32[5,16,16,256]{3,2,1,0:T(8,128)} %get-tuple-element.105), channel_id=1, source_target_pairs={{0,2},{1,3},{2,0},{3,1},{4,6},{5,7},{6,4},{7,5},{8,10},{9,11},{10,... | collective-permute-start | bytes 3932168 | tf_op jit(solution)/shard_map/ppermute | solution.py:349
  1098.2 87.7 %collective-permute-start.22 = (f32[5,16,16,256]{3,2,1,0:T(8,128)}, f32[5,16,16,256]{3,2,1,0:T(8,128)}, u32[]{:S(2)}, u32[]{:S(2)}) collective-permute-start(f32[5,16,16,256]{3,2,1,0:T(8,128)} %get-tuple-element.101), channel_id=1, source_target_pairs={{0,1},{1,0},{2,3},{3,2},{4,5},{5,4},{6,7},{7,6},{8,9},{9,8},{10,11... | collective-permute-start | bytes 3932168 | tf_op jit(solution)/shard_map/ppermute | solution.py:349
  1100.0 100.8 %collective-permute-start.27 = (f32[5,16,16,256]{3,2,1,0:T(8,128)}, f32[5,16,16,256]{3,2,1,0:T(8,128)}, u32[]{:S(2)}, u32[]{:S(2)}) collective-permute-start(f32[5,16,16,256]{3,2,1,0:T(8,128)} %get-tuple-element.117), channel_id=1, source_target_pairs={{0,4},{1,5},{2,6},{3,7},{4,0},{5,1},{6,2},{7,3},{8,12},{9,13},{10,... | collective-permute-start | bytes 3932168 | tf_op jit(solution)/shard_map/ppermute | solution.py:349

commit v3 on v2

--- a/solution.py
+++ b/solution.py
@@ -9,7 +9,8 @@
 
 gamma_less = 0.4
 time_step = 0.1
-vmem_bytes = 56 * 1024 * 1024
+vmem_bytes = 63 * 1024 * 1024
+WIDTH = 4
 
 
 def divisor_up_to(number, limit):
@@ -53,9 +54,28 @@
     return jnp.dot(a, b, preferred_element_type=jnp.float32)
 
 
-def call(body, name, order, operands, grid, in_specs, out_specs, out_shape, scratch=(), aliases=None, flops=0):
+def call(body, name, order, operands, grid, in_specs, out_specs, out_shape, scratch=(), aliases=None, flops=0, mark=False, wait=()):
     scalars = tuple(order)
     moved = sum(4 * o.size for o in operands) + sum(4 * o.size for o in jax.tree.leaves(out_shape))
+    if wait:
+        begin = len(scalars) + len(operands)
+        plain = body
+
+        def body(*refs):
+            plain(*refs[:begin], *refs[begin + len(wait) :])
+
+        operands = [*operands, *wait]
+        in_specs = [*in_specs, *[pl.BlockSpec(memory_space=pl.ANY)] * len(wait)]
+    inner = body
+    if mark:
+        place = len(scalars) + len(operands) + len(out_shape)
+
+        def body(*refs):
+            inner(*refs[:place], *refs[place + 1 :])
+            refs[place][...] = jnp.zeros_like(refs[place])
+
+        out_specs = [*out_specs, pl.BlockSpec((8, 128), lambda *_: (0, 0))]
+        out_shape = [*out_shape, jax.ShapeDtypeStruct((8, 128), jnp.float32)]
     return pl.pallas_call(
         body,
         name=name,
@@ -80,7 +100,7 @@
     piece[4] = energy[0]
 
 
-def pack_span(order, chunk, chunks, density, momentum, energy):
+def pack_span(order, chunk, chunks, density, momentum, energy, wait=()):
     _, share, zl, nx = density.shape
     rows = share // chunks
     r = divisor_up_to(rows, 8)
@@ -95,6 +115,7 @@
         [flat, pl.BlockSpec((3, 1, r, zl, nx), lambda i, s: (0, s[0], first + i, 0, 0)), flat],
         pl.BlockSpec((5, r, zl, nx), lambda i, s: (0, i, 0, 0)),
         jax.ShapeDtypeStruct((5, rows, zl, nx), jnp.float32),
+        wait=wait,
     )
 
 
@@ -151,7 +172,7 @@
                 pieces[z // zz, f, z % zz, :, lanes] = narrow[half, f, lines, :]
 
 
-def pack_wall(m, density, momentum, energy):
+def pack_wall(m, density, momentum, energy, wait=()):
     jl, zl, nx = density.shape
     zz = zl // m
     lane = divisor_up_to(nx, 128)
@@ -166,14 +187,16 @@
         [flat, pl.BlockSpec((3, rows * zl, nx), lambda i: (0, i, 0)), flat],
         pl.BlockSpec((m, 5, zz, rows, nx), lambda i: (0, 0, 0, i, 0)),
         jax.ShapeDtypeStruct((m, 5, zz, jl, nx), jnp.float32),
+        wait=wait,
         scratch=[pltpu.VMEM((nx // lane, 5, rows * zl, lane), jnp.float32)],
     )
 
 
-def wall_kernel(high, low, damping, pieces, outs, kept, flux_high, flux_low):
+def wall_kernel(both, damping, pieces, *refs):
+    outs, kept, flux_high, flux_low = refs[-4:]
     m, _, _, jl, nx = pieces.shape
     ny = m * jl
-    step = divisor_up_to(jl, 32)
+    step = divisor_up_to(jl, 64)
     for f in range(5):
         kept[f, 0:8] = jnp.zeros((8, nx), jnp.float32)
         kept[f, 8 + ny : 16 + ny] = jnp.zeros((8, nx), jnp.float32)
@@ -188,20 +211,19 @@
                 kept[f, pl.ds(there + 8, step), :] = fields[f]
                 flux_high[f, pl.ds(there, step), :], flux_low[f, pl.ds(there, step), :] = halves(flux)
 
-    for k in range(m):
-        first = k * jl
-        rows = pl.ds(first, jl)
-
-        @pl.loop(0, 5)
-        def _(f):
-            total = dot(high[rows, :], flux_high[f]) + dot(low[rows, :], flux_high[f])
-            outs[k, f, 0] = total + dot(high[rows, :], flux_low[f])
-            part = divisor_up_to(jl, 64)
+    @pl.loop(0, 5)
+    def _(f):
+        large = dot(both[...], flux_high[f])
+        total = large[:ny] + large[ny:] + dot(both[:ny], flux_low[f])
+        for k in range(m):
+            outs[k, f, 0] = total[k * jl : (k + 1) * jl]
+        part = divisor_up_to(jl, 128)
+        for k in range(m):
 
             @pl.loop(0, jl // part)
             def _(i):
                 at = pl.multiple_of(i * part, part)
-                c = kept[f, pl.ds(first + at, part + 16), :]
+                c = kept[f, pl.ds(k * jl + at, part + 16), :]
 
                 def shifted(offset):
                     return c[8 + offset : 8 + offset + part]
@@ -209,31 +231,33 @@
                 fourth = (
                     shifted(-2) - 4.0 * shifted(-1) + 6.0 * shifted(0) - 4.0 * shifted(1) + shifted(2)
                 )
-                weight = damping[pl.ds(first + at, part), :]
+                weight = damping[pl.ds(k * jl + at, part), :]
                 outs[k, f, 0, pl.ds(at, part), :] += weight * fourth
 
 
-def wall_terms(operator, damping, pieces):
+def wall_terms(both, damping, pieces, part, parts, made=(), wait=()):
     m, _, zz, jl, nx = pieces.shape
     ny = m * jl
-    high, low = split_outside(operator)
-    spec = pl.BlockSpec((m, 5, 1, jl, nx), lambda i: (0, 0, i, 0, 0))
-    whole = pl.BlockSpec((ny, ny), lambda i: (0, 0))
+    steps = zz // parts
+    spec = pl.BlockSpec((m, 5, 1, jl, nx), lambda i: (0, 0, part * steps + i, 0, 0))
     return call(
         wall_kernel,
-        "wall_terms",
+        f"wall_terms_{part}",
         (),
-        (high, low, damping.reshape(ny, 1), pieces),
-        (zz,),
-        [whole, whole, pl.BlockSpec((ny, 1), lambda i: (0, 0)), spec],
-        spec,
-        jax.ShapeDtypeStruct(pieces.shape, jnp.float32),
+        (both, damping, pieces, *made),
+        (steps,),
+        [pl.BlockSpec((2 * ny, ny), lambda i: (0, 0)), pl.BlockSpec((ny, 1), lambda i: (0, 0)), spec]
+        + [pl.BlockSpec(memory_space=pl.ANY)] * len(made),
+        [spec],
+        [jax.ShapeDtypeStruct(pieces.shape, jnp.float32)],
         scratch=[
             pltpu.VMEM((5, ny + 16, nx), jnp.float32),
             pltpu.VMEM((5, ny, nx), jnp.bfloat16),
             pltpu.VMEM((5, ny, nx), jnp.bfloat16),
         ],
-        flops=6 * 5 * zz * ny * ny * nx,
+        aliases={3: 0} if made else None,
+        wait=wait,
+        flops=6 * 5 * steps * ny * ny * nx,
     )
 
 
@@ -247,7 +271,7 @@
             lanes = slice(half * lane, (half + 1) * lane)
             for f in range(5):
                 wall[half, f, lines, :] = pieces[z // zz, f, z % zz, :, lanes]
-    part = 16
+    part = divisor_up_to(rows * zl, 64)
 
     @pl.loop(0, rows * zl // part)
     def _(i):
@@ -271,7 +295,7 @@
                 outs[1][f - 1, here, :] = value
 
 
-def base_fields(density, momentum, energy, pieces):
+def base_fields(density, momentum, energy, pieces, wait=()):
     m = pieces.shape[0]
     jl, zl, nx = density.shape
     zz = zl // m
@@ -290,6 +314,8 @@
         [flat, three, flat],
         [shape, jax.ShapeDtypeStruct((3, jl * zl, nx), jnp.float32), shape],
         scratch=[pltpu.VMEM((nx // lane, 5, rows * zl, lane), jnp.float32)],
+        mark=True,
+        wait=wait,
     )
     return outs
 
@@ -306,7 +332,7 @@
             outs[2][0] = energy[0] - time_step * piece[4]
 
 
-def add_span(order, chunk, chunks, fields, pieces):
+def add_span(order, chunk, chunks, fields, pieces, wait=()):
     share, zl, nx = fields[0].shape[1:]
     rows = share // chunks
     r = divisor_up_to(rows, 8)
@@ -331,40 +357,52 @@
         [flat, three, flat],
         [jax.ShapeDtypeStruct(f.shape, f.dtype) for f in fields],
         aliases={1: 0, 2: 1, 3: 2},
-    )
-
-
-def after(value, earlier):
-    if len(earlier) == 0:
+        mark=True,
+        wait=wait,
+    )
+
+
+def after(value, wait):
+    if not wait:
         return value
-    return lax.optimization_barrier((value, *earlier))[0]
+    anywhere = pl.BlockSpec(memory_space=pl.ANY)
+    return pl.pallas_call(
+        lambda *refs: None,
+        name="after",
+        in_specs=[anywhere] * (1 + len(wait)),
+        out_specs=anywhere,
+        out_shape=jax.ShapeDtypeStruct(value.shape, value.dtype),
+        input_output_aliases={0: 0},
+        compiler_params=pltpu.CompilerParams(vmem_limit_bytes=vmem_bytes),
+        cost_estimate=pl.CostEstimate(flops=0, bytes_accessed=0, transcendentals=0),
+    )(value, *wait)
 
 
 class Sender:
     def __init__(self, axis, size, width):
         self.axis, self.size, self.width, self.far = axis, size, width, []
 
-    def permute(self, piece, step, sign, earlier):
+    def permute(self, piece, step, sign):
         pairs = [(i, hop(i, step, self.size, sign)) for i in range(self.size)]
-        return lax.ppermute(after(piece, earlier), self.axis, pairs)
-
-    def exchange(self, pieces, sign, earlier=()):
-        pieces = list(pieces)
-        first = self.size // 2
-        sent = []
-        for k in range(self.size - 1, first - 1, -1):
+        return lax.ppermute(piece, self.axis, pairs)
+
+    def send_far(self, make, steps, sign, wait=()):
+        out = {}
+        for k in steps:
             held = [self.far[-self.width]] if len(self.far) >= self.width else []
-            pieces[k] = self.permute(pieces[k], k, sign, [*held, *earlier])
-            self.far.append(pieces[k])
-            sent.append(pieces[k])
-        for j, k in enumerate(range(1, first)):
-            pieces[k] = self.permute(pieces[k], k, sign, [sent[j]])
-        return pieces
+            out[k] = self.permute(make(k, [*held, *wait]), k, sign)
+            self.far.append(out[k])
+        return out
+
+    def send_near(self, make, steps, sign, begin):
+        return {
+            k: self.permute(make(k, self.far[: begin + j][-1:]), k, sign) for j, k in enumerate(steps)
+        }
 
 
 def local(density, momentum, energy, wall_operator, span_operator, damping, *, chunks):
     jl, zl, nx = density.shape
-    nz = span_operator.shape[0]
+    ny, nz = wall_operator.shape[0], span_operator.shape[0]
     m, n = lax.axis_size("gy"), lax.axis_size("gz")
     gy, gz = lax.axis_index("gy"), lax.axis_index("gz")
     share = jl // n
@@ -379,12 +417,24 @@
         energy.reshape(n, share, zl, nx),
     )
     far, near = list(range(n // 2, n))[::-1], list(range(1, n // 2))
-    sender = Sender("gz", n, 4)
-
-    packs = [[pack_span(span_to[k], c, chunks, *by_share) for k in range(n)] for c in range(chunks)]
-    packed = pack_wall(m, after(density, packs[0]), momentum, energy)
+    count = len(far)
+    sender = Sender("gz", n, WIDTH)
+
+    def pack(c):
+        return lambda k, wait: pack_span(span_to[k], c, chunks, *by_share, wait=wait)
+
+    def ordered(pieces):
+        return [pieces[k] for k in range(n)]
+
+    first_far = sender.send_far(pack(0), far, 1)
+    first_near = sender.send_near(pack(0), near, 1, 0)
+    span_out = [ordered({0: pack(0)(0, ()), **first_far, **first_near})]
+    packed = pack_wall(m, density, momentum, energy, [first_near[k] for k in near[:1]])
     wall_out = lax.all_to_all(packed, "gy", split_axis=0, concat_axis=0, tiled=True)
-    span_out = [sender.exchange(packs[c], 1, [] if c == 0 else [packed]) for c in range(chunks)]
+    for c in range(1, chunks):
+        later_far = sender.send_far(pack(c), far, 1, [packed])
+        later_near = sender.send_near(pack(c), near, 1, c * count)
+        span_out.append(ordered({0: pack(c)(0, ()), **later_far, **later_near}))
 
     identity = jnp.eye(nz, dtype=jnp.float32)
     fourth = 6.0 * identity
@@ -398,29 +448,55 @@
 
     both = jnp.concatenate([in_order_of_arrival(span_operator), in_order_of_arrival(fourth)], axis=1)
     both = jnp.concatenate(split_outside(both), axis=0)
+    wall_both = jnp.concatenate(split_outside(wall_operator), axis=0)
 
     def weights(c):
         return lax.dynamic_slice_in_dim(damping, gy * jl + gz * share + c * rows, rows)
 
-    span_back = [sender.exchange(span_terms(0, weights(0), both, span_out[0]), -1)]
-    begun = span_out[-1][far[0]] if chunks > 1 else wall_out
-    wall_back = wall_terms(wall_operator, damping, after(wall_out, [begun]))
-    wall_back = lax.all_to_all(wall_back, "gy", split_axis=0, concat_axis=0, tiled=True)
-    for c in range(1, chunks):
-        span_back.append(sender.exchange(span_terms(c, weights(c), both, span_out[c]), -1))
-
-    middle = span_back[0][far[n // 4]]
-    fields = base_fields(density, momentum, energy, after(wall_back, [middle]))
+    def back(c):
+        pieces = span_terms(c, weights(c), both, span_out[c])
+        return pieces, lambda k, wait: after(pieces[k], wait)
+
+    zz = zl // m
+    parts = divisor_up_to(zz, 2)
+    wall_back = ()
+    for part in range(parts):
+        begun = sender.far[: count + 1] if part == 0 else sender.far[count + part : count + part + 1]
+        wall_back = wall_terms(wall_both, damping.reshape(ny, 1), wall_out, part, parts, wall_back, begun)
+    wall_back = lax.all_to_all(wall_back[0], "gy", split_axis=0, concat_axis=0, tiled=True)
+
+    pieces, make = back(0)
+    far_back = sender.send_far(make, far, -1)
+    near_back = sender.send_near(make, near, -1, chunks * count)
+    span_back = [ordered({0: pieces[0], **far_back, **near_back})]
+    held = sender.far[-(1 + count // 4) :][:1]
+    *fields, mark = base_fields(density, momentum, energy, wall_back, [*held, *near_back.values()])
     fields = (
         fields[0].reshape(n, share, zl, nx),
         fields[1].reshape(3, n, share, zl, nx),
         fields[2].reshape(n, share, zl, nx),
     )
-    groups = [(c, [0, *near, *far]) for c in range(chunks - 1)]
-    groups += [(chunks - 1, g) for g in ([0, *near], far[: n // 4], far[n // 4 :]) if g]
+
+    def add(c, group, wait=()):
+        order = jnp.concatenate([span_to[k] for k in group])
+        *out, mark = add_span(order, c, chunks, fields, [span_back[c][k] for k in group], wait)
+        return out, mark
+
+    for c in range(1, chunks):
+        pieces, make = back(c)
+        far_back = sender.send_far(make, far[:1], -1)
+        far_back |= sender.send_far(make, far[1:2], -1, [mark])
+        far_back |= sender.send_far(make, far[2:], -1)
+        fields, mark = add(c - 1, [0, *near, *far], [far_back[far[0]]])
+        begin = (chunks + c) * count + 2
+        near_back = sender.send_near(make, near[:-1], -1, begin)
+        near_back |= {k: sender.permute(make(k, [mark, far_back[far[-2]]]), k, -1) for k in near[-1:]}
+        span_back.append(ordered({0: pieces[0], **far_back, **near_back}))
+    last = chunks - 1
+    groups = [(last, [0, *near]), (last, far[: count // 2]), (last, far[count // 2 :])]
     for c, group in groups:
-        order = jnp.concatenate([span_to[k] for k in group])
-        fields = add_span(order, c, chunks, fields, [span_back[c][k] for k in group])
+        if group:
+            fields, _ = add(c, group)
     return (
         fields[0].reshape(jl, zl, nx),
         fields[1].reshape(3, jl, zl, nx),

time: 1210 us -> 1030 us (0.85)
  waiting for transfers between devices: 845 us -> 712 us
  Pallas kernels: 270 us -> 239 us
  starting transfers between devices: 74.2 us -> 48.4 us
    all_to_all x1, waiting for transfers between devices: 106 us -> 0.01 us  [local(): lax.all_to_all(packed, 'gy', split_axis=0, concat_axis=0, tiled=True)]
    pallas_call x25 -> x26, Pallas kernels: 270 us -> 239 us  [call(): pl.pallas_call(body, name=name, grid_spec=pltpu.PrefetchScalarGridSpec(nu...]
    ppermute x28, waiting for transfers between devices: 739 us -> 712 us  [permute(): return lax.ppermute(piece, self.axis, pairs)]
    ppermute x28, starting transfers between devices: 57.3 us -> 32.6 us  [permute(): return lax.ppermute(piece, self.axis, pairs)]
  transfers between devices with their start and end apart: 30 -> 30, of which waited for: 16 -> 19; matrix products, arithmetic and copies ran while one was open for 1% -> 2% of each run, Pallas kernels for 12% -> 17%
where the time goes in v3:
time: 1030 us; the launch traced here: 1020 us
  waiting for transfers between devices  712 us (69%)
  Pallas kernels  239 us (23%)
  starting transfers between devices  48.4 us (5%)
  other arithmetic  12 us (1%)
  local copies, waits for them, and re-layouts  11.2 us (1%)
    ppermute x28, waiting for transfers between devices, permute(): return lax.ppermute(piece, self.axis, pairs)  712 us
    pallas_call x26, Pallas kernels, call(): pl.pallas_call(body, name=name, grid_spec=pltpu.PrefetchScalarGridSpec(nu...  239 us
    ppermute x28, starting transfers between devices, permute(): return lax.ppermute(piece, self.axis, pairs)  32.6 us
  transfers between devices with their start and end apart: 30, of which 19 were waited for; matrix products, arithmetic and copies ran while one was open for 2% of the time, Pallas kernels for 17%

profile of v3, /device:TPU:15, one launch (start us, length us, event | category | flops | bytes accessed | tf_op | source)
XLA Modules:
  0.0 1023.4 jit_solution(18316332542305822990)
XLA Ops:
  0.6 2.2 pack_span_0.8
  3.5 3.0 collective-permute-done.refs_3_.refs_1_
  6.5 20.3 %pack_wall.1.refs_5_ = f32[4,5,4,256,256]{4,3,2,1,0:T(8,128)} custom-call(f32[4096,256]{1,0:T(8,128)} %bitcast.48, f32[3,4096,256]{2,1,0:T(8,128)} %bitcast.30, f32[4096,256]{1,0:T(8,128)} %bitcast.66, f32[5,16,16,256]{3,2,1,0:T(8,128)} %collective-permute-done.refs_3_.refs_1_), custom_call_target="tpu_custom_call" | custom-call | bytes 41943040 | tf_op jit(solution)/shard_map/pack_wall/pallas_call | solution.py:79
  26.8 7.9 all-to-all-start
  43.3 4.1 collective-permute-start.3
  47.4 2.2 pack_span_0.12
  49.7 187.5 %collective-permute-done.1.refs_4_.refs_3_.refs_7_ = f32[5,16,16,256]{3,2,1,0:T(8,128)} collective-permute-done((f32[5,16,16,256]{3,2,1,0:T(8,128)}, f32[5,16,16,256]{3,2,1,0:T(8,128)}, u32[]{:S(2)}, u32[]{:S(2)}) %collective-permute-start.1) | collective-permute-done | bytes 1310752 | tf_op jit(solution)/shard_map/ppermute | solution.py:387
  237.2 2.2 pack_span_1.8
  241.9 3.1 reduce-precision_convert_fusion
  245.0 2.5 pad_maximum_fusion.refs_0_
  247.4 17.6 %collective-permute-done.2.refs_4_.refs_6_ = f32[5,16,16,256]{3,2,1,0:T(8,128)} collective-permute-done((f32[5,16,16,256]{3,2,1,0:T(8,128)}, f32[5,16,16,256]{3,2,1,0:T(8,128)}, u32[]{:S(2)}, u32[]{:S(2)}) %collective-permute-start.2) | collective-permute-done | bytes 1310752 | tf_op jit(solution)/shard_map/ppermute | solution.py:387
  265.0 2.2 pack_span_1.9
  268.6 23.7 %collective-permute-done.3.refs_5_.refs_4_ = f32[5,16,16,256]{3,2,1,0:T(8,128)} collective-permute-done((f32[5,16,16,256]{3,2,1,0:T(8,128)}, f32[5,16,16,256]{3,2,1,0:T(8,128)}, u32[]{:S(2)}, u32[]{:S(2)}) %collective-permute-start.3) | collective-permute-done | bytes 1310752 | tf_op jit(solution)/shard_map/ppermute | solution.py:387
  292.3 28.1 %collective-permute-done.4.refs_6_.refs_4_ = f32[5,16,16,256]{3,2,1,0:T(8,128)} collective-permute-done((f32[5,16,16,256]{3,2,1,0:T(8,128)}, f32[5,16,16,256]{3,2,1,0:T(8,128)}, u32[]{:S(2)}, u32[]{:S(2)}) %collective-permute-start.4) | collective-permute-done | bytes 1310752 | tf_op jit(solution)/shard_map/ppermute | solution.py:387
  320.4 28.9 %collective-permute-done.5.refs_7_.refs_1_.refs_4_ = f32[5,16,16,256]{3,2,1,0:T(8,128)} collective-permute-done((f32[5,16,16,256]{3,2,1,0:T(8,128)}, f32[5,16,16,256]{3,2,1,0:T(8,128)}, u32[]{:S(2)}, u32[]{:S(2)}) %collective-permute-start.5) | collective-permute-done | bytes 1310752 | tf_op jit(solution)/shard_map/ppermute | solution.py:387
  349.3 34.3 %wall_terms_0.1.refs_3_ = f32[4,5,4,256,256]{4,3,2,1,0:T(8,128)} custom-call(bf16[2048,1024]{1,0:T(8,128)(2,1)} %pad_maximum_fusion.refs_0_, f32[1024,1]{1,0:T(8,128)} %copy.41.refs_1_, f32[4,5,4,256,256]{4,3,2,1,0:T(8,128)} %all-to-all-done.refs_2_, f32[5,16,16,256]{3,2,1,0:T(8,128)} %collective-permute-done.1.refs_4_.refs_3_.refs_7_, ...), custom_call_target="tpu_custom_call" | custom-call | flops 16106127360 | bytes 50335744 | tf_op jit(solution)/shard_map/wall_terms_0/pallas_call | solution.py:79
  383.6 34.3 %wall_terms_1.1 = f32[4,5,4,256,256]{4,3,2,1,0:T(8,128)} custom-call(bf16[2048,1024]{1,0:T(8,128)(2,1)} %pad_maximum_fusion.refs_0_, f32[1024,1]{1,0:T(8,128)} %copy.41.refs_1_, f32[4,5,4,256,256]{4,3,2,1,0:T(8,128)} %all-to-all-done.refs_2_, f32[4,5,4,256,256]{4,3,2,1,0:T(8,128)} %wall_terms_0.1.refs_3_, ...), custom_call_target="tpu_custom_call", output_to_operand_aliasing={{}: (3, {})} | custom-call | flops 16106127360 | bytes 71307264 | tf_op jit(solution)/shard_map/wall_terms_1/pallas_call | solution.py:79
  417.9 7.9 all-to-all-start.1
  432.8 2.4 add_add_fusion
  437.4 2.3 pack_span_0.15
  445.2 2.3 pack_span_1.10
  452.5 2.2 pack_span_1.11
  455.3 57.7 %collective-permute-done.7.refs_2_ = f32[5,16,16,256]{3,2,1,0:T(8,128)} collective-permute-done((f32[5,16,16,256]{3,2,1,0:T(8,128)}, f32[5,16,16,256]{3,2,1,0:T(8,128)}, u32[]{:S(2)}, u32[]{:S(2)}) %collective-permute-start.7) | collective-permute-done | bytes 1310752 | tf_op jit(solution)/shard_map/ppermute | solution.py:387
  513.0 28.1 %collective-permute-done.8.refs_3_ = f32[5,16,16,256]{3,2,1,0:T(8,128)} collective-permute-done((f32[5,16,16,256]{3,2,1,0:T(8,128)}, f32[5,16,16,256]{3,2,1,0:T(8,128)}, u32[]{:S(2)}, u32[]{:S(2)}) %collective-permute-start.8) | collective-permute-done | bytes 1310752 | tf_op jit(solution)/shard_map/ppermute | solution.py:387
  541.1 13.8 %span_terms_0.1 = (f32[5,16,16,256]{3,2,1,0:T(8,128)}, f32[5,16,16,256]{3,2,1,0:T(8,128)}, f32[5,16,16,256]{3,2,1,0:T(8,128)}, f32[5,16,16,256]{3,2,1,0:T(8,128)...) custom-call(f32[16]{0:T(128)} %get-tuple-element.84.weights, ...), custom_call_target="tpu_custom_call" | custom-call | flops 4026531840 | bytes 21233664 | tf_op jit(solution)/shard_map/span_terms_0/pallas_call | solution.py:79
  559.4 2.3 pack_span_1.14
  561.6 4.4 collective-permute-start.19
  566.0 2.2 pack_span_1.15
  568.2 50.2 %collective-permute-done.11.refs_1_.refs_4_ = f32[5,16,16,256]{3,2,1,0:T(8,128)} collective-permute-done((f32[5,16,16,256]{3,2,1,0:T(8,128)}, f32[5,16,16,256]{3,2,1,0:T(8,128)}, u32[]{:S(2)}, u32[]{:S(2)}) %collective-permute-start.11) | collective-permute-done | bytes 1310752 | tf_op jit(solution)/shard_map/ppermute | solution.py:387
  618.4 2.4 collective-permute-start.20
  620.7 26.6 %collective-permute-done.13.refs_1_.refs_8_ = f32[5,16,16,256]{3,2,1,0:T(8,128)} collective-permute-done((f32[5,16,16,256]{3,2,1,0:T(8,128)}, f32[5,16,16,256]{3,2,1,0:T(8,128)}, u32[]{:S(2)}, u32[]{:S(2)}) %collective-permute-start.13) | collective-permute-done | bytes 1310752 | tf_op jit(solution)/shard_map/ppermute | solution.py:387
  647.3 56.1 %collective-permute-done.15.refs_1_.refs_9_ = f32[5,16,16,256]{3,2,1,0:T(8,128)} collective-permute-done((f32[5,16,16,256]{3,2,1,0:T(8,128)}, f32[5,16,16,256]{3,2,1,0:T(8,128)}, u32[]{:S(2)}, u32[]{:S(2)}) %collective-permute-start.15) | collective-permute-done | bytes 1310752 | tf_op jit(solution)/shard_map/ppermute | solution.py:387
  707.8 13.9 %span_terms_1.1 = (f32[5,16,16,256]{3,2,1,0:T(8,128)}, f32[5,16,16,256]{3,2,1,0:T(8,128)}, f32[5,16,16,256]{3,2,1,0:T(8,128)}, f32[5,16,16,256]{3,2,1,0:T(8,128)...) custom-call(f32[16]{0:T(128)} %get-tuple-element.83.weights, ...), custom_call_target="tpu_custom_call" | custom-call | flops 4026531840 | bytes 21233664 | tf_op jit(solution)/shard_map/span_terms_1/pallas_call | solution.py:79
  721.7 9.1 collective-permute-done.10.refs_4_.refs_10_.refs_1_
  730.8 3.4 collective-permute-start.24
  734.6 52.4 %collective-permute-done.14.refs_6_ = f32[5,16,16,256]{3,2,1,0:T(8,128)} collective-permute-done((f32[5,16,16,256]{3,2,1,0:T(8,128)}, f32[5,16,16,256]{3,2,1,0:T(8,128)}, u32[]{:S(2)}, u32[]{:S(2)}) %collective-permute-start.14) | collective-permute-done | bytes 1310752 | tf_op jit(solution)/shard_map/ppermute | solution.py:387
  787.0 28.1 %collective-permute-done.16.refs_7_ = f32[5,16,16,256]{3,2,1,0:T(8,128)} collective-permute-done((f32[5,16,16,256]{3,2,1,0:T(8,128)}, f32[5,16,16,256]{3,2,1,0:T(8,128)}, u32[]{:S(2)}, u32[]{:S(2)}) %collective-permute-start.16) | collective-permute-done | bytes 1310752 | tf_op jit(solution)/shard_map/ppermute | solution.py:387
  815.1 48.6 %base_fields.1 = (f32[4096,256]{1,0:T(8,128)}, f32[3,4096,256]{2,1,0:T(8,128)}, f32[4096,256]{1,0:T(8,128)}, f32[8,128]{1,0:T(8,128)}) custom-call(f32[4096,256]{1,0:T(8,128)} %bitcast.64, f32[3,4096,256]{2,1,0:T(8,128)} %bitcast.46, f32[4096,256]{1,0:T(8,128)} %bitcast.82, f32[4,5,4,256,256]{4,3,2,1,0:T(8,128)} %all-to-all-done.1.refs_3_, ...), custom_call_target="tpu_custom_call" | custom-call | bytes 62914560 | tf_op jit(solution)/shard_map/base_fields/pallas_call | solution.py:79
  864.5 3.1 collective-permute-start.25
  867.6 35.8 %collective-permute-done.17.refs_11_.refs_1_ = f32[5,16,16,256]{3,2,1,0:T(8,128)} collective-permute-done((f32[5,16,16,256]{3,2,1,0:T(8,128)}, f32[5,16,16,256]{3,2,1,0:T(8,128)}, u32[]{:S(2)}, u32[]{:S(2)}) %collective-permute-start.17) | collective-permute-done | bytes 1310752 | tf_op jit(solution)/shard_map/ppermute | solution.py:387
  903.4 29.1 %collective-permute-done.21.refs_12_.refs_4_ = f32[5,16,16,256]{3,2,1,0:T(8,128)} collective-permute-done((f32[5,16,16,256]{3,2,1,0:T(8,128)}, f32[5,16,16,256]{3,2,1,0:T(8,128)}, u32[]{:S(2)}, u32[]{:S(2)}) %collective-permute-start.21) | collective-permute-done | bytes 1310752 | tf_op jit(solution)/shard_map/ppermute | solution.py:387
  932.5 18.0 %add_span_0.1 = (f32[8,32,16,256]{3,2,1,0:T(8,128)}, f32[3,8,32,16,256]{4,3,2,1,0:T(8,128)}, f32[8,32,16,256]{3,2,1,0:T(8,128)}, f32[8,128]{1,0:T(8,128)}) custom-call(s32[8]{0:T(128)} %concatenate.47.refs_0_, f32[8,32,16,256]{3,2,1,0:T(8,128)} %bitcast.85, ...), custom_call_target="tpu_custom_call", output_to_operand_aliasing={{0}: (1, {}), {1}: (2, {}), {2}: (3, {})} | custom-call | bytes 52428800 | tf_op jit(solution)/shard_map/add_span_0/pallas_call | solution.py:79
  950.6 9.8 collective-permute-done.22.refs_1_.refs_5_
  962.8 35.3 %collective-permute-done.26.refs_7_ = f32[5,16,16,256]{3,2,1,0:T(8,128)} collective-permute-done((f32[5,16,16,256]{3,2,1,0:T(8,128)}, f32[5,16,16,256]{3,2,1,0:T(8,128)}, u32[]{:S(2)}, u32[]{:S(2)}) %collective-permute-start.26) | collective-permute-done | bytes 1310752 | tf_op jit(solution)/shard_map/ppermute | solution.py:387
  998.1 9.5 add_span_1.3
  1007.6 5.4 add_span_1.4
  1013.0 4.9 collective-permute-done.27.refs_5_
  1017.9 5.4 add_span_1.5
  (102 shorter events, 45.9 us)
Async XLA Ops:
  2.9 3.7 collective-permute-start
  26.8 322.5 %all-to-all-start = ((f32[4,5,4,256,256]{4,3,2,1,0:T(8,128)}), f32[4,5,4,256,256]{4,3,2,1,0:T(8,128)}, u32[]{:S(2)}, u32[]{:S(2)}) async-start(f32[4,5,4,256,256]{4,3,2,1,0:T(8,128)} %pack_wall.1.refs_5_), calls=%async_computation | async-start | bytes 41943040 | tf_op jit(solution)/shard_map/all_to_all | solution.py:433
  36.9 200.3 %collective-permute-start.1 = (f32[5,16,16,256]{3,2,1,0:T(8,128)}, f32[5,16,16,256]{3,2,1,0:T(8,128)}, u32[]{:S(2)}, u32[]{:S(2)}) collective-permute-start(f32[5,16,16,256]{3,2,1,0:T(8,128)} %pack_span_0.9), channel_id=1, source_target_pairs={{0,7},{1,6},{2,5},{3,4},{4,3},{5,2},{6,1},{7,0},{8,15},{9,14},{10,... | collective-permute-start | bytes 3932168 | tf_op jit(solution)/shard_map/ppermute | solution.py:387
  40.9 224.1 %collective-permute-start.2 = (f32[5,16,16,256]{3,2,1,0:T(8,128)}, f32[5,16,16,256]{3,2,1,0:T(8,128)}, u32[]{:S(2)}, u32[]{:S(2)}) collective-permute-start(f32[5,16,16,256]{3,2,1,0:T(8,128)} %pack_span_0.10), channel_id=1, source_target_pairs={{0,6},{1,7},{2,4},{3,5},{4,2},{5,3},{6,0},{7,1},{8,14},{9,15},{10,... | collective-permute-start | bytes 3932168 | tf_op jit(solution)/shard_map/ppermute | solution.py:387
  43.3 249.0 %collective-permute-start.3 = (f32[5,16,16,256]{3,2,1,0:T(8,128)}, f32[5,16,16,256]{3,2,1,0:T(8,128)}, u32[]{:S(2)}, u32[]{:S(2)}) collective-permute-start(f32[5,16,16,256]{3,2,1,0:T(8,128)} %pack_span_0.11), channel_id=1, source_target_pairs={{0,5},{1,4},{2,7},{3,6},{4,1},{5,0},{6,3},{7,2},{8,13},{9,12},{10,... | collective-permute-start | bytes 3932168 | tf_op jit(solution)/shard_map/ppermute | solution.py:387
  49.7 191.2 %copy-start.3 = (f32[1024]{0:T(1024)S(1)}, f32[1024]{0:T(1024)}, u32[]{:S(2)}) copy-start(f32[1024]{0:T(1024)} %param.15) | copy-start | bytes 12292
  49.7 270.7 %collective-permute-start.4 = (f32[5,16,16,256]{3,2,1,0:T(8,128)}, f32[5,16,16,256]{3,2,1,0:T(8,128)}, u32[]{:S(2)}, u32[]{:S(2)}) collective-permute-start(f32[5,16,16,256]{3,2,1,0:T(8,128)} %pack_span_0.12), channel_id=1, source_target_pairs={{0,4},{1,5},{2,6},{3,7},{4,0},{5,1},{6,2},{7,3},{8,12},{9,13},{10,... | collective-permute-start | bytes 3932168 | tf_op jit(solution)/shard_map/ppermute | solution.py:387
  239.4 109.9 %collective-permute-start.5 = (f32[5,16,16,256]{3,2,1,0:T(8,128)}, f32[5,16,16,256]{3,2,1,0:T(8,128)}, u32[]{:S(2)}, u32[]{:S(2)}) collective-permute-start(f32[5,16,16,256]{3,2,1,0:T(8,128)} %pack_span_1.8), channel_id=1, source_target_pairs={{0,7},{1,6},{2,5},{3,4},{4,3},{5,2},{6,1},{7,0},{8,15},{9,14},{10,... | collective-permute-start | bytes 3932168 | tf_op jit(solution)/shard_map/ppermute | solution.py:387
  267.2 116.4 %collective-permute-start.6 = (f32[5,16,16,256]{3,2,1,0:T(8,128)}, f32[5,16,16,256]{3,2,1,0:T(8,128)}, u32[]{:S(2)}, u32[]{:S(2)}) collective-permute-start(f32[5,16,16,256]{3,2,1,0:T(8,128)} %pack_span_1.9), channel_id=1, source_target_pairs={{0,6},{1,7},{2,4},{3,5},{4,2},{5,3},{6,0},{7,1},{8,14},{9,15},{10,... | collective-permute-start | bytes 3932168 | tf_op jit(solution)/shard_map/ppermute | solution.py:387
  417.9 397.2 %all-to-all-start.1 = ((f32[4,5,4,256,256]{4,3,2,1,0:T(8,128)}), f32[4,5,4,256,256]{4,3,2,1,0:T(8,128)}, u32[]{:S(2)}, u32[]{:S(2)}) async-start(f32[4,5,4,256,256]{4,3,2,1,0:T(8,128)} %wall_terms_1.1), calls=%async_computation.1 | async-start | bytes 41943040 | tf_op jit(solution)/shard_map/all_to_all | solution.py:466
  426.3 3.2 copy-start.2
  437.4 4.2 copy-start
  437.4 75.6 %collective-permute-start.7 = (f32[5,16,16,256]{3,2,1,0:T(8,128)}, f32[5,16,16,256]{3,2,1,0:T(8,128)}, u32[]{:S(2)}, u32[]{:S(2)}) collective-permute-start(f32[5,16,16,256]{3,2,1,0:T(8,128)} %pack_span_0.14), channel_id=1, source_target_pairs={{0,2},{1,3},{2,0},{3,1},{4,6},{5,7},{6,4},{7,5},{8,10},{9,11},{10,... | collective-permute-start | bytes 3932168 | tf_op jit(solution)/shard_map/ppermute | solution.py:387
  439.7 2.6 copy-start.1
  439.7 101.4 %collective-permute-start.8 = (f32[5,16,16,256]{3,2,1,0:T(8,128)}, f32[5,16,16,256]{3,2,1,0:T(8,128)}, u32[]{:S(2)}, u32[]{:S(2)}) collective-permute-start(f32[5,16,16,256]{3,2,1,0:T(8,128)} %pack_span_0.15), channel_id=1, source_target_pairs={{0,3},{1,2},{2,1},{3,0},{4,7},{5,6},{6,5},{7,4},{8,11},{9,10},{10,... | collective-permute-start | bytes 3932168 | tf_op jit(solution)/shard_map/ppermute | solution.py:387
  447.4 114.2 %collective-permute-start.9 = (f32[5,16,16,256]{3,2,1,0:T(8,128)}, f32[5,16,16,256]{3,2,1,0:T(8,128)}, u32[]{:S(2)}, u32[]{:S(2)}) collective-permute-start(f32[5,16,16,256]{3,2,1,0:T(8,128)} %pack_span_1.10), channel_id=1, source_target_pairs={{0,5},{1,4},{2,7},{3,6},{4,1},{5,0},{6,3},{7,2},{8,13},{9,12},{10,... | collective-permute-start | bytes 3932168 | tf_op jit(solution)/shard_map/ppermute | solution.py:387
  454.8 163.6 %collective-permute-start.11 = (f32[5,16,16,256]{3,2,1,0:T(8,128)}, f32[5,16,16,256]{3,2,1,0:T(8,128)}, u32[]{:S(2)}, u32[]{:S(2)}) collective-permute-start(f32[5,16,16,256]{3,2,1,0:T(8,128)} %pack_span_1.11), channel_id=1, source_target_pairs={{0,4},{1,5},{2,6},{3,7},{4,0},{5,1},{6,2},{7,3},{8,12},{9,13},{10,... | collective-permute-start | bytes 3932168 | tf_op jit(solution)/shard_map/ppermute | solution.py:387
  554.8 92.5 %collective-permute-start.13 = (f32[5,16,16,256]{3,2,1,0:T(8,128)}, f32[5,16,16,256]{3,2,1,0:T(8,128)}, u32[]{:S(2)}, u32[]{:S(2)}) collective-permute-start(f32[5,16,16,256]{3,2,1,0:T(8,128)} %after.16), channel_id=1, source_target_pairs={{0,7},{1,6},{2,5},{3,4},{4,3},{5,2},{6,1},{7,0},{8,15},{9,14},{10,... | collective-permute-start | bytes 3932168 | tf_op jit(solution)/shard_map/ppermute | solution.py:387
  555.8 147.7 %collective-permute-start.15 = (f32[5,16,16,256]{3,2,1,0:T(8,128)}, f32[5,16,16,256]{3,2,1,0:T(8,128)}, u32[]{:S(2)}, u32[]{:S(2)}) collective-permute-start(f32[5,16,16,256]{3,2,1,0:T(8,128)} %after.18), channel_id=1, source_target_pairs={{0,6},{1,7},{2,4},{3,5},{4,2},{5,3},{6,0},{7,1},{8,14},{9,15},{10,... | collective-permute-start | bytes 3932168 | tf_op jit(solution)/shard_map/ppermute | solution.py:387
  559.4 144.5 %collective-permute-start.18 = (f32[5,16,16,256]{3,2,1,0:T(8,128)}, f32[5,16,16,256]{3,2,1,0:T(8,128)}, u32[]{:S(2)}, u32[]{:S(2)}) collective-permute-start(f32[5,16,16,256]{3,2,1,0:T(8,128)} %pack_span_1.13), channel_id=1, source_target_pairs={{0,1},{1,0},{2,3},{3,2},{4,5},{5,4},{6,7},{7,6},{8,9},{9,8},{10,11... | collective-permute-start | bytes 3932168 | tf_op jit(solution)/shard_map/ppermute | solution.py:387
  561.6 142.3 %collective-permute-start.19 = (f32[5,16,16,256]{3,2,1,0:T(8,128)}, f32[5,16,16,256]{3,2,1,0:T(8,128)}, u32[]{:S(2)}, u32[]{:S(2)}) collective-permute-start(f32[5,16,16,256]{3,2,1,0:T(8,128)} %pack_span_1.14), channel_id=1, source_target_pairs={{0,2},{1,3},{2,0},{3,1},{4,6},{5,7},{6,4},{7,5},{8,10},{9,11},{10,... | collective-permute-start | bytes 3932168 | tf_op jit(solution)/shard_map/ppermute | solution.py:387
  618.4 89.4 %collective-permute-start.20 = (f32[5,16,16,256]{3,2,1,0:T(8,128)}, f32[5,16,16,256]{3,2,1,0:T(8,128)}, u32[]{:S(2)}, u32[]{:S(2)}) collective-permute-start(f32[5,16,16,256]{3,2,1,0:T(8,128)} %pack_span_1.15), channel_id=1, source_target_pairs={{0,3},{1,2},{2,1},{3,0},{4,7},{5,6},{6,5},{7,4},{8,11},{9,10},{10,... | collective-permute-start | bytes 3932168 | tf_op jit(solution)/shard_map/ppermute | solution.py:387
  647.3 83.5 %collective-permute-start.10 = (f32[5,16,16,256]{3,2,1,0:T(8,128)}, f32[5,16,16,256]{3,2,1,0:T(8,128)}, u32[]{:S(2)}, u32[]{:S(2)}) collective-permute-start(f32[5,16,16,256]{3,2,1,0:T(8,128)} %after.14), channel_id=1, source_target_pairs={{0,5},{1,4},{2,7},{3,6},{4,1},{5,0},{6,3},{7,2},{8,13},{9,12},{10,... | collective-permute-start | bytes 3932168 | tf_op jit(solution)/shard_map/ppermute | solution.py:387
  703.5 30.8 %collective-permute-start.12 = (f32[5,16,16,256]{3,2,1,0:T(8,128)}, f32[5,16,16,256]{3,2,1,0:T(8,128)}, u32[]{:S(2)}, u32[]{:S(2)}) collective-permute-start(f32[5,16,16,256]{3,2,1,0:T(8,128)} %after.15), channel_id=1, source_target_pairs={{0,1},{1,0},{2,3},{3,2},{4,5},{5,4},{6,7},{7,6},{8,9},{9,8},{10,11... | collective-permute-start | bytes 3932168 | tf_op jit(solution)/shard_map/ppermute | solution.py:387
  703.9 83.1 %collective-permute-start.14 = (f32[5,16,16,256]{3,2,1,0:T(8,128)}, f32[5,16,16,256]{3,2,1,0:T(8,128)}, u32[]{:S(2)}, u32[]{:S(2)}) collective-permute-start(f32[5,16,16,256]{3,2,1,0:T(8,128)} %after.17), channel_id=1, source_target_pairs={{0,2},{1,3},{2,0},{3,1},{4,6},{5,7},{6,4},{7,5},{8,10},{9,11},{10,... | collective-permute-start | bytes 3932168 | tf_op jit(solution)/shard_map/ppermute | solution.py:387
  703.9 111.2 %collective-permute-start.16 = (f32[5,16,16,256]{3,2,1,0:T(8,128)}, f32[5,16,16,256]{3,2,1,0:T(8,128)}, u32[]{:S(2)}, u32[]{:S(2)}) collective-permute-start(f32[5,16,16,256]{3,2,1,0:T(8,128)} %after.19), channel_id=1, source_target_pairs={{0,3},{1,2},{2,1},{3,0},{4,7},{5,6},{6,5},{7,4},{8,11},{9,10},{10,... | collective-permute-start | bytes 3932168 | tf_op jit(solution)/shard_map/ppermute | solution.py:387
  730.8 133.7 %collective-permute-start.24 = (f32[5,16,16,256]{3,2,1,0:T(8,128)}, f32[5,16,16,256]{3,2,1,0:T(8,128)}, u32[]{:S(2)}, u32[]{:S(2)}) collective-permute-start(f32[5,16,16,256]{3,2,1,0:T(8,128)} %after.24), channel_id=1, source_target_pairs={{0,5},{1,4},{2,7},{3,6},{4,1},{5,0},{6,3},{7,2},{8,13},{9,12},{10,... | collective-permute-start | bytes 3932168 | tf_op jit(solution)/shard_map/ppermute | solution.py:387
  734.2 169.2 %collective-permute-start.17 = (f32[5,16,16,256]{3,2,1,0:T(8,128)}, f32[5,16,16,256]{3,2,1,0:T(8,128)}, u32[]{:S(2)}, u32[]{:S(2)}) collective-permute-start(f32[5,16,16,256]{3,2,1,0:T(8,128)} %after.20), channel_id=1, source_target_pairs={{0,4},{1,5},{2,6},{3,7},{4,0},{5,1},{6,2},{7,3},{8,12},{9,13},{10,... | collective-permute-start | bytes 3932168 | tf_op jit(solution)/shard_map/ppermute | solution.py:387
  734.2 198.3 %collective-permute-start.21 = (f32[5,16,16,256]{3,2,1,0:T(8,128)}, f32[5,16,16,256]{3,2,1,0:T(8,128)}, u32[]{:S(2)}, u32[]{:S(2)}) collective-permute-start(f32[5,16,16,256]{3,2,1,0:T(8,128)} %after.21), channel_id=1, source_target_pairs={{0,7},{1,6},{2,5},{3,4},{4,3},{5,2},{6,1},{7,0},{8,15},{9,14},{10,... | collective-permute-start | bytes 3932168 | tf_op jit(solution)/shard_map/ppermute | solution.py:387
  863.7 96.7 %collective-permute-start.22 = (f32[5,16,16,256]{3,2,1,0:T(8,128)}, f32[5,16,16,256]{3,2,1,0:T(8,128)}, u32[]{:S(2)}, u32[]{:S(2)}) collective-permute-start(f32[5,16,16,256]{3,2,1,0:T(8,128)} %after.22), channel_id=1, source_target_pairs={{0,6},{1,7},{2,4},{3,5},{4,2},{5,3},{6,0},{7,1},{8,14},{9,15},{10,... | collective-permute-start | bytes 3932168 | tf_op jit(solution)/shard_map/ppermute | solution.py:387
  864.5 98.3 %collective-permute-start.25 = (f32[5,16,16,256]{3,2,1,0:T(8,128)}, f32[5,16,16,256]{3,2,1,0:T(8,128)}, u32[]{:S(2)}, u32[]{:S(2)}) collective-permute-start(f32[5,16,16,256]{3,2,1,0:T(8,128)} %after.25), channel_id=1, source_target_pairs={{0,2},{1,3},{2,0},{3,1},{4,6},{5,7},{6,4},{7,5},{8,10},{9,11},{10,... | collective-permute-start | bytes 3932168 | tf_op jit(solution)/shard_map/ppermute | solution.py:387
  950.5 47.6 %collective-permute-start.26 = (f32[5,16,16,256]{3,2,1,0:T(8,128)}, f32[5,16,16,256]{3,2,1,0:T(8,128)}, u32[]{:S(2)}, u32[]{:S(2)}) collective-permute-start(f32[5,16,16,256]{3,2,1,0:T(8,128)} %after.26), channel_id=1, source_target_pairs={{0,3},{1,2},{2,1},{3,0},{4,7},{5,6},{6,5},{7,4},{8,11},{9,10},{10,... | collective-permute-start | bytes 3932168 | tf_op jit(solution)/shard_map/ppermute | solution.py:387
  960.4 37.7 %collective-permute-start.23 = (f32[5,16,16,256]{3,2,1,0:T(8,128)}, f32[5,16,16,256]{3,2,1,0:T(8,128)}, u32[]{:S(2)}, u32[]{:S(2)}) collective-permute-start(f32[5,16,16,256]{3,2,1,0:T(8,128)} %after.23), channel_id=1, source_target_pairs={{0,1},{1,0},{2,3},{3,2},{4,5},{5,4},{6,7},{7,6},{8,9},{9,8},{10,11... | collective-permute-start | bytes 3932168 | tf_op jit(solution)/shard_map/ppermute | solution.py:387
  961.0 56.9 %collective-permute-start.27 = (f32[5,16,16,256]{3,2,1,0:T(8,128)}, f32[5,16,16,256]{3,2,1,0:T(8,128)}, u32[]{:S(2)}, u32[]{:S(2)}) collective-permute-start(f32[5,16,16,256]{3,2,1,0:T(8,128)} %after.27), channel_id=1, source_target_pairs={{0,4},{1,5},{2,6},{3,7},{4,0},{5,1},{6,2},{7,3},{8,12},{9,13},{10,... | collective-permute-start | bytes 3932168 | tf_op jit(solution)/shard_map/ppermute | solution.py:387

commit v4 on v3

--- a/solution.py
+++ b/solution.py
@@ -10,7 +10,8 @@
 gamma_less = 0.4
 time_step = 0.1
 vmem_bytes = 63 * 1024 * 1024
-WIDTH = 4
+WIDTH = 99
+NEAR = 1
 
 
 def divisor_up_to(number, limit):
@@ -155,8 +156,9 @@
     )
 
 
-def pack_wall_kernel(zl, density, momentum, energy, pieces, narrow):
-    m, _, zz, rows, nx = pieces.shape
+def pack_wall_kernel(zl, order, density, momentum, energy, *refs):
+    pieces, narrow = refs[:-1], refs[-1]
+    _, zz, rows, nx = pieces[0].shape
     lane = narrow.shape[-1]
     for half in range(nx // lane):
         lanes = slice(half * lane, (half + 1) * lane)
@@ -164,37 +166,40 @@
         for column in range(3):
             narrow[half, 1 + column] = momentum[column, :, lanes]
         narrow[half, 4] = energy[:, lanes]
-    for z in range(zl):
-        lines = pl.ds(z, rows, stride=zl)
-        for half in range(nx // lane):
-            lanes = slice(half * lane, (half + 1) * lane)
-            for f in range(5):
-                pieces[z // zz, f, z % zz, :, lanes] = narrow[half, f, lines, :]
-
-
-def pack_wall(m, density, momentum, energy, wait=()):
+    for k, piece in enumerate(pieces):
+        for z in range(zz):
+            lines = pl.ds(order[k] * zz + z, rows, stride=zl)
+            for half in range(nx // lane):
+                lanes = slice(half * lane, (half + 1) * lane)
+                for f in range(5):
+                    piece[f, z, :, lanes] = narrow[half, f, lines, :]
+
+
+def pack_wall(blocks, density, momentum, energy, wait=()):
+    m = blocks.shape[0]
     jl, zl, nx = density.shape
     zz = zl // m
     lane = divisor_up_to(nx, 128)
     rows = divisor_up_to(jl, 32)
-    flat = pl.BlockSpec((rows * zl, nx), lambda i: (i, 0))
+    flat = pl.BlockSpec((rows * zl, nx), lambda i, s: (i, 0))
     return call(
         functools.partial(pack_wall_kernel, zl),
         "pack_wall",
-        (),
+        (blocks,),
         (density.reshape(jl * zl, nx), momentum.reshape(3, jl * zl, nx), energy.reshape(jl * zl, nx)),
         (jl // rows,),
-        [flat, pl.BlockSpec((3, rows * zl, nx), lambda i: (0, i, 0)), flat],
-        pl.BlockSpec((m, 5, zz, rows, nx), lambda i: (0, 0, 0, i, 0)),
-        jax.ShapeDtypeStruct((m, 5, zz, jl, nx), jnp.float32),
+        [flat, pl.BlockSpec((3, rows * zl, nx), lambda i, s: (0, i, 0)), flat],
+        [pl.BlockSpec((5, zz, rows, nx), lambda i, s: (0, 0, i, 0))] * m,
+        [jax.ShapeDtypeStruct((5, zz, jl, nx), jnp.float32)] * m,
         wait=wait,
         scratch=[pltpu.VMEM((nx // lane, 5, rows * zl, lane), jnp.float32)],
     )
 
 
-def wall_kernel(both, damping, pieces, *refs):
-    outs, kept, flux_high, flux_low = refs[-4:]
-    m, _, _, jl, nx = pieces.shape
+def wall_kernel(m, order, both, damping, *refs):
+    pieces, outs = refs[:m], refs[-4 - m : -4]
+    kept, flux_high, flux_low, summed = refs[-4:]
+    jl, nx = pieces[0].shape[2:]
     ny = m * jl
     step = divisor_up_to(jl, 64)
     for f in range(5):
@@ -205,8 +210,8 @@
         @pl.loop(0, jl // step)
         def _(i):
             here = pl.ds(pl.multiple_of(i * step, step), step)
-            there = pl.multiple_of(k * jl + i * step, step)
-            fields = [pieces[k, f, 0, here, :] for f in range(5)]
+            there = pl.multiple_of(order[k] * jl + i * step, step)
+            fields = [pieces[k][f, 0, here, :] for f in range(5)]
             for f, flux in enumerate(fluxes(fields, 1)):
                 kept[f, pl.ds(there + 8, step), :] = fields[f]
                 flux_high[f, pl.ds(there, step), :], flux_low[f, pl.ds(there, step), :] = halves(flux)
@@ -214,16 +219,15 @@
     @pl.loop(0, 5)
     def _(f):
         large = dot(both[...], flux_high[f])
-        total = large[:ny] + large[ny:] + dot(both[:ny], flux_low[f])
-        for k in range(m):
-            outs[k, f, 0] = total[k * jl : (k + 1) * jl]
+        summed[...] = large[:ny] + large[ny:] + dot(both[:ny], flux_low[f])
         part = divisor_up_to(jl, 128)
         for k in range(m):
 
             @pl.loop(0, jl // part)
             def _(i):
                 at = pl.multiple_of(i * part, part)
-                c = kept[f, pl.ds(k * jl + at, part + 16), :]
+                there = pl.multiple_of(order[k] * jl + at, part)
+                c = kept[f, pl.ds(there, part + 16), :]
 
                 def shifted(offset):
                     return c[8 + offset : 8 + offset + part]
@@ -231,46 +235,50 @@
                 fourth = (
                     shifted(-2) - 4.0 * shifted(-1) + 6.0 * shifted(0) - 4.0 * shifted(1) + shifted(2)
                 )
-                weight = damping[pl.ds(k * jl + at, part), :]
-                outs[k, f, 0, pl.ds(at, part), :] += weight * fourth
-
-
-def wall_terms(both, damping, pieces, part, parts, made=(), wait=()):
-    m, _, zz, jl, nx = pieces.shape
+                rows = pl.ds(there, part)
+                outs[k][f, 0, pl.ds(at, part), :] = summed[rows, :] + damping[rows, :] * fourth
+
+
+def wall_terms(blocks, both, damping, pieces, part, parts, made=(), wait=()):
+    m = len(pieces)
+    _, zz, jl, nx = pieces[0].shape
     ny = m * jl
     steps = zz // parts
-    spec = pl.BlockSpec((m, 5, 1, jl, nx), lambda i: (0, 0, part * steps + i, 0, 0))
+    spec = pl.BlockSpec((5, 1, jl, nx), lambda i, s: (0, part * steps + i, 0, 0))
     return call(
-        wall_kernel,
+        functools.partial(wall_kernel, m),
         f"wall_terms_{part}",
-        (),
-        (both, damping, pieces, *made),
+        (blocks,),
+        (both, damping, *pieces, *made),
         (steps,),
-        [pl.BlockSpec((2 * ny, ny), lambda i: (0, 0)), pl.BlockSpec((ny, 1), lambda i: (0, 0)), spec]
+        [pl.BlockSpec((2 * ny, ny), lambda i, s: (0, 0)), pl.BlockSpec((ny, 1), lambda i, s: (0, 0))]
+        + [spec] * m
         + [pl.BlockSpec(memory_space=pl.ANY)] * len(made),
-        [spec],
-        [jax.ShapeDtypeStruct(pieces.shape, jnp.float32)],
+        [spec] * m,
+        [jax.ShapeDtypeStruct(p.shape, jnp.float32) for p in pieces],
         scratch=[
             pltpu.VMEM((5, ny + 16, nx), jnp.float32),
             pltpu.VMEM((5, ny, nx), jnp.bfloat16),
             pltpu.VMEM((5, ny, nx), jnp.bfloat16),
+            pltpu.VMEM((ny, nx), jnp.float32),
         ],
-        aliases={3: 0} if made else None,
+        aliases={3 + m + k: k for k in range(m)} if made else None,
         wait=wait,
         flops=6 * 5 * steps * ny * ny * nx,
     )
 
 
-def base_kernel(zl, density, momentum, energy, pieces, *refs):
-    outs, wall = refs[:3], refs[3]
-    _, _, zz, rows, nx = pieces.shape
+def base_kernel(m, zl, order, density, momentum, energy, *refs):
+    pieces, outs, wall = refs[:m], refs[m : m + 3], refs[m + 3]
+    _, zz, rows, nx = pieces[0].shape
     lane = wall.shape[-1]
-    for z in range(zl):
-        lines = pl.ds(z, rows, stride=zl)
-        for half in range(nx // lane):
-            lanes = slice(half * lane, (half + 1) * lane)
-            for f in range(5):
-                wall[half, f, lines, :] = pieces[z // zz, f, z % zz, :, lanes]
+    for k, piece in enumerate(pieces):
+        for z in range(zz):
+            lines = pl.ds(order[k] * zz + z, rows, stride=zl)
+            for half in range(nx // lane):
+                lanes = slice(half * lane, (half + 1) * lane)
+                for f in range(5):
+                    wall[half, f, lines, :] = piece[f, z, :, lanes]
     part = divisor_up_to(rows * zl, 64)
 
     @pl.loop(0, rows * zl // part)
@@ -295,22 +303,22 @@
                 outs[1][f - 1, here, :] = value
 
 
-def base_fields(density, momentum, energy, pieces, wait=()):
-    m = pieces.shape[0]
+def base_fields(blocks, density, momentum, energy, pieces, wait=()):
+    m = len(pieces)
     jl, zl, nx = density.shape
     zz = zl // m
     lane = divisor_up_to(nx, 128)
     rows = divisor_up_to(jl, 16)
-    flat = pl.BlockSpec((rows * zl, nx), lambda i: (i, 0))
-    three = pl.BlockSpec((3, rows * zl, nx), lambda i: (0, i, 0))
+    flat = pl.BlockSpec((rows * zl, nx), lambda i, s: (i, 0))
+    three = pl.BlockSpec((3, rows * zl, nx), lambda i, s: (0, i, 0))
     shape = jax.ShapeDtypeStruct((jl * zl, nx), jnp.float32)
     outs = call(
-        functools.partial(base_kernel, zl),
+        functools.partial(base_kernel, m, zl),
         "base_fields",
-        (),
-        (density.reshape(jl * zl, nx), momentum.reshape(3, jl * zl, nx), energy.reshape(jl * zl, nx), pieces),
+        (blocks,),
+        (density.reshape(jl * zl, nx), momentum.reshape(3, jl * zl, nx), energy.reshape(jl * zl, nx), *pieces),
         (jl // rows,),
-        [flat, three, flat, pl.BlockSpec((m, 5, zz, rows, nx), lambda i: (0, 0, 0, i, 0))],
+        [flat, three, flat] + [pl.BlockSpec((5, zz, rows, nx), lambda i, s: (0, 0, i, 0))] * m,
         [flat, three, flat],
         [shape, jax.ShapeDtypeStruct((3, jl * zl, nx), jnp.float32), shape],
         scratch=[pltpu.VMEM((nx // lane, 5, rows * zl, lane), jnp.float32)],
@@ -410,6 +418,8 @@
     rows = share // chunks
 
     span_to = [jnp.asarray(hop(gz, k, n, 1), jnp.int32).reshape(1) for k in range(n)]
+    wall_to = jnp.concatenate([jnp.asarray(hop(gy, k, m, 1), jnp.int32).reshape(1) for k in range(m)])
+    wall_from = jnp.concatenate([jnp.asarray(hop(gy, k, m, -1), jnp.int32).reshape(1) for k in range(m)])
     span_from = jnp.concatenate([jnp.asarray(hop(gz, k, n, -1), jnp.int32).reshape(1) for k in range(n)])
     by_share = (
         density.reshape(n, share, zl, nx),
@@ -426,15 +436,18 @@
     def ordered(pieces):
         return [pieces[k] for k in range(n)]
 
-    first_far = sender.send_far(pack(0), far, 1)
-    first_near = sender.send_near(pack(0), near, 1, 0)
-    span_out = [ordered({0: pack(0)(0, ()), **first_far, **first_near})]
-    packed = pack_wall(m, density, momentum, energy, [first_near[k] for k in near[:1]])
-    wall_out = lax.all_to_all(packed, "gy", split_axis=0, concat_axis=0, tiled=True)
-    for c in range(1, chunks):
-        later_far = sender.send_far(pack(c), far, 1, [packed])
-        later_near = sender.send_near(pack(c), near, 1, c * count)
-        span_out.append(ordered({0: pack(c)(0, ()), **later_far, **later_near}))
+    def wall_exchange(pieces, sign):
+        walls = Sender("gy", m, m)
+        moved = walls.send_far(lambda k, wait: after(pieces[k], wait), range(1, m), sign)
+        return [pieces[0], *[moved[k] for k in range(1, m)]]
+
+    span_out = []
+    for c in range(chunks):
+        far_out = sender.send_far(pack(c), far, 1)
+        near_out = sender.send_near(pack(c), near, 1, c * count + NEAR)
+        span_out.append(ordered({0: pack(c)(0, ()), **far_out, **near_out}))
+        if c == 0:
+            wall_out = wall_exchange(pack_wall(wall_to, density, momentum, energy), 1)
 
     identity = jnp.eye(nz, dtype=jnp.float32)
     fourth = 6.0 * identity
@@ -461,16 +474,17 @@
     parts = divisor_up_to(zz, 2)
     wall_back = ()
     for part in range(parts):
-        begun = sender.far[: count + 1] if part == 0 else sender.far[count + part : count + part + 1]
-        wall_back = wall_terms(wall_both, damping.reshape(ny, 1), wall_out, part, parts, wall_back, begun)
-    wall_back = lax.all_to_all(wall_back[0], "gy", split_axis=0, concat_axis=0, tiled=True)
+        begun = []
+        wall_back = wall_terms(
+            wall_from, wall_both, damping.reshape(ny, 1), wall_out, part, parts, wall_back, begun
+        )
+    wall_back = wall_exchange(wall_back, -1)
 
     pieces, make = back(0)
     far_back = sender.send_far(make, far, -1)
-    near_back = sender.send_near(make, near, -1, chunks * count)
+    near_back = sender.send_near(make, near, -1, chunks * count + NEAR)
     span_back = [ordered({0: pieces[0], **far_back, **near_back})]
-    held = sender.far[-(1 + count // 4) :][:1]
-    *fields, mark = base_fields(density, momentum, energy, wall_back, [*held, *near_back.values()])
+    *fields, mark = base_fields(wall_to, density, momentum, energy, wall_back)
     fields = (
         fields[0].reshape(n, share, zl, nx),
         fields[1].reshape(3, n, share, zl, nx),
@@ -484,13 +498,10 @@
 
     for c in range(1, chunks):
         pieces, make = back(c)
-        far_back = sender.send_far(make, far[:1], -1)
-        far_back |= sender.send_far(make, far[1:2], -1, [mark])
-        far_back |= sender.send_far(make, far[2:], -1)
-        fields, mark = add(c - 1, [0, *near, *far], [far_back[far[0]]])
-        begin = (chunks + c) * count + 2
-        near_back = sender.send_near(make, near[:-1], -1, begin)
-        near_back |= {k: sender.permute(make(k, [mark, far_back[far[-2]]]), k, -1) for k in near[-1:]}
+        far_back = sender.send_far(make, far[:-2], -1)
+        far_back |= sender.send_far(make, far[-2:], -1, [mark])
+        fields, mark = add(c - 1, [0, *near, *far])
+        near_back = sender.send_near(make, near, -1, (chunks + c) * count + NEAR - 0)
         span_back.append(ordered({0: pieces[0], **far_back, **near_back}))
     last = chunks - 1
     groups = [(last, [0, *near]), (last, far[: count // 2]), (last, far[count // 2 :])]

time: 1030 us -> 1130 us (1.097)
  starting transfers between devices: 48.4 us -> 124 us
  waiting for transfers between devices: 712 us -> 737 us
    ppermute x28 -> x34, starting transfers between devices: 32.6 us -> 124 us  [permute(): return lax.ppermute(piece, self.axis, pairs)]
    ppermute x28 -> x34, waiting for transfers between devices: 712 us -> 737 us  [permute(): return lax.ppermute(piece, self.axis, pairs)]
    all_to_all x2 -> x0, starting transfers between devices: 15.8 us -> none  [the longest x1 7.9 us: local(): lax.all_to_all(packed, 'gy', split_axis=0, concat_axis=0, tiled=True)]
  transfers between devices with their start and end apart: 30 -> 34, of which waited for: 19 -> 18; matrix products, arithmetic and copies ran while one was open for 2% -> 2% of each run, Pallas kernels for 17% -> 19%
where the time goes in v4:
time: 1130 us; the launch traced here: 1120 us
  waiting for transfers between devices  737 us (65%)
  Pallas kernels  243 us (22%)
  starting transfers between devices  124 us (11%)
    ppermute x34, waiting for transfers between devices, permute(): return lax.ppermute(piece, self.axis, pairs)  737 us
    pallas_call x26, Pallas kernels, call(): pl.pallas_call(body, name=name, grid_spec=pltpu.PrefetchScalarGridSpec(nu...  243 us
    ppermute x34, starting transfers between devices, permute(): return lax.ppermute(piece, self.axis, pairs)  124 us
  transfers between devices with their start and end apart: 34, of which 18 were waited for; matrix products, arithmetic and copies ran while one was open for 2% of the time, Pallas kernels for 19%

profile of v4, /device:TPU:15, one launch (start us, length us, event | category | flops | bytes accessed | tf_op | source)
XLA Modules:
  0.0 1123.8 jit_solution(17490483968849322684)
XLA Ops:
  1.3 20.8 %pack_wall.1 = (f32[5,4,256,256]{3,2,1,0:T(8,128)}, f32[5,4,256,256]{3,2,1,0:T(8,128)}, f32[5,4,256,256]{3,2,1,0:T(8,128)}, f32[5,4,256,256]{3,2,1,0:T(8,128)}) custom-call(s32[4]{0:T(128)} %pad_add_fusion.3.order.refs_0_, f32[4096,256]{1,0:T(8,128)} %bitcast.51, f32[3,4096,256]{2,1,0:T(8,128)} %bitcast.33, f32[4096,256]{1,0:T(8,128)} %bitcast.69), custom_call_target="tpu_custom_call" | custom-call | bytes 41943040 | tf_op jit(solution)/shard_map/pack_wall/pallas_call | solution.py:80
  27.0 2.7 collective-permute-start.6
  32.0 2.3 pack_span_1.9
  36.5 2.2 pack_span_0.13
  38.8 2.3 pack_span_1.13
  42.0 2.3 pack_span_0.15
  44.3 3.1 reduce-precision_convert_fusion
  47.4 2.5 pad_maximum_fusion.both
  49.9 86.5 %collective-permute-done.refs_1_ = f32[5,4,256,256]{3,2,1,0:T(8,128)} collective-permute-done((f32[5,4,256,256]{3,2,1,0:T(8,128)}, f32[5,4,256,256]{3,2,1,0:T(8,128)}, u32[]{:S(2)}, u32[]{:S(2)}) %collective-permute-start) | collective-permute-done | bytes 5242912 | tf_op jit(solution)/shard_map/ppermute | solution.py:395
  136.3 4.9 collective-permute-start.10
  141.3 107.5 %collective-permute-done.2.refs_3_ = f32[5,4,256,256]{3,2,1,0:T(8,128)} collective-permute-done((f32[5,4,256,256]{3,2,1,0:T(8,128)}, f32[5,4,256,256]{3,2,1,0:T(8,128)}, u32[]{:S(2)}, u32[]{:S(2)}) %collective-permute-start.2) | collective-permute-done | bytes 5242912 | tf_op jit(solution)/shard_map/ppermute | solution.py:395
  248.8 3.2 collective-permute-start.20
  252.0 35.4 %wall_terms_0.1 = (f32[5,4,256,256]{3,2,1,0:T(8,128)}, f32[5,4,256,256]{3,2,1,0:T(8,128)}, f32[5,4,256,256]{3,2,1,0:T(8,128)}, f32[5,4,256,256]{3,2,1,0:T(8,128)}) custom-call(s32[4]{0:T(128)} %pad_add_fusion.3.order.refs_0_, bf16[2048,1024]{1,0:T(8,128)(2,1)} %pad_maximum_fusion.both, f32[1024,1]{1,0:T(8,128)} %copy.38.damping, ...), custom_call_target="tpu_custom_call" | custom-call | flops 16106127360 | bytes 50335744 | tf_op jit(solution)/shard_map/wall_terms_0/pallas_call | solution.py:80
  287.5 2.5 collective-permute-start.22
  291.0 35.4 %wall_terms_1.1 = (f32[5,4,256,256]{3,2,1,0:T(8,128)}, f32[5,4,256,256]{3,2,1,0:T(8,128)}, f32[5,4,256,256]{3,2,1,0:T(8,128)}, f32[5,4,256,256]{3,2,1,0:T(8,128)}) custom-call(s32[4]{0:T(128)} %pad_add_fusion.3.order.refs_0_, bf16[2048,1024]{1,0:T(8,128)(2,1)} %pad_maximum_fusion.both, ...), custom_call_target="tpu_custom_call", output_to_operand_aliasing={{0}: (7, {}), {1}: (8, {}), {2}: (9, {}), {3}: (10, {})} | custom-call | flops 16106127360 | bytes 71307264 | tf_op jit(solution)/shard_map/wall_terms_1/pallas_call | solution.py:80
  330.7 104.6 %collective-permute-done.20.refs_4_.refs_7_ = f32[5,16,16,256]{3,2,1,0:T(8,128)} collective-permute-done((f32[5,16,16,256]{3,2,1,0:T(8,128)}, f32[5,16,16,256]{3,2,1,0:T(8,128)}, u32[]{:S(2)}, u32[]{:S(2)}) %collective-permute-start.20) | collective-permute-done | bytes 1310752 | tf_op jit(solution)/shard_map/ppermute | solution.py:395
  439.7 25.5 %collective-permute-start.7 = (f32[5,16,16,256]{3,2,1,0:T(8,128)}, f32[5,16,16,256]{3,2,1,0:T(8,128)}, u32[]{:S(2)}, u32[]{:S(2)}) collective-permute-start(f32[5,16,16,256]{3,2,1,0:T(8,128)} %pack_span_0.10), channel_id=1, source_target_pairs={{0,1},{1,0},{2,3},{3,2},{4,5},{5,4},{6,7},{7,6},{8,9},{9,8},{10,11... | collective-permute-start | bytes 3932168 | tf_op jit(solution)/shard_map/ppermute | solution.py:395
  465.2 27.2 %collective-permute-start.9 = (f32[5,16,16,256]{3,2,1,0:T(8,128)}, f32[5,16,16,256]{3,2,1,0:T(8,128)}, u32[]{:S(2)}, u32[]{:S(2)}) collective-permute-start(f32[5,16,16,256]{3,2,1,0:T(8,128)} %pack_span_0.12), channel_id=1, source_target_pairs={{0,2},{1,3},{2,0},{3,1},{4,6},{5,7},{6,4},{7,5},{8,10},{9,11},{10,... | collective-permute-start | bytes 3932168 | tf_op jit(solution)/shard_map/ppermute | solution.py:395
  493.8 2.2 pack_span_0.8.refs_0_
  496.0 2.2 pack_span_1.8.refs_0_
  499.9 2.2 pack_span_0.14
  502.1 2.2 pack_span_1.10
  504.4 16.2 %collective-permute-start.11 = (f32[5,16,16,256]{3,2,1,0:T(8,128)}, f32[5,16,16,256]{3,2,1,0:T(8,128)}, u32[]{:S(2)}, u32[]{:S(2)}) collective-permute-start(f32[5,16,16,256]{3,2,1,0:T(8,128)} %pack_span_0.14), channel_id=1, source_target_pairs={{0,3},{1,2},{2,1},{3,0},{4,7},{5,6},{6,5},{7,4},{8,11},{9,10},{10,... | collective-permute-start | bytes 3932168 | tf_op jit(solution)/shard_map/ppermute | solution.py:395
  520.5 13.2 %collective-permute-done.9.refs_2_ = f32[5,16,16,256]{3,2,1,0:T(8,128)} collective-permute-done((f32[5,16,16,256]{3,2,1,0:T(8,128)}, f32[5,16,16,256]{3,2,1,0:T(8,128)}, u32[]{:S(2)}, u32[]{:S(2)}) %collective-permute-start.9) | collective-permute-done | bytes 1310752 | tf_op jit(solution)/shard_map/ppermute | solution.py:395
  543.0 18.8 %collective-permute-done.11.refs_3_ = f32[5,16,16,256]{3,2,1,0:T(8,128)} collective-permute-done((f32[5,16,16,256]{3,2,1,0:T(8,128)}, f32[5,16,16,256]{3,2,1,0:T(8,128)}, u32[]{:S(2)}, u32[]{:S(2)}) %collective-permute-start.11) | collective-permute-done | bytes 1310752 | tf_op jit(solution)/shard_map/ppermute | solution.py:395
  568.0 13.9 %span_terms_0.1 = (f32[5,16,16,256]{3,2,1,0:T(8,128)}, f32[5,16,16,256]{3,2,1,0:T(8,128)}, f32[5,16,16,256]{3,2,1,0:T(8,128)}, f32[5,16,16,256]{3,2,1,0:T(8,128)...) custom-call(f32[16]{0:T(128)} %get-tuple-element.106.weights, ...), custom_call_target="tpu_custom_call" | custom-call | flops 4026531840 | bytes 21233664 | tf_op jit(solution)/shard_map/span_terms_0/pallas_call | solution.py:80
  581.9 11.3 %collective-permute-done.23.refs_2_ = f32[5,16,16,256]{3,2,1,0:T(8,128)} collective-permute-done((f32[5,16,16,256]{3,2,1,0:T(8,128)}, f32[5,16,16,256]{3,2,1,0:T(8,128)}, u32[]{:S(2)}, u32[]{:S(2)}) %collective-permute-start.23) | collective-permute-done | bytes 1310752 | tf_op jit(solution)/shard_map/ppermute | solution.py:395
  593.1 2.5 collective-permute-start.13
  595.7 26.6 %collective-permute-done.25.refs_3_ = f32[5,16,16,256]{3,2,1,0:T(8,128)} collective-permute-done((f32[5,16,16,256]{3,2,1,0:T(8,128)}, f32[5,16,16,256]{3,2,1,0:T(8,128)}, u32[]{:S(2)}, u32[]{:S(2)}) %collective-permute-start.25) | collective-permute-done | bytes 1310752 | tf_op jit(solution)/shard_map/ppermute | solution.py:395
  625.0 13.9 %span_terms_1.1 = (f32[5,16,16,256]{3,2,1,0:T(8,128)}, f32[5,16,16,256]{3,2,1,0:T(8,128)}, f32[5,16,16,256]{3,2,1,0:T(8,128)}, f32[5,16,16,256]{3,2,1,0:T(8,128)...) custom-call(f32[16]{0:T(128)} %get-tuple-element.105.weights, ...), custom_call_target="tpu_custom_call" | custom-call | flops 4026531840 | bytes 21233664 | tf_op jit(solution)/shard_map/span_terms_1/pallas_call | solution.py:80
  638.9 21.8 %collective-permute-done.4.refs_6_ = f32[5,4,256,256]{3,2,1,0:T(8,128)} collective-permute-done((f32[5,4,256,256]{3,2,1,0:T(8,128)}, f32[5,4,256,256]{3,2,1,0:T(8,128)}, u32[]{:S(2)}, u32[]{:S(2)}) %collective-permute-start.4) | collective-permute-done | bytes 5242912 | tf_op jit(solution)/shard_map/ppermute | solution.py:395
  660.7 22.0 %collective-permute-start.27 = (f32[5,16,16,256]{3,2,1,0:T(8,128)}, f32[5,16,16,256]{3,2,1,0:T(8,128)}, u32[]{:S(2)}, u32[]{:S(2)}) collective-permute-start(f32[5,16,16,256]{3,2,1,0:T(8,128)} %get-tuple-element.77), channel_id=1, source_target_pairs={{0,7},{1,6},{2,5},{3,4},{4,3},{5,2},{6,1},{7,0},{8,15},{9,14},{10,... | collective-permute-start | bytes 3932168 | tf_op jit(solution)/shard_map/ppermute | solution.py:395
  682.6 49.4 %base_fields.1 = (f32[4096,256]{1,0:T(8,128)}, f32[3,4096,256]{2,1,0:T(8,128)}, f32[4096,256]{1,0:T(8,128)}, f32[8,128]{1,0:T(8,128)}) custom-call(s32[4]{0:T(128)} %pad_add_fusion.3.order.refs_0_, f32[4096,256]{1,0:T(8,128)} %bitcast.68, f32[3,4096,256]{2,1,0:T(8,128)} %bitcast.50, f32[4096,256]{1,0:T(8,128)} %bitcast.86, ...), custom_call_target="tpu_custom_call" | custom-call | bytes 62914560 | tf_op jit(solution)/shard_map/base_fields/pallas_call | solution.py:80
  732.1 33.9 %collective-permute-done.13.refs_1_.refs_8_ = f32[5,16,16,256]{3,2,1,0:T(8,128)} collective-permute-done((f32[5,16,16,256]{3,2,1,0:T(8,128)}, f32[5,16,16,256]{3,2,1,0:T(8,128)}, u32[]{:S(2)}, u32[]{:S(2)}) %collective-permute-start.13) | collective-permute-done | bytes 1310752 | tf_op jit(solution)/shard_map/ppermute | solution.py:395
  766.0 56.2 %collective-permute-done.15.refs_1_.refs_9_ = f32[5,16,16,256]{3,2,1,0:T(8,128)} collective-permute-done((f32[5,16,16,256]{3,2,1,0:T(8,128)}, f32[5,16,16,256]{3,2,1,0:T(8,128)}, u32[]{:S(2)}, u32[]{:S(2)}) %collective-permute-start.15) | collective-permute-done | bytes 1310752 | tf_op jit(solution)/shard_map/ppermute | solution.py:395
  822.2 55.2 %collective-permute-done.17.refs_1_.refs_10_ = f32[5,16,16,256]{3,2,1,0:T(8,128)} collective-permute-done((f32[5,16,16,256]{3,2,1,0:T(8,128)}, f32[5,16,16,256]{3,2,1,0:T(8,128)}, u32[]{:S(2)}, u32[]{:S(2)}) %collective-permute-start.17) | collective-permute-done | bytes 1310752 | tf_op jit(solution)/shard_map/ppermute | solution.py:395
  877.3 29.1 %collective-permute-done.27.refs_1_.refs_4_ = f32[5,16,16,256]{3,2,1,0:T(8,128)} collective-permute-done((f32[5,16,16,256]{3,2,1,0:T(8,128)}, f32[5,16,16,256]{3,2,1,0:T(8,128)}, u32[]{:S(2)}, u32[]{:S(2)}) %collective-permute-start.27) | collective-permute-done | bytes 1310752 | tf_op jit(solution)/shard_map/ppermute | solution.py:395
  906.4 28.1 %collective-permute-done.29.refs_1_.refs_5_ = f32[5,16,16,256]{3,2,1,0:T(8,128)} collective-permute-done((f32[5,16,16,256]{3,2,1,0:T(8,128)}, f32[5,16,16,256]{3,2,1,0:T(8,128)}, u32[]{:S(2)}, u32[]{:S(2)}) %collective-permute-start.29) | collective-permute-done | bytes 1310752 | tf_op jit(solution)/shard_map/ppermute | solution.py:395
  934.5 27.1 %collective-permute-done.31.refs_1_.refs_4_ = f32[5,16,16,256]{3,2,1,0:T(8,128)} collective-permute-done((f32[5,16,16,256]{3,2,1,0:T(8,128)}, f32[5,16,16,256]{3,2,1,0:T(8,128)}, u32[]{:S(2)}, u32[]{:S(2)}) %collective-permute-start.31) | collective-permute-done | bytes 1310752 | tf_op jit(solution)/shard_map/ppermute | solution.py:395
  961.7 27.2 %collective-permute-done.19.refs_11_ = f32[5,16,16,256]{3,2,1,0:T(8,128)} collective-permute-done((f32[5,16,16,256]{3,2,1,0:T(8,128)}, f32[5,16,16,256]{3,2,1,0:T(8,128)}, u32[]{:S(2)}, u32[]{:S(2)}) %collective-permute-start.19) | collective-permute-done | bytes 1310752 | tf_op jit(solution)/shard_map/ppermute | solution.py:395
  988.9 3.1 collective-permute-start.30
  995.7 51.5 %collective-permute-done.18.refs_7_ = f32[5,16,16,256]{3,2,1,0:T(8,128)} collective-permute-done((f32[5,16,16,256]{3,2,1,0:T(8,128)}, f32[5,16,16,256]{3,2,1,0:T(8,128)}, u32[]{:S(2)}, u32[]{:S(2)}) %collective-permute-start.18) | collective-permute-done | bytes 1310752 | tf_op jit(solution)/shard_map/ppermute | solution.py:395
  1047.2 18.0 %add_span_0.1 = (f32[8,32,16,256]{3,2,1,0:T(8,128)}, f32[3,8,32,16,256]{4,3,2,1,0:T(8,128)}, f32[8,32,16,256]{3,2,1,0:T(8,128)}, f32[8,128]{1,0:T(8,128)}) custom-call(s32[8]{0:T(128)} %concatenate.51.refs_0_, f32[8,32,16,256]{3,2,1,0:T(8,128)} %bitcast.89, ...), custom_call_target="tpu_custom_call", output_to_operand_aliasing={{0}: (1, {}), {1}: (2, {}), {2}: (3, {})} | custom-call | bytes 52428800 | tf_op jit(solution)/shard_map/add_span_0/pallas_call | solution.py:80
  1065.2 10.1 collective-permute-done.30.refs_6_
  1075.3 28.1 %collective-permute-done.32.refs_7_ = f32[5,16,16,256]{3,2,1,0:T(8,128)} collective-permute-done((f32[5,16,16,256]{3,2,1,0:T(8,128)}, f32[5,16,16,256]{3,2,1,0:T(8,128)}, u32[]{:S(2)}, u32[]{:S(2)}) %collective-permute-start.32) | collective-permute-done | bytes 1310752 | tf_op jit(solution)/shard_map/ppermute | solution.py:395
  1103.4 9.5 add_span_1.3
  1112.8 5.4 add_span_1.4
  1118.3 5.4 add_span_1.5
  (103 shorter events, 45.6 us)
Async XLA Ops:
  22.1 114.2 %collective-permute-start = (f32[5,4,256,256]{3,2,1,0:T(8,128)}, f32[5,4,256,256]{3,2,1,0:T(8,128)}, u32[]{:S(2)}, u32[]{:S(2)}) collective-permute-start(f32[5,4,256,256]{3,2,1,0:T(8,128)} %get-tuple-element.50), channel_id=1, source_target_pairs={{0,8},{8,0},{16,24},{24,16},{1,9},{9,1},{17,25},{25,17},{2,10},{10... | collective-permute-start | bytes 15728648 | tf_op jit(solution)/shard_map/ppermute | solution.py:395
  22.4 118.9 %collective-permute-start.1 = (f32[5,4,256,256]{3,2,1,0:T(8,128)}, f32[5,4,256,256]{3,2,1,0:T(8,128)}, u32[]{:S(2)}, u32[]{:S(2)}) collective-permute-start(f32[5,4,256,256]{3,2,1,0:T(8,128)} %get-tuple-element.51), channel_id=1, source_target_pairs={{0,16},{8,24},{16,0},{24,8},{1,17},{9,25},{17,1},{25,9},{2,18},{10... | collective-permute-start | bytes 15728648 | tf_op jit(solution)/shard_map/ppermute | solution.py:395
  22.7 226.1 %collective-permute-start.2 = (f32[5,4,256,256]{3,2,1,0:T(8,128)}, f32[5,4,256,256]{3,2,1,0:T(8,128)}, u32[]{:S(2)}, u32[]{:S(2)}) collective-permute-start(f32[5,4,256,256]{3,2,1,0:T(8,128)} %get-tuple-element.52), channel_id=1, source_target_pairs={{0,24},{8,16},{16,8},{24,0},{1,25},{9,17},{17,9},{25,1},{2,26},{10... | collective-permute-start | bytes 15728648 | tf_op jit(solution)/shard_map/ppermute | solution.py:395
  27.0 260.5 %collective-permute-start.6 = (f32[5,16,16,256]{3,2,1,0:T(8,128)}, f32[5,16,16,256]{3,2,1,0:T(8,128)}, u32[]{:S(2)}, u32[]{:S(2)}) collective-permute-start(f32[5,16,16,256]{3,2,1,0:T(8,128)} %pack_span_0.9), channel_id=1, source_target_pairs={{0,7},{1,6},{2,5},{3,4},{4,3},{5,2},{6,1},{7,0},{8,15},{9,14},{10,... | collective-permute-start | bytes 3932168 | tf_op jit(solution)/shard_map/ppermute | solution.py:395
  31.8 258.1 %collective-permute-start.8 = (f32[5,16,16,256]{3,2,1,0:T(8,128)}, f32[5,16,16,256]{3,2,1,0:T(8,128)}, u32[]{:S(2)}, u32[]{:S(2)}) collective-permute-start(f32[5,16,16,256]{3,2,1,0:T(8,128)} %pack_span_0.11), channel_id=1, source_target_pairs={{0,6},{1,7},{2,4},{3,5},{4,2},{5,3},{6,0},{7,1},{8,14},{9,15},{10,... | collective-permute-start | bytes 3932168 | tf_op jit(solution)/shard_map/ppermute | solution.py:395
  38.8 2.3 copy-start.2
  136.3 190.1 %collective-permute-start.10 = (f32[5,16,16,256]{3,2,1,0:T(8,128)}, f32[5,16,16,256]{3,2,1,0:T(8,128)}, u32[]{:S(2)}, u32[]{:S(2)}) collective-permute-start(f32[5,16,16,256]{3,2,1,0:T(8,128)} %pack_span_0.13), channel_id=1, source_target_pairs={{0,5},{1,4},{2,7},{3,6},{4,1},{5,0},{6,3},{7,2},{8,13},{9,12},{10,... | collective-permute-start | bytes 3932168 | tf_op jit(solution)/shard_map/ppermute | solution.py:395
  141.2 188.7 %collective-permute-start.12 = (f32[5,16,16,256]{3,2,1,0:T(8,128)}, f32[5,16,16,256]{3,2,1,0:T(8,128)}, u32[]{:S(2)}, u32[]{:S(2)}) collective-permute-start(f32[5,16,16,256]{3,2,1,0:T(8,128)} %pack_span_0.15), channel_id=1, source_target_pairs={{0,4},{1,5},{2,6},{3,7},{4,0},{5,1},{6,2},{7,3},{8,12},{9,13},{10,... | collective-permute-start | bytes 3932168 | tf_op jit(solution)/shard_map/ppermute | solution.py:395
  248.8 186.4 %collective-permute-start.20 = (f32[5,16,16,256]{3,2,1,0:T(8,128)}, f32[5,16,16,256]{3,2,1,0:T(8,128)}, u32[]{:S(2)}, u32[]{:S(2)}) collective-permute-start(f32[5,16,16,256]{3,2,1,0:T(8,128)} %pack_span_1.9), channel_id=1, source_target_pairs={{0,7},{1,6},{2,5},{3,4},{4,3},{5,2},{6,1},{7,0},{8,15},{9,14},{10,... | collective-permute-start | bytes 3932168 | tf_op jit(solution)/shard_map/ppermute | solution.py:395
  287.5 152.2 %collective-permute-start.22 = (f32[5,16,16,256]{3,2,1,0:T(8,128)}, f32[5,16,16,256]{3,2,1,0:T(8,128)}, u32[]{:S(2)}, u32[]{:S(2)}) collective-permute-start(f32[5,16,16,256]{3,2,1,0:T(8,128)} %pack_span_1.11), channel_id=1, source_target_pairs={{0,6},{1,7},{2,4},{3,5},{4,2},{5,3},{6,0},{7,1},{8,14},{9,15},{10,... | collective-permute-start | bytes 3932168 | tf_op jit(solution)/shard_map/ppermute | solution.py:395
  290.0 175.2 %collective-permute-start.24 = (f32[5,16,16,256]{3,2,1,0:T(8,128)}, f32[5,16,16,256]{3,2,1,0:T(8,128)}, u32[]{:S(2)}, u32[]{:S(2)}) collective-permute-start(f32[5,16,16,256]{3,2,1,0:T(8,128)} %pack_span_1.13), channel_id=1, source_target_pairs={{0,5},{1,4},{2,7},{3,6},{4,1},{5,0},{6,3},{7,2},{8,13},{9,12},{10,... | collective-permute-start | bytes 3932168 | tf_op jit(solution)/shard_map/ppermute | solution.py:395
  326.4 297.0 %collective-permute-start.3 = (f32[5,4,256,256]{3,2,1,0:T(8,128)}, f32[5,4,256,256]{3,2,1,0:T(8,128)}, u32[]{:S(2)}, u32[]{:S(2)}) collective-permute-start(f32[5,4,256,256]{3,2,1,0:T(8,128)} %get-tuple-element.58), channel_id=1, source_target_pairs={{0,8},{8,0},{16,24},{24,16},{1,9},{9,1},{17,25},{25,17},{2,10},{10... | collective-permute-start | bytes 15728648 | tf_op jit(solution)/shard_map/ppermute | solution.py:395
  329.9 162.4 %collective-permute-start.26 = (f32[5,16,16,256]{3,2,1,0:T(8,128)}, f32[5,16,16,256]{3,2,1,0:T(8,128)}, u32[]{:S(2)}, u32[]{:S(2)}) collective-permute-start(f32[5,16,16,256]{3,2,1,0:T(8,128)} %pack_span_1.15), channel_id=1, source_target_pairs={{0,4},{1,5},{2,6},{3,7},{4,0},{5,1},{6,2},{7,3},{8,12},{9,13},{10,... | collective-permute-start | bytes 3932168 | tf_op jit(solution)/shard_map/ppermute | solution.py:395
  435.3 225.4 %collective-permute-start.4 = (f32[5,4,256,256]{3,2,1,0:T(8,128)}, f32[5,4,256,256]{3,2,1,0:T(8,128)}, u32[]{:S(2)}, u32[]{:S(2)}) collective-permute-start(f32[5,4,256,256]{3,2,1,0:T(8,128)} %get-tuple-element.59), channel_id=1, source_target_pairs={{0,16},{8,24},{16,0},{24,8},{1,17},{9,25},{17,1},{25,9},{2,18},{10... | collective-permute-start | bytes 15728648 | tf_op jit(solution)/shard_map/ppermute | solution.py:395
  439.7 64.7 %collective-permute-start.7 = (f32[5,16,16,256]{3,2,1,0:T(8,128)}, f32[5,16,16,256]{3,2,1,0:T(8,128)}, u32[]{:S(2)}, u32[]{:S(2)}) collective-permute-start(f32[5,16,16,256]{3,2,1,0:T(8,128)} %pack_span_0.10), channel_id=1, source_target_pairs={{0,1},{1,0},{2,3},{3,2},{4,5},{5,4},{6,7},{7,6},{8,9},{9,8},{10,11... | collective-permute-start | bytes 3932168 | tf_op jit(solution)/shard_map/ppermute | solution.py:395
  465.2 68.6 %collective-permute-start.9 = (f32[5,16,16,256]{3,2,1,0:T(8,128)}, f32[5,16,16,256]{3,2,1,0:T(8,128)}, u32[]{:S(2)}, u32[]{:S(2)}) collective-permute-start(f32[5,16,16,256]{3,2,1,0:T(8,128)} %pack_span_0.12), channel_id=1, source_target_pairs={{0,2},{1,3},{2,0},{3,1},{4,6},{5,7},{6,4},{7,5},{8,10},{9,11},{10,... | collective-permute-start | bytes 3932168 | tf_op jit(solution)/shard_map/ppermute | solution.py:395
  492.4 190.3 %collective-permute-start.5 = (f32[5,4,256,256]{3,2,1,0:T(8,128)}, f32[5,4,256,256]{3,2,1,0:T(8,128)}, u32[]{:S(2)}, u32[]{:S(2)}) collective-permute-start(f32[5,4,256,256]{3,2,1,0:T(8,128)} %get-tuple-element.60), channel_id=1, source_target_pairs={{0,24},{8,16},{16,8},{24,0},{1,25},{9,17},{17,9},{25,1},{2,26},{10... | collective-permute-start | bytes 15728648 | tf_op jit(solution)/shard_map/ppermute | solution.py:395
  504.4 30.3 %copy-start.1 = (f32[128,128]{1,0:T(8,128)S(1)}, f32[128,128]{1,0:T(8,128)}, u32[]{:S(2)}) copy-start(f32[128,128]{1,0:T(8,128)} %param.14) | copy-start | bytes 196612
  504.4 30.5 %copy-start = (f32[8,16,8,16]{3,2,1,0:T(8,128)S(1)}, f32[8,16,8,16]{3,2,1,0:T(8,128)}, u32[]{:S(2)}) copy-start(f32[8,16,8,16]{3,2,1,0:T(8,128)} %concatenate.58) | copy-start | bytes 196612
  504.4 57.5 %collective-permute-start.11 = (f32[5,16,16,256]{3,2,1,0:T(8,128)}, f32[5,16,16,256]{3,2,1,0:T(8,128)}, u32[]{:S(2)}, u32[]{:S(2)}) collective-permute-start(f32[5,16,16,256]{3,2,1,0:T(8,128)} %pack_span_0.14), channel_id=1, source_target_pairs={{0,3},{1,2},{2,1},{3,0},{4,7},{5,6},{6,5},{7,4},{8,11},{9,10},{10,... | collective-permute-start | bytes 3932168 | tf_op jit(solution)/shard_map/ppermute | solution.py:395
  533.7 30.3 %collective-permute-start.21 = (f32[5,16,16,256]{3,2,1,0:T(8,128)}, f32[5,16,16,256]{3,2,1,0:T(8,128)}, u32[]{:S(2)}, u32[]{:S(2)}) collective-permute-start(f32[5,16,16,256]{3,2,1,0:T(8,128)} %pack_span_1.10), channel_id=1, source_target_pairs={{0,1},{1,0},{2,3},{3,2},{4,5},{5,4},{6,7},{7,6},{8,9},{9,8},{10,11... | collective-permute-start | bytes 3932168 | tf_op jit(solution)/shard_map/ppermute | solution.py:395
  561.8 31.3 %collective-permute-start.23 = (f32[5,16,16,256]{3,2,1,0:T(8,128)}, f32[5,16,16,256]{3,2,1,0:T(8,128)}, u32[]{:S(2)}, u32[]{:S(2)}) collective-permute-start(f32[5,16,16,256]{3,2,1,0:T(8,128)} %pack_span_1.12), channel_id=1, source_target_pairs={{0,2},{1,3},{2,0},{3,1},{4,6},{5,7},{6,4},{7,5},{8,10},{9,11},{10,... | collective-permute-start | bytes 3932168 | tf_op jit(solution)/shard_map/ppermute | solution.py:395
  564.0 58.3 %collective-permute-start.25 = (f32[5,16,16,256]{3,2,1,0:T(8,128)}, f32[5,16,16,256]{3,2,1,0:T(8,128)}, u32[]{:S(2)}, u32[]{:S(2)}) collective-permute-start(f32[5,16,16,256]{3,2,1,0:T(8,128)} %pack_span_1.14), channel_id=1, source_target_pairs={{0,3},{1,2},{2,1},{3,0},{4,7},{5,6},{6,5},{7,4},{8,11},{9,10},{10,... | collective-permute-start | bytes 3932168 | tf_op jit(solution)/shard_map/ppermute | solution.py:395
  593.1 172.9 %collective-permute-start.13 = (f32[5,16,16,256]{3,2,1,0:T(8,128)}, f32[5,16,16,256]{3,2,1,0:T(8,128)}, u32[]{:S(2)}, u32[]{:S(2)}) collective-permute-start(f32[5,16,16,256]{3,2,1,0:T(8,128)} %get-tuple-element.66), channel_id=1, source_target_pairs={{0,7},{1,6},{2,5},{3,4},{4,3},{5,2},{6,1},{7,0},{8,15},{9,14},{10,... | collective-permute-start | bytes 3932168 | tf_op jit(solution)/shard_map/ppermute | solution.py:395
  622.3 199.9 %collective-permute-start.15 = (f32[5,16,16,256]{3,2,1,0:T(8,128)}, f32[5,16,16,256]{3,2,1,0:T(8,128)}, u32[]{:S(2)}, u32[]{:S(2)}) collective-permute-start(f32[5,16,16,256]{3,2,1,0:T(8,128)} %get-tuple-element.68), channel_id=1, source_target_pairs={{0,6},{1,7},{2,4},{3,5},{4,2},{5,3},{6,0},{7,1},{8,14},{9,15},{10,... | collective-permute-start | bytes 3932168 | tf_op jit(solution)/shard_map/ppermute | solution.py:395
  623.5 253.9 %collective-permute-start.17 = (f32[5,16,16,256]{3,2,1,0:T(8,128)}, f32[5,16,16,256]{3,2,1,0:T(8,128)}, u32[]{:S(2)}, u32[]{:S(2)}) collective-permute-start(f32[5,16,16,256]{3,2,1,0:T(8,128)} %get-tuple-element.70), channel_id=1, source_target_pairs={{0,5},{1,4},{2,7},{3,6},{4,1},{5,0},{6,3},{7,2},{8,13},{9,12},{10,... | collective-permute-start | bytes 3932168 | tf_op jit(solution)/shard_map/ppermute | solution.py:395
  660.7 245.8 %collective-permute-start.27 = (f32[5,16,16,256]{3,2,1,0:T(8,128)}, f32[5,16,16,256]{3,2,1,0:T(8,128)}, u32[]{:S(2)}, u32[]{:S(2)}) collective-permute-start(f32[5,16,16,256]{3,2,1,0:T(8,128)} %get-tuple-element.77), channel_id=1, source_target_pairs={{0,7},{1,6},{2,5},{3,4},{4,3},{5,2},{6,1},{7,0},{8,15},{9,14},{10,... | collective-permute-start | bytes 3932168 | tf_op jit(solution)/shard_map/ppermute | solution.py:395
  682.6 251.9 %collective-permute-start.29 = (f32[5,16,16,256]{3,2,1,0:T(8,128)}, f32[5,16,16,256]{3,2,1,0:T(8,128)}, u32[]{:S(2)}, u32[]{:S(2)}) collective-permute-start(f32[5,16,16,256]{3,2,1,0:T(8,128)} %get-tuple-element.79), channel_id=1, source_target_pairs={{0,6},{1,7},{2,4},{3,5},{4,2},{5,3},{6,0},{7,1},{8,14},{9,15},{10,... | collective-permute-start | bytes 3932168 | tf_op jit(solution)/shard_map/ppermute | solution.py:395
  766.0 195.7 %collective-permute-start.31 = (f32[5,16,16,256]{3,2,1,0:T(8,128)}, f32[5,16,16,256]{3,2,1,0:T(8,128)}, u32[]{:S(2)}, u32[]{:S(2)}) collective-permute-start(f32[5,16,16,256]{3,2,1,0:T(8,128)} %after.13), channel_id=1, source_target_pairs={{0,5},{1,4},{2,7},{3,6},{4,1},{5,0},{6,3},{7,2},{8,13},{9,12},{10,... | collective-permute-start | bytes 3932168 | tf_op jit(solution)/shard_map/ppermute | solution.py:395
  822.2 166.7 %collective-permute-start.19 = (f32[5,16,16,256]{3,2,1,0:T(8,128)}, f32[5,16,16,256]{3,2,1,0:T(8,128)}, u32[]{:S(2)}, u32[]{:S(2)}) collective-permute-start(f32[5,16,16,256]{3,2,1,0:T(8,128)} %get-tuple-element.71), channel_id=1, source_target_pairs={{0,4},{1,5},{2,6},{3,7},{4,0},{5,1},{6,2},{7,3},{8,12},{9,13},{10,... | collective-permute-start | bytes 3932168 | tf_op jit(solution)/shard_map/ppermute | solution.py:395
  877.3 114.6 %collective-permute-start.14 = (f32[5,16,16,256]{3,2,1,0:T(8,128)}, f32[5,16,16,256]{3,2,1,0:T(8,128)}, u32[]{:S(2)}, u32[]{:S(2)}) collective-permute-start(f32[5,16,16,256]{3,2,1,0:T(8,128)} %after.8), channel_id=1, source_target_pairs={{0,1},{1,0},{2,3},{3,2},{4,5},{5,4},{6,7},{7,6},{8,9},{9,8},{10,11... | collective-permute-start | bytes 3932168 | tf_op jit(solution)/shard_map/ppermute | solution.py:395
  906.4 85.9 %collective-permute-start.16 = (f32[5,16,16,256]{3,2,1,0:T(8,128)}, f32[5,16,16,256]{3,2,1,0:T(8,128)}, u32[]{:S(2)}, u32[]{:S(2)}) collective-permute-start(f32[5,16,16,256]{3,2,1,0:T(8,128)} %after.9), channel_id=1, source_target_pairs={{0,2},{1,3},{2,0},{3,1},{4,6},{5,7},{6,4},{7,5},{8,10},{9,11},{10,... | collective-permute-start | bytes 3932168 | tf_op jit(solution)/shard_map/ppermute | solution.py:395
  934.5 112.7 %collective-permute-start.18 = (f32[5,16,16,256]{3,2,1,0:T(8,128)}, f32[5,16,16,256]{3,2,1,0:T(8,128)}, u32[]{:S(2)}, u32[]{:S(2)}) collective-permute-start(f32[5,16,16,256]{3,2,1,0:T(8,128)} %after.10), channel_id=1, source_target_pairs={{0,3},{1,2},{2,1},{3,0},{4,7},{5,6},{6,5},{7,4},{8,11},{9,10},{10,... | collective-permute-start | bytes 3932168 | tf_op jit(solution)/shard_map/ppermute | solution.py:395
  961.7 103.5 %collective-permute-start.28 = (f32[5,16,16,256]{3,2,1,0:T(8,128)}, f32[5,16,16,256]{3,2,1,0:T(8,128)}, u32[]{:S(2)}, u32[]{:S(2)}) collective-permute-start(f32[5,16,16,256]{3,2,1,0:T(8,128)} %after.11), channel_id=1, source_target_pairs={{0,1},{1,0},{2,3},{3,2},{4,5},{5,4},{6,7},{7,6},{8,9},{9,8},{10,11... | collective-permute-start | bytes 3932168 | tf_op jit(solution)/shard_map/ppermute | solution.py:395
  988.9 86.4 %collective-permute-start.30 = (f32[5,16,16,256]{3,2,1,0:T(8,128)}, f32[5,16,16,256]{3,2,1,0:T(8,128)}, u32[]{:S(2)}, u32[]{:S(2)}) collective-permute-start(f32[5,16,16,256]{3,2,1,0:T(8,128)} %after.12), channel_id=1, source_target_pairs={{0,2},{1,3},{2,0},{3,1},{4,6},{5,7},{6,4},{7,5},{8,10},{9,11},{10,... | collective-permute-start | bytes 3932168 | tf_op jit(solution)/shard_map/ppermute | solution.py:395
  991.9 111.4 %collective-permute-start.32 = (f32[5,16,16,256]{3,2,1,0:T(8,128)}, f32[5,16,16,256]{3,2,1,0:T(8,128)}, u32[]{:S(2)}, u32[]{:S(2)}) collective-permute-start(f32[5,16,16,256]{3,2,1,0:T(8,128)} %after.14), channel_id=1, source_target_pairs={{0,3},{1,2},{2,1},{3,0},{4,7},{5,6},{6,5},{7,4},{8,11},{9,10},{10,... | collective-permute-start | bytes 3932168 | tf_op jit(solution)/shard_map/ppermute | solution.py:395
  992.3 125.9 %collective-permute-start.33 = (f32[5,16,16,256]{3,2,1,0:T(8,128)}, f32[5,16,16,256]{3,2,1,0:T(8,128)}, u32[]{:S(2)}, u32[]{:S(2)}) collective-permute-start(f32[5,16,16,256]{3,2,1,0:T(8,128)} %after.15), channel_id=1, source_target_pairs={{0,4},{1,5},{2,6},{3,7},{4,0},{5,1},{6,2},{7,3},{8,12},{9,13},{10,... | collective-permute-start | bytes 3932168 | tf_op jit(solution)/shard_map/ppermute | solution.py:395

commit v5 on v4

--- a/solution.py
+++ b/solution.py
@@ -447,7 +447,8 @@
         near_out = sender.send_near(pack(c), near, 1, c * count + NEAR)
         span_out.append(ordered({0: pack(c)(0, ()), **far_out, **near_out}))
         if c == 0:
-            wall_out = wall_exchange(pack_wall(wall_to, density, momentum, energy), 1)
+            begun = [far_out[far[0]]]
+            wall_out = wall_exchange(pack_wall(wall_to, density, momentum, energy, begun), 1)
 
     identity = jnp.eye(nz, dtype=jnp.float32)
     fourth = 6.0 * identity
@@ -498,13 +499,12 @@
 
     for c in range(1, chunks):
         pieces, make = back(c)
-        far_back = sender.send_far(make, far[:-2], -1)
-        far_back |= sender.send_far(make, far[-2:], -1, [mark])
-        fields, mark = add(c - 1, [0, *near, *far])
-        near_back = sender.send_near(make, near, -1, (chunks + c) * count + NEAR - 0)
+        far_back = sender.send_far(make, far, -1)
+        near_back = sender.send_near(make, near, -1, (chunks + c) * count + NEAR)
         span_back.append(ordered({0: pieces[0], **far_back, **near_back}))
     last = chunks - 1
-    groups = [(last, [0, *near]), (last, far[: count // 2]), (last, far[count // 2 :])]
+    groups = [(c, [0, *near, *far]) for c in range(last)]
+    groups += [(last, [0, *near]), (last, far[: count // 2]), (last, far[count // 2 :])]
     for c, group in groups:
         if group:
             fields, _ = add(c, group)

time: 1130 us -> 1070 us (0.947)
  starting transfers between devices: 124 us -> 35.8 us
  waiting for transfers between devices: 737 us -> 770 us
    ppermute x34, starting transfers between devices: 124 us -> 35.8 us  [permute(): return lax.ppermute(piece, self.axis, pairs)]
    ppermute x34, waiting for transfers between devices: 737 us -> 770 us  [permute(): return lax.ppermute(piece, self.axis, pairs)]
  transfers between devices with their start and end apart: 34 -> 34, of which waited for: 18 -> 18; matrix products, arithmetic and copies ran while one was open for 2% -> 2% of each run, Pallas kernels for 19% -> 22%
where the time goes in v5:
time: 1070 us
  waiting for transfers between devices  770 us (72%)
  Pallas kernels  243 us (23%)
  starting transfers between devices  35.8 us (3%)
    ppermute x34, waiting for transfers between devices, permute(): return lax.ppermute(piece, self.axis, pairs)  770 us
    pallas_call x26, Pallas kernels, call(): pl.pallas_call(body, name=name, grid_spec=pltpu.PrefetchScalarGridSpec(nu...  243 us
    ppermute x34, starting transfers between devices, permute(): return lax.ppermute(piece, self.axis, pairs)  35.8 us
  transfers between devices with their start and end apart: 34, of which 18 were waited for; matrix products, arithmetic and copies ran while one was open for 2% of the time, Pallas kernels for 22%

profile of v5, /device:TPU:15, one launch (start us, length us, event | category | flops | bytes accessed | tf_op | source)
XLA Modules:
  0.0 1066.3 jit_solution(16202483984513451284)
XLA Ops:
  0.6 2.2 pack_span_0.8
  4.7 2.2 pack_span_0.11
  7.1 2.2 pack_span_0.13
  9.3 4.1 collective-permute-start.10
  13.4 2.2 pack_span_0.15
  16.3 130.4 %collective-permute-done.refs_4_.refs_7_ = f32[5,16,16,256]{3,2,1,0:T(8,128)} collective-permute-done((f32[5,16,16,256]{3,2,1,0:T(8,128)}, f32[5,16,16,256]{3,2,1,0:T(8,128)}, u32[]{:S(2)}, u32[]{:S(2)}) %collective-permute-start) | collective-permute-done | bytes 1310752 | tf_op jit(solution)/shard_map/ppermute | solution.py:395
  146.8 20.8 %pack_wall.1 = (f32[5,4,256,256]{3,2,1,0:T(8,128)}, f32[5,4,256,256]{3,2,1,0:T(8,128)}, f32[5,4,256,256]{3,2,1,0:T(8,128)}, f32[5,4,256,256]{3,2,1,0:T(8,128)}) custom-call(s32[4]{0:T(128)} %pad_add_fusion.3.refs_0_.order, f32[4096,256]{1,0:T(8,128)} %bitcast.55, f32[3,4096,256]{2,1,0:T(8,128)} %bitcast.37, f32[4096,256]{1,0:T(8,128)} %bitcast.73, ...), custom_call_target="tpu_custom_call" | custom-call | bytes 41943040 | tf_op jit(solution)/shard_map/pack_wall/pallas_call | solution.py:80
  168.1 6.7 collective-permute-done.8.refs_4_.refs_6_
  177.2 2.3 pack_span_1.11
  179.5 2.2 pack_span_1.13
  181.8 20.3 %collective-permute-done.10.refs_4_.refs_5_ = f32[5,16,16,256]{3,2,1,0:T(8,128)} collective-permute-done((f32[5,16,16,256]{3,2,1,0:T(8,128)}, f32[5,16,16,256]{3,2,1,0:T(8,128)}, u32[]{:S(2)}, u32[]{:S(2)}) %collective-permute-start.10) | collective-permute-done | bytes 1310752 | tf_op jit(solution)/shard_map/ppermute | solution.py:395
  202.7 55.6 %collective-permute-done.12.refs_4_ = f32[5,16,16,256]{3,2,1,0:T(8,128)} collective-permute-done((f32[5,16,16,256]{3,2,1,0:T(8,128)}, f32[5,16,16,256]{3,2,1,0:T(8,128)}, u32[]{:S(2)}, u32[]{:S(2)}) %collective-permute-start.12) | collective-permute-done | bytes 1310752 | tf_op jit(solution)/shard_map/ppermute | solution.py:395
  258.9 2.2 pack_span_0.10
  261.2 54.4 %collective-permute-done.20.refs_4_.refs_7_ = f32[5,16,16,256]{3,2,1,0:T(8,128)} collective-permute-done((f32[5,16,16,256]{3,2,1,0:T(8,128)}, f32[5,16,16,256]{3,2,1,0:T(8,128)}, u32[]{:S(2)}, u32[]{:S(2)}) %collective-permute-start.20) | collective-permute-done | bytes 1310752 | tf_op jit(solution)/shard_map/ppermute | solution.py:395
  315.5 55.9 %collective-permute-done.22.refs_4_.refs_6_ = f32[5,16,16,256]{3,2,1,0:T(8,128)} collective-permute-done((f32[5,16,16,256]{3,2,1,0:T(8,128)}, f32[5,16,16,256]{3,2,1,0:T(8,128)}, u32[]{:S(2)}, u32[]{:S(2)}) %collective-permute-start.22) | collective-permute-done | bytes 1310752 | tf_op jit(solution)/shard_map/ppermute | solution.py:395
  374.3 2.2 pack_span_1.15
  382.8 2.3 pack_span_0.12
  385.1 2.2 pack_span_0.14
  387.3 11.5 %collective-permute-done.24.refs_4_.refs_5_ = f32[5,16,16,256]{3,2,1,0:T(8,128)} collective-permute-done((f32[5,16,16,256]{3,2,1,0:T(8,128)}, f32[5,16,16,256]{3,2,1,0:T(8,128)}, u32[]{:S(2)}, u32[]{:S(2)}) %collective-permute-start.24) | collective-permute-done | bytes 1310752 | tf_op jit(solution)/shard_map/ppermute | solution.py:395
  402.4 3.1 reduce-precision_convert_fusion
  405.5 2.5 pad_maximum_fusion.both
  408.0 2.2 pack_span_1.10
  410.2 2.3 pack_span_1.12
  412.5 2.3 pack_span_1.14
  414.8 15.1 %collective-permute-done.9.refs_2_ = f32[5,16,16,256]{3,2,1,0:T(8,128)} collective-permute-done((f32[5,16,16,256]{3,2,1,0:T(8,128)}, f32[5,16,16,256]{3,2,1,0:T(8,128)}, u32[]{:S(2)}, u32[]{:S(2)}) %collective-permute-start.9) | collective-permute-done | bytes 1310752 | tf_op jit(solution)/shard_map/ppermute | solution.py:395
  429.9 2.3 collective-permute-start.26
  432.1 50.7 %collective-permute-done.11.refs_3_ = f32[5,16,16,256]{3,2,1,0:T(8,128)} collective-permute-done((f32[5,16,16,256]{3,2,1,0:T(8,128)}, f32[5,16,16,256]{3,2,1,0:T(8,128)}, u32[]{:S(2)}, u32[]{:S(2)}) %collective-permute-start.11) | collective-permute-done | bytes 1310752 | tf_op jit(solution)/shard_map/ppermute | solution.py:395
  484.0 13.9 %span_terms_0.1 = (f32[5,16,16,256]{3,2,1,0:T(8,128)}, f32[5,16,16,256]{3,2,1,0:T(8,128)}, f32[5,16,16,256]{3,2,1,0:T(8,128)}, f32[5,16,16,256]{3,2,1,0:T(8,128)...) custom-call(f32[16]{0:T(128)} %get-tuple-element.104.weights, ...), custom_call_target="tpu_custom_call" | custom-call | flops 4026531840 | bytes 21233664 | tf_op jit(solution)/shard_map/span_terms_0/pallas_call | solution.py:80
  500.6 35.4 %wall_terms_0.1 = (f32[5,4,256,256]{3,2,1,0:T(8,128)}, f32[5,4,256,256]{3,2,1,0:T(8,128)}, f32[5,4,256,256]{3,2,1,0:T(8,128)}, f32[5,4,256,256]{3,2,1,0:T(8,128)}) custom-call(s32[4]{0:T(128)} %pad_add_fusion.3.refs_0_.order, bf16[2048,1024]{1,0:T(8,128)(2,1)} %pad_maximum_fusion.both, f32[1024,1]{1,0:T(8,128)} %copy.36.damping, ...), custom_call_target="tpu_custom_call" | custom-call | flops 16106127360 | bytes 50335744 | tf_op jit(solution)/shard_map/wall_terms_0/pallas_call | solution.py:80
  537.5 3.5 collective-permute-start.17
  541.0 35.5 %wall_terms_1.1 = (f32[5,4,256,256]{3,2,1,0:T(8,128)}, f32[5,4,256,256]{3,2,1,0:T(8,128)}, f32[5,4,256,256]{3,2,1,0:T(8,128)}, f32[5,4,256,256]{3,2,1,0:T(8,128)}) custom-call(s32[4]{0:T(128)} %pad_add_fusion.3.refs_0_.order, bf16[2048,1024]{1,0:T(8,128)(2,1)} %pad_maximum_fusion.both, ...), custom_call_target="tpu_custom_call", output_to_operand_aliasing={{0}: (7, {}), {1}: (8, {}), {2}: (9, {}), {3}: (10, {})} | custom-call | flops 16106127360 | bytes 71307264 | tf_op jit(solution)/shard_map/wall_terms_1/pallas_call | solution.py:80
  581.5 69.4 %collective-permute-done.15.refs_1_.refs_9_ = f32[5,16,16,256]{3,2,1,0:T(8,128)} collective-permute-done((f32[5,16,16,256]{3,2,1,0:T(8,128)}, f32[5,16,16,256]{3,2,1,0:T(8,128)}, u32[]{:S(2)}, u32[]{:S(2)}) %collective-permute-start.15) | collective-permute-done | bytes 1310752 | tf_op jit(solution)/shard_map/ppermute | solution.py:395
  650.9 13.8 %span_terms_1.1 = (f32[5,16,16,256]{3,2,1,0:T(8,128)}, f32[5,16,16,256]{3,2,1,0:T(8,128)}, f32[5,16,16,256]{3,2,1,0:T(8,128)}, f32[5,16,16,256]{3,2,1,0:T(8,128)...) custom-call(f32[16]{0:T(128)} %get-tuple-element.103.weights, ...), custom_call_target="tpu_custom_call" | custom-call | flops 4026531840 | bytes 21233664 | tf_op jit(solution)/shard_map/span_terms_1/pallas_call | solution.py:80
  664.7 41.6 %collective-permute-done.17.refs_1_.refs_10_ = f32[5,16,16,256]{3,2,1,0:T(8,128)} collective-permute-done((f32[5,16,16,256]{3,2,1,0:T(8,128)}, f32[5,16,16,256]{3,2,1,0:T(8,128)}, u32[]{:S(2)}, u32[]{:S(2)}) %collective-permute-start.17) | collective-permute-done | bytes 1310752 | tf_op jit(solution)/shard_map/ppermute | solution.py:395
  707.7 54.7 %collective-permute-done.19.refs_11_ = f32[5,16,16,256]{3,2,1,0:T(8,128)} collective-permute-done((f32[5,16,16,256]{3,2,1,0:T(8,128)}, f32[5,16,16,256]{3,2,1,0:T(8,128)}, u32[]{:S(2)}, u32[]{:S(2)}) %collective-permute-start.19) | collective-permute-done | bytes 1310752 | tf_op jit(solution)/shard_map/ppermute | solution.py:395
  762.5 57.7 %collective-permute-done.27.refs_1_.refs_4_ = f32[5,16,16,256]{3,2,1,0:T(8,128)} collective-permute-done((f32[5,16,16,256]{3,2,1,0:T(8,128)}, f32[5,16,16,256]{3,2,1,0:T(8,128)}, u32[]{:S(2)}, u32[]{:S(2)}) %collective-permute-start.27) | collective-permute-done | bytes 1310752 | tf_op jit(solution)/shard_map/ppermute | solution.py:395
  820.2 55.4 %collective-permute-done.29.refs_1_.refs_5_ = f32[5,16,16,256]{3,2,1,0:T(8,128)} collective-permute-done((f32[5,16,16,256]{3,2,1,0:T(8,128)}, f32[5,16,16,256]{3,2,1,0:T(8,128)}, u32[]{:S(2)}, u32[]{:S(2)}) %collective-permute-start.29) | collective-permute-done | bytes 1310752 | tf_op jit(solution)/shard_map/ppermute | solution.py:395
  877.1 25.8 %collective-permute-done.31.refs_1_.refs_4_ = f32[5,16,16,256]{3,2,1,0:T(8,128)} collective-permute-done((f32[5,16,16,256]{3,2,1,0:T(8,128)}, f32[5,16,16,256]{3,2,1,0:T(8,128)}, u32[]{:S(2)}, u32[]{:S(2)}) %collective-permute-start.31) | collective-permute-done | bytes 1310752 | tf_op jit(solution)/shard_map/ppermute | solution.py:395
  902.9 2.2 collective-permute-start.16
  905.5 28.7 %collective-permute-done.16.refs_6_ = f32[5,16,16,256]{3,2,1,0:T(8,128)} collective-permute-done((f32[5,16,16,256]{3,2,1,0:T(8,128)}, f32[5,16,16,256]{3,2,1,0:T(8,128)}, u32[]{:S(2)}, u32[]{:S(2)}) %collective-permute-start.16) | collective-permute-done | bytes 1310752 | tf_op jit(solution)/shard_map/ppermute | solution.py:395
  937.4 2.6 collective-permute-start.33
  942.4 49.4 %base_fields.1 = (f32[4096,256]{1,0:T(8,128)}, f32[3,4096,256]{2,1,0:T(8,128)}, f32[4096,256]{1,0:T(8,128)}, f32[8,128]{1,0:T(8,128)}) custom-call(s32[4]{0:T(128)} %pad_add_fusion.3.refs_0_.order, f32[4096,256]{1,0:T(8,128)} %bitcast.68, f32[3,4096,256]{2,1,0:T(8,128)} %bitcast.50, f32[4096,256]{1,0:T(8,128)} %bitcast.86, ...), custom_call_target="tpu_custom_call" | custom-call | bytes 62914560 | tf_op jit(solution)/shard_map/base_fields/pallas_call | solution.py:80
  991.8 18.0 %add_span_0.1 = (f32[8,32,16,256]{3,2,1,0:T(8,128)}, f32[3,8,32,16,256]{4,3,2,1,0:T(8,128)}, f32[8,32,16,256]{3,2,1,0:T(8,128)}, f32[8,128]{1,0:T(8,128)}) custom-call(s32[8]{0:T(128)} %concatenate.51.refs_0_, f32[8,32,16,256]{3,2,1,0:T(8,128)} %bitcast.89, ...), custom_call_target="tpu_custom_call", output_to_operand_aliasing={{0}: (1, {}), {1}: (2, {}), {2}: (3, {})} | custom-call | bytes 52428800 | tf_op jit(solution)/shard_map/add_span_0/pallas_call | solution.py:80
  1009.8 7.9 collective-permute-done.30.refs_6_
  1017.8 28.1 %collective-permute-done.32.refs_7_ = f32[5,16,16,256]{3,2,1,0:T(8,128)} collective-permute-done((f32[5,16,16,256]{3,2,1,0:T(8,128)}, f32[5,16,16,256]{3,2,1,0:T(8,128)}, u32[]{:S(2)}, u32[]{:S(2)}) %collective-permute-start.32) | collective-permute-done | bytes 1310752 | tf_op jit(solution)/shard_map/ppermute | solution.py:395
  1045.8 9.5 add_span_1.3
  1055.3 5.4 add_span_1.4
  1060.7 5.4 add_span_1.5
  (99 shorter events, 38.9 us)
Async XLA Ops:
  2.9 143.9 %collective-permute-start = (f32[5,16,16,256]{3,2,1,0:T(8,128)}, f32[5,16,16,256]{3,2,1,0:T(8,128)}, u32[]{:S(2)}, u32[]{:S(2)}) collective-permute-start(f32[5,16,16,256]{3,2,1,0:T(8,128)} %pack_span_0.8), channel_id=1, source_target_pairs={{0,7},{1,6},{2,5},{3,4},{4,3},{5,2},{6,1},{7,0},{8,15},{9,14},{10,... | collective-permute-start | bytes 3932168 | tf_op jit(solution)/shard_map/ppermute | solution.py:395
  6.9 167.9 %collective-permute-start.8 = (f32[5,16,16,256]{3,2,1,0:T(8,128)}, f32[5,16,16,256]{3,2,1,0:T(8,128)}, u32[]{:S(2)}, u32[]{:S(2)}) collective-permute-start(f32[5,16,16,256]{3,2,1,0:T(8,128)} %pack_span_0.11), channel_id=1, source_target_pairs={{0,6},{1,7},{2,4},{3,5},{4,2},{5,3},{6,0},{7,1},{8,14},{9,15},{10,... | collective-permute-start | bytes 3932168 | tf_op jit(solution)/shard_map/ppermute | solution.py:395
  9.3 192.8 %collective-permute-start.10 = (f32[5,16,16,256]{3,2,1,0:T(8,128)}, f32[5,16,16,256]{3,2,1,0:T(8,128)}, u32[]{:S(2)}, u32[]{:S(2)}) collective-permute-start(f32[5,16,16,256]{3,2,1,0:T(8,128)} %pack_span_0.13), channel_id=1, source_target_pairs={{0,5},{1,4},{2,7},{3,6},{4,1},{5,0},{6,3},{7,2},{8,13},{9,12},{10,... | collective-permute-start | bytes 3932168 | tf_op jit(solution)/shard_map/ppermute | solution.py:395
  15.6 242.7 %collective-permute-start.12 = (f32[5,16,16,256]{3,2,1,0:T(8,128)}, f32[5,16,16,256]{3,2,1,0:T(8,128)}, u32[]{:S(2)}, u32[]{:S(2)}) collective-permute-start(f32[5,16,16,256]{3,2,1,0:T(8,128)} %pack_span_0.15), channel_id=1, source_target_pairs={{0,4},{1,5},{2,6},{3,7},{4,0},{5,1},{6,2},{7,3},{8,12},{9,13},{10,... | collective-permute-start | bytes 3932168 | tf_op jit(solution)/shard_map/ppermute | solution.py:395
  167.5 330.4 %collective-permute-start.1 = (f32[5,4,256,256]{3,2,1,0:T(8,128)}, f32[5,4,256,256]{3,2,1,0:T(8,128)}, u32[]{:S(2)}, u32[]{:S(2)}) collective-permute-start(f32[5,4,256,256]{3,2,1,0:T(8,128)} %get-tuple-element.49), channel_id=1, source_target_pairs={{0,8},{8,0},{16,24},{24,16},{1,9},{9,1},{17,25},{25,17},{2,10},{10... | collective-permute-start | bytes 15728648 | tf_op jit(solution)/shard_map/ppermute | solution.py:395
  167.8 332.0 %collective-permute-start.2 = (f32[5,4,256,256]{3,2,1,0:T(8,128)}, f32[5,4,256,256]{3,2,1,0:T(8,128)}, u32[]{:S(2)}, u32[]{:S(2)}) collective-permute-start(f32[5,4,256,256]{3,2,1,0:T(8,128)} %get-tuple-element.50), channel_id=1, source_target_pairs={{0,16},{8,24},{16,0},{24,8},{1,17},{9,25},{17,1},{25,9},{2,18},{10... | collective-permute-start | bytes 15728648 | tf_op jit(solution)/shard_map/ppermute | solution.py:395
  174.8 325.4 %collective-permute-start.3 = (f32[5,4,256,256]{3,2,1,0:T(8,128)}, f32[5,4,256,256]{3,2,1,0:T(8,128)}, u32[]{:S(2)}, u32[]{:S(2)}) collective-permute-start(f32[5,4,256,256]{3,2,1,0:T(8,128)} %get-tuple-element.51), channel_id=1, source_target_pairs={{0,24},{8,16},{16,8},{24,0},{1,25},{9,17},{17,9},{25,1},{2,26},{10... | collective-permute-start | bytes 15728648 | tf_op jit(solution)/shard_map/ppermute | solution.py:395
  202.1 113.4 %collective-permute-start.20 = (f32[5,16,16,256]{3,2,1,0:T(8,128)}, f32[5,16,16,256]{3,2,1,0:T(8,128)}, u32[]{:S(2)}, u32[]{:S(2)}) collective-permute-start(f32[5,16,16,256]{3,2,1,0:T(8,128)} %pack_span_1.9), channel_id=1, source_target_pairs={{0,7},{1,6},{2,5},{3,4},{4,3},{5,2},{6,1},{7,0},{8,15},{9,14},{10,... | collective-permute-start | bytes 3932168 | tf_op jit(solution)/shard_map/ppermute | solution.py:395
  258.3 113.1 %collective-permute-start.22 = (f32[5,16,16,256]{3,2,1,0:T(8,128)}, f32[5,16,16,256]{3,2,1,0:T(8,128)}, u32[]{:S(2)}, u32[]{:S(2)}) collective-permute-start(f32[5,16,16,256]{3,2,1,0:T(8,128)} %pack_span_1.11), channel_id=1, source_target_pairs={{0,6},{1,7},{2,4},{3,5},{4,2},{5,3},{6,0},{7,1},{8,14},{9,15},{10,... | collective-permute-start | bytes 3932168 | tf_op jit(solution)/shard_map/ppermute | solution.py:395
  315.5 83.2 %collective-permute-start.24 = (f32[5,16,16,256]{3,2,1,0:T(8,128)}, f32[5,16,16,256]{3,2,1,0:T(8,128)}, u32[]{:S(2)}, u32[]{:S(2)}) collective-permute-start(f32[5,16,16,256]{3,2,1,0:T(8,128)} %pack_span_1.13), channel_id=1, source_target_pairs={{0,5},{1,4},{2,7},{3,6},{4,1},{5,0},{6,3},{7,2},{8,13},{9,12},{10,... | collective-permute-start | bytes 3932168 | tf_op jit(solution)/shard_map/ppermute | solution.py:395
  371.5 29.3 %collective-permute-start.7 = (f32[5,16,16,256]{3,2,1,0:T(8,128)}, f32[5,16,16,256]{3,2,1,0:T(8,128)}, u32[]{:S(2)}, u32[]{:S(2)}) collective-permute-start(f32[5,16,16,256]{3,2,1,0:T(8,128)} %pack_span_0.10), channel_id=1, source_target_pairs={{0,1},{1,0},{2,3},{3,2},{4,5},{5,4},{6,7},{7,6},{8,9},{9,8},{10,11... | collective-permute-start | bytes 3932168 | tf_op jit(solution)/shard_map/ppermute | solution.py:395
  374.3 2.2 copy-start.1
  377.6 0.8 copy-start
  398.8 31.1 %collective-permute-start.9 = (f32[5,16,16,256]{3,2,1,0:T(8,128)}, f32[5,16,16,256]{3,2,1,0:T(8,128)}, u32[]{:S(2)}, u32[]{:S(2)}) collective-permute-start(f32[5,16,16,256]{3,2,1,0:T(8,128)} %pack_span_0.12), channel_id=1, source_target_pairs={{0,2},{1,3},{2,0},{3,1},{4,6},{5,7},{6,4},{7,5},{8,10},{9,11},{10,... | collective-permute-start | bytes 3932168 | tf_op jit(solution)/shard_map/ppermute | solution.py:395
  400.7 82.1 %collective-permute-start.11 = (f32[5,16,16,256]{3,2,1,0:T(8,128)}, f32[5,16,16,256]{3,2,1,0:T(8,128)}, u32[]{:S(2)}, u32[]{:S(2)}) collective-permute-start(f32[5,16,16,256]{3,2,1,0:T(8,128)} %pack_span_0.14), channel_id=1, source_target_pairs={{0,3},{1,2},{2,1},{3,0},{4,7},{5,6},{6,5},{7,4},{8,11},{9,10},{10,... | collective-permute-start | bytes 3932168 | tf_op jit(solution)/shard_map/ppermute | solution.py:395
  429.9 106.1 %collective-permute-start.26 = (f32[5,16,16,256]{3,2,1,0:T(8,128)}, f32[5,16,16,256]{3,2,1,0:T(8,128)}, u32[]{:S(2)}, u32[]{:S(2)}) collective-permute-start(f32[5,16,16,256]{3,2,1,0:T(8,128)} %pack_span_1.15), channel_id=1, source_target_pairs={{0,4},{1,5},{2,6},{3,7},{4,0},{5,1},{6,2},{7,3},{8,12},{9,13},{10,... | collective-permute-start | bytes 3932168 | tf_op jit(solution)/shard_map/ppermute | solution.py:395
  482.8 54.7 %collective-permute-start.21 = (f32[5,16,16,256]{3,2,1,0:T(8,128)}, f32[5,16,16,256]{3,2,1,0:T(8,128)}, u32[]{:S(2)}, u32[]{:S(2)}) collective-permute-start(f32[5,16,16,256]{3,2,1,0:T(8,128)} %pack_span_1.10), channel_id=1, source_target_pairs={{0,1},{1,0},{2,3},{3,2},{4,5},{5,4},{6,7},{7,6},{8,9},{9,8},{10,11... | collective-permute-start | bytes 3932168 | tf_op jit(solution)/shard_map/ppermute | solution.py:395
  497.9 78.7 %collective-permute-start.23 = (f32[5,16,16,256]{3,2,1,0:T(8,128)}, f32[5,16,16,256]{3,2,1,0:T(8,128)}, u32[]{:S(2)}, u32[]{:S(2)}) collective-permute-start(f32[5,16,16,256]{3,2,1,0:T(8,128)} %pack_span_1.12), channel_id=1, source_target_pairs={{0,2},{1,3},{2,0},{3,1},{4,6},{5,7},{6,4},{7,5},{8,10},{9,11},{10,... | collective-permute-start | bytes 3932168 | tf_op jit(solution)/shard_map/ppermute | solution.py:395
  499.8 77.1 %collective-permute-start.25 = (f32[5,16,16,256]{3,2,1,0:T(8,128)}, f32[5,16,16,256]{3,2,1,0:T(8,128)}, u32[]{:S(2)}, u32[]{:S(2)}) collective-permute-start(f32[5,16,16,256]{3,2,1,0:T(8,128)} %pack_span_1.14), channel_id=1, source_target_pairs={{0,3},{1,2},{2,1},{3,0},{4,7},{5,6},{6,5},{7,4},{8,11},{9,10},{10,... | collective-permute-start | bytes 3932168 | tf_op jit(solution)/shard_map/ppermute | solution.py:395
  500.3 76.8 %collective-permute-start.13 = (f32[5,16,16,256]{3,2,1,0:T(8,128)}, f32[5,16,16,256]{3,2,1,0:T(8,128)}, u32[]{:S(2)}, u32[]{:S(2)}) collective-permute-start(f32[5,16,16,256]{3,2,1,0:T(8,128)} %get-tuple-element.65), channel_id=1, source_target_pairs={{0,7},{1,6},{2,5},{3,4},{4,3},{5,2},{6,1},{7,0},{8,15},{9,14},{10,... | collective-permute-start | bytes 3932168 | tf_op jit(solution)/shard_map/ppermute | solution.py:395
  536.0 114.9 %collective-permute-start.15 = (f32[5,16,16,256]{3,2,1,0:T(8,128)}, f32[5,16,16,256]{3,2,1,0:T(8,128)}, u32[]{:S(2)}, u32[]{:S(2)}) collective-permute-start(f32[5,16,16,256]{3,2,1,0:T(8,128)} %get-tuple-element.67), channel_id=1, source_target_pairs={{0,6},{1,7},{2,4},{3,5},{4,2},{5,3},{6,0},{7,1},{8,14},{9,15},{10,... | collective-permute-start | bytes 3932168 | tf_op jit(solution)/shard_map/ppermute | solution.py:395
  537.5 168.8 %collective-permute-start.17 = (f32[5,16,16,256]{3,2,1,0:T(8,128)}, f32[5,16,16,256]{3,2,1,0:T(8,128)}, u32[]{:S(2)}, u32[]{:S(2)}) collective-permute-start(f32[5,16,16,256]{3,2,1,0:T(8,128)} %get-tuple-element.69), channel_id=1, source_target_pairs={{0,5},{1,4},{2,7},{3,6},{4,1},{5,0},{6,3},{7,2},{8,13},{9,12},{10,... | collective-permute-start | bytes 3932168 | tf_op jit(solution)/shard_map/ppermute | solution.py:395
  576.6 359.2 %collective-permute-start.4 = (f32[5,4,256,256]{3,2,1,0:T(8,128)}, f32[5,4,256,256]{3,2,1,0:T(8,128)}, u32[]{:S(2)}, u32[]{:S(2)}) collective-permute-start(f32[5,4,256,256]{3,2,1,0:T(8,128)} %get-tuple-element.57), channel_id=1, source_target_pairs={{0,8},{8,0},{16,24},{24,16},{1,9},{9,1},{17,25},{25,17},{2,10},{10... | collective-permute-start | bytes 15728648 | tf_op jit(solution)/shard_map/ppermute | solution.py:395
  576.9 360.3 %collective-permute-start.5 = (f32[5,4,256,256]{3,2,1,0:T(8,128)}, f32[5,4,256,256]{3,2,1,0:T(8,128)}, u32[]{:S(2)}, u32[]{:S(2)}) collective-permute-start(f32[5,4,256,256]{3,2,1,0:T(8,128)} %get-tuple-element.58), channel_id=1, source_target_pairs={{0,16},{8,24},{16,0},{24,8},{1,17},{9,25},{17,1},{25,9},{2,18},{10... | collective-permute-start | bytes 15728648 | tf_op jit(solution)/shard_map/ppermute | solution.py:395
  577.1 360.3 %collective-permute-start.6 = (f32[5,4,256,256]{3,2,1,0:T(8,128)}, f32[5,4,256,256]{3,2,1,0:T(8,128)}, u32[]{:S(2)}, u32[]{:S(2)}) collective-permute-start(f32[5,4,256,256]{3,2,1,0:T(8,128)} %get-tuple-element.59), channel_id=1, source_target_pairs={{0,24},{8,16},{16,8},{24,0},{1,25},{9,17},{17,9},{25,1},{2,26},{10... | collective-permute-start | bytes 15728648 | tf_op jit(solution)/shard_map/ppermute | solution.py:395
  650.9 111.6 %collective-permute-start.19 = (f32[5,16,16,256]{3,2,1,0:T(8,128)}, f32[5,16,16,256]{3,2,1,0:T(8,128)}, u32[]{:S(2)}, u32[]{:S(2)}) collective-permute-start(f32[5,16,16,256]{3,2,1,0:T(8,128)} %get-tuple-element.70), channel_id=1, source_target_pairs={{0,4},{1,5},{2,6},{3,7},{4,0},{5,1},{6,2},{7,3},{8,12},{9,13},{10,... | collective-permute-start | bytes 3932168 | tf_op jit(solution)/shard_map/ppermute | solution.py:395
  706.3 113.9 %collective-permute-start.27 = (f32[5,16,16,256]{3,2,1,0:T(8,128)}, f32[5,16,16,256]{3,2,1,0:T(8,128)}, u32[]{:S(2)}, u32[]{:S(2)}) collective-permute-start(f32[5,16,16,256]{3,2,1,0:T(8,128)} %get-tuple-element.76), channel_id=1, source_target_pairs={{0,7},{1,6},{2,5},{3,4},{4,3},{5,2},{6,1},{7,0},{8,15},{9,14},{10,... | collective-permute-start | bytes 3932168 | tf_op jit(solution)/shard_map/ppermute | solution.py:395
  762.5 113.1 %collective-permute-start.29 = (f32[5,16,16,256]{3,2,1,0:T(8,128)}, f32[5,16,16,256]{3,2,1,0:T(8,128)}, u32[]{:S(2)}, u32[]{:S(2)}) collective-permute-start(f32[5,16,16,256]{3,2,1,0:T(8,128)} %get-tuple-element.78), channel_id=1, source_target_pairs={{0,6},{1,7},{2,4},{3,5},{4,2},{5,3},{6,0},{7,1},{8,14},{9,15},{10,... | collective-permute-start | bytes 3932168 | tf_op jit(solution)/shard_map/ppermute | solution.py:395
  820.2 82.7 %collective-permute-start.31 = (f32[5,16,16,256]{3,2,1,0:T(8,128)}, f32[5,16,16,256]{3,2,1,0:T(8,128)}, u32[]{:S(2)}, u32[]{:S(2)}) collective-permute-start(f32[5,16,16,256]{3,2,1,0:T(8,128)} %get-tuple-element.80), channel_id=1, source_target_pairs={{0,5},{1,4},{2,7},{3,6},{4,1},{5,0},{6,3},{7,2},{8,13},{9,12},{10,... | collective-permute-start | bytes 3932168 | tf_op jit(solution)/shard_map/ppermute | solution.py:395
  875.6 29.5 %collective-permute-start.14 = (f32[5,16,16,256]{3,2,1,0:T(8,128)}, f32[5,16,16,256]{3,2,1,0:T(8,128)}, u32[]{:S(2)}, u32[]{:S(2)}) collective-permute-start(f32[5,16,16,256]{3,2,1,0:T(8,128)} %after.6), channel_id=1, source_target_pairs={{0,1},{1,0},{2,3},{3,2},{4,5},{5,4},{6,7},{7,6},{8,9},{9,8},{10,11... | collective-permute-start | bytes 3932168 | tf_op jit(solution)/shard_map/ppermute | solution.py:395
  902.9 31.3 %collective-permute-start.16 = (f32[5,16,16,256]{3,2,1,0:T(8,128)}, f32[5,16,16,256]{3,2,1,0:T(8,128)}, u32[]{:S(2)}, u32[]{:S(2)}) collective-permute-start(f32[5,16,16,256]{3,2,1,0:T(8,128)} %after.7), channel_id=1, source_target_pairs={{0,2},{1,3},{2,0},{3,1},{4,6},{5,7},{6,4},{7,5},{8,10},{9,11},{10,... | collective-permute-start | bytes 3932168 | tf_op jit(solution)/shard_map/ppermute | solution.py:395
  905.1 86.6 %collective-permute-start.18 = (f32[5,16,16,256]{3,2,1,0:T(8,128)}, f32[5,16,16,256]{3,2,1,0:T(8,128)}, u32[]{:S(2)}, u32[]{:S(2)}) collective-permute-start(f32[5,16,16,256]{3,2,1,0:T(8,128)} %after.8), channel_id=1, source_target_pairs={{0,3},{1,2},{2,1},{3,0},{4,7},{5,6},{6,5},{7,4},{8,11},{9,10},{10,... | collective-permute-start | bytes 3932168 | tf_op jit(solution)/shard_map/ppermute | solution.py:395
  934.2 75.6 %collective-permute-start.28 = (f32[5,16,16,256]{3,2,1,0:T(8,128)}, f32[5,16,16,256]{3,2,1,0:T(8,128)}, u32[]{:S(2)}, u32[]{:S(2)}) collective-permute-start(f32[5,16,16,256]{3,2,1,0:T(8,128)} %after.9), channel_id=1, source_target_pairs={{0,1},{1,0},{2,3},{3,2},{4,5},{5,4},{6,7},{7,6},{8,9},{9,8},{10,11... | collective-permute-start | bytes 3932168 | tf_op jit(solution)/shard_map/ppermute | solution.py:395
  935.8 82.0 %collective-permute-start.30 = (f32[5,16,16,256]{3,2,1,0:T(8,128)}, f32[5,16,16,256]{3,2,1,0:T(8,128)}, u32[]{:S(2)}, u32[]{:S(2)}) collective-permute-start(f32[5,16,16,256]{3,2,1,0:T(8,128)} %after.10), channel_id=1, source_target_pairs={{0,2},{1,3},{2,0},{3,1},{4,6},{5,7},{6,4},{7,5},{8,10},{9,11},{10,... | collective-permute-start | bytes 3932168 | tf_op jit(solution)/shard_map/ppermute | solution.py:395
  937.2 108.6 %collective-permute-start.32 = (f32[5,16,16,256]{3,2,1,0:T(8,128)}, f32[5,16,16,256]{3,2,1,0:T(8,128)}, u32[]{:S(2)}, u32[]{:S(2)}) collective-permute-start(f32[5,16,16,256]{3,2,1,0:T(8,128)} %after.11), channel_id=1, source_target_pairs={{0,3},{1,2},{2,1},{3,0},{4,7},{5,6},{6,5},{7,4},{8,11},{9,10},{10,... | collective-permute-start | bytes 3932168 | tf_op jit(solution)/shard_map/ppermute | solution.py:395
  937.4 123.3 %collective-permute-start.33 = (f32[5,16,16,256]{3,2,1,0:T(8,128)}, f32[5,16,16,256]{3,2,1,0:T(8,128)}, u32[]{:S(2)}, u32[]{:S(2)}) collective-permute-start(f32[5,16,16,256]{3,2,1,0:T(8,128)} %get-tuple-element.87), channel_id=1, source_target_pairs={{0,4},{1,5},{2,6},{3,7},{4,0},{5,1},{6,2},{7,3},{8,12},{9,13},{10,... | collective-permute-start | bytes 3932168 | tf_op jit(solution)/shard_map/ppermute | solution.py:395

commit v6 on v1

--- a/solution.py
+++ b/solution.py
@@ -180,7 +180,7 @@
     kept, flux_high, flux_low = refs[2 * m :]
     jl, nx = pieces[0].shape[2:]
     ny = m * jl
-    step = divisor_up_to(jl, 32)
+    step = divisor_up_to(jl, 64)
     for f in range(5):
         kept[f, 0:8] = jnp.zeros((8, nx), jnp.float32)
         kept[f, 8 + ny : 16 + ny] = jnp.zeros((8, nx), jnp.float32)
@@ -203,7 +203,7 @@
         def _(f):
             total = dot(high[rows, :], flux_high[f]) + dot(low[rows, :], flux_high[f])
             outs[k][f, 0] = total + dot(high[rows, :], flux_low[f])
-            part = divisor_up_to(jl, 64)
+            part = divisor_up_to(jl, 128)
 
             @pl.loop(0, jl // part)
             def _(i):
@@ -256,7 +256,7 @@
                 lanes = slice(half * lane, (half + 1) * lane)
                 for f in range(5):
                     wall[half, f, lines, :] = piece[f, z, :, lanes]
-    part = 16
+    part = divisor_up_to(rows * zl, 64)
 
     @pl.loop(0, rows * zl // part)
     def _(i):

time: 1010 us -> 1000 us (0.990)
  Pallas kernels: 246 us -> 220 us
  waiting for transfers between devices: 705 us -> 723 us
    pallas_call x9, Pallas kernels: 246 us -> 220 us  [call(): pl.pallas_call(body, name=name, grid_spec=pltpu.PrefetchScalarGridSpec(nu...]
    ppermute x34, waiting for transfers between devices: 705 us -> 723 us  [exchange(): out[k] = lax.ppermute(pieces[k], axis, pairs)]
  transfers between devices with their start and end apart: 34 -> 34, of which waited for: 17 -> 19; matrix products, arithmetic and copies ran while one was open for 1% -> 1% of each run, Pallas kernels for 22% -> 20%
where the time goes in v6:
time: 1000 us
  waiting for transfers between devices  723 us (72%)
  Pallas kernels  220 us (22%)
  starting transfers between devices  41.5 us (4%)
    ppermute x34, waiting for transfers between devices, exchange(): out[k] = lax.ppermute(pieces[k], axis, pairs)  723 us
    pallas_call x9, Pallas kernels, call(): pl.pallas_call(body, name=name, grid_spec=pltpu.PrefetchScalarGridSpec(nu...  220 us
    ppermute x34, starting transfers between devices, exchange(): out[k] = lax.ppermute(pieces[k], axis, pairs)  41.5 us
  transfers between devices with their start and end apart: 34, of which 19 were waited for; matrix products, arithmetic and copies ran while one was open for 1% of the time, Pallas kernels for 20%

profile of v6, /device:TPU:15, one launch (start us, length us, event | category | flops | bytes accessed | tf_op | source)
XLA Modules:
  0.0 1001.8 jit_solution(5586705122835674642)
XLA Ops:
  1.3 10.6 %pack_span_0.1 = (f32[5,16,16,256]{3,2,1,0:T(8,128)}, f32[5,16,16,256]{3,2,1,0:T(8,128)}, f32[5,16,16,256]{3,2,1,0:T(8,128)}, f32[5,16,16,256]{3,2,1,0:T(8,128)}...) custom-call(s32[8]{0:T(128)} %stack.64.order, ...), custom_call_target="tpu_custom_call" | custom-call | bytes 31457280 | tf_op jit(solution)/shard_map/pack_span_0/pallas_call | solution.py:59
  12.8 1.5 collective-permute-start.8
  14.4 2.3 collective-permute-start.9
  17.1 1.3 collective-permute-start.11
  19.0 20.8 %pack_wall.1 = (f32[5,4,256,256]{3,2,1,0:T(8,128)}, f32[5,4,256,256]{3,2,1,0:T(8,128)}, f32[5,4,256,256]{3,2,1,0:T(8,128)}, f32[5,4,256,256]{3,2,1,0:T(8,128)}) custom-call(s32[4]{0:T(128)} %pad_add_fusion.order, f32[4096,256]{1,0:T(8,128)} %bitcast.38, f32[3,4096,256]{2,1,0:T(8,128)} %bitcast.34, f32[4096,256]{1,0:T(8,128)} %bitcast.42), custom_call_target="tpu_custom_call" | custom-call | bytes 41943040 | tf_op jit(solution)/shard_map/pack_wall/pallas_call | solution.py:59
  39.8 57.2 %collective-permute-done.7.refs_2_ = f32[5,16,16,256]{3,2,1,0:T(8,128)S(1)} collective-permute-done((f32[5,16,16,256]{3,2,1,0:T(8,128)}, f32[5,16,16,256]{3,2,1,0:T(8,128)S(1)}, u32[]{:S(2)}, u32[]{:S(2)}) %collective-permute-start.7) | collective-permute-done | bytes 1310752 | tf_op jit(solution)/shard_map/ppermute | solution.py:342
  97.2 27.8 %collective-permute-done.8.refs_3_ = f32[5,16,16,256]{3,2,1,0:T(8,128)S(1)} collective-permute-done((f32[5,16,16,256]{3,2,1,0:T(8,128)}, f32[5,16,16,256]{3,2,1,0:T(8,128)S(1)}, u32[]{:S(2)}, u32[]{:S(2)}) %collective-permute-start.8) | collective-permute-done | bytes 1310752 | tf_op jit(solution)/shard_map/ppermute | solution.py:342
  125.2 1.2 collective-permute-start.2
  126.5 10.6 %pack_span_1.1 = (f32[5,16,16,256]{3,2,1,0:T(8,128)}, f32[5,16,16,256]{3,2,1,0:T(8,128)}, f32[5,16,16,256]{3,2,1,0:T(8,128)}, f32[5,16,16,256]{3,2,1,0:T(8,128)}...) custom-call(s32[8]{0:T(128)} %stack.64.order, ...), custom_call_target="tpu_custom_call" | custom-call | bytes 31457280 | tf_op jit(solution)/shard_map/pack_span_1/pallas_call | solution.py:59
  137.1 20.3 %collective-permute-done.10.refs_5_ = f32[5,16,16,256]{3,2,1,0:T(8,128)} collective-permute-done((f32[5,16,16,256]{3,2,1,0:T(8,128)}, f32[5,16,16,256]{3,2,1,0:T(8,128)}, u32[]{:S(2)}, u32[]{:S(2)}) %collective-permute-start.10) | collective-permute-done | bytes 1310752 | tf_op jit(solution)/shard_map/ppermute | solution.py:342
  157.9 55.7 %collective-permute-done.11.refs_6_ = f32[5,16,16,256]{3,2,1,0:T(8,128)} collective-permute-done((f32[5,16,16,256]{3,2,1,0:T(8,128)}, f32[5,16,16,256]{3,2,1,0:T(8,128)}, u32[]{:S(2)}, u32[]{:S(2)}) %collective-permute-start.11) | collective-permute-done | bytes 1310752 | tf_op jit(solution)/shard_map/ppermute | solution.py:342
  213.6 1.5 collective-permute-start.20
  215.7 26.3 %collective-permute-done.12.refs_7_ = f32[5,16,16,256]{3,2,1,0:T(8,128)S(1)} collective-permute-done((f32[5,16,16,256]{3,2,1,0:T(8,128)S(1)}, f32[5,16,16,256]{3,2,1,0:T(8,128)S(1)}, u32[]{:S(2)}, u32[]{:S(2)}) %collective-permute-start.12) | collective-permute-done | bytes 1310752 | tf_op jit(solution)/shard_map/ppermute | solution.py:342
  242.0 1.1 copy-done.8
  243.2 2.1 collective-permute-start.22
  249.9 22.3 %collective-permute-done.21.refs_2_ = f32[5,16,16,256]{3,2,1,0:T(8,128)} collective-permute-done((f32[5,16,16,256]{3,2,1,0:T(8,128)}, f32[5,16,16,256]{3,2,1,0:T(8,128)}, u32[]{:S(2)}, u32[]{:S(2)}) %collective-permute-start.21) | collective-permute-done | bytes 1310752 | tf_op jit(solution)/shard_map/ppermute | solution.py:342
  272.2 3.1 collective-permute-start.23
  275.3 49.6 %collective-permute-done.22.refs_3_ = f32[5,16,16,256]{3,2,1,0:T(8,128)} collective-permute-done((f32[5,16,16,256]{3,2,1,0:T(8,128)}, f32[5,16,16,256]{3,2,1,0:T(8,128)}, u32[]{:S(2)}, u32[]{:S(2)}) %collective-permute-start.22) | collective-permute-done | bytes 1310752 | tf_op jit(solution)/shard_map/ppermute | solution.py:342
  324.9 2.9 collective-permute-start.24
  330.6 5.1 fusion
  335.8 14.1 %span_terms_0.1 = (f32[5,16,16,256]{3,2,1,0:T(8,128)}, f32[5,16,16,256]{3,2,1,0:T(8,128)}, f32[5,16,16,256]{3,2,1,0:T(8,128)}, f32[5,16,16,256]{3,2,1,0:T(8,128)...) custom-call(f32[16]{0:T(128)} %get-tuple-element.116.weights, ...), custom_call_target="tpu_custom_call" | custom-call | flops 4026531840 | bytes 21233664 | tf_op jit(solution)/shard_map/span_terms_0/pallas_call | solution.py:59
  349.8 10.0 collective-permute-done.23.refs_4_
  359.8 56.1 %collective-permute-done.24.refs_5_ = f32[5,16,16,256]{3,2,1,0:T(8,128)} collective-permute-done((f32[5,16,16,256]{3,2,1,0:T(8,128)S(1)}, f32[5,16,16,256]{3,2,1,0:T(8,128)}, u32[]{:S(2)}, u32[]{:S(2)}) %collective-permute-start.24) | collective-permute-done | bytes 1310752 | tf_op jit(solution)/shard_map/ppermute | solution.py:342
  415.9 1.9 collective-permute-start.26
  417.8 3.8 collective-permute-start.14
  421.6 74.1 %wall_terms.1 = (f32[5,4,256,256]{3,2,1,0:T(8,128)}, f32[5,4,256,256]{3,2,1,0:T(8,128)}, f32[5,4,256,256]{3,2,1,0:T(8,128)}, f32[5,4,256,256]{3,2,1,0:T(8,128)}) custom-call(s32[4]{0:T(128)} %pad_add_fusion.order, bf16[1024,1024]{1,0:T(8,128)(2,1)} %get-tuple-element.104.high, bf16[1024,1024]{1,0:T(8,128)(2,1)} %get-tuple-element.103.low, ...), custom_call_target="tpu_custom_call" | custom-call | flops 32212254720 | bytes 50335744 | tf_op jit(solution)/shard_map/wall_terms/pallas_call | solution.py:59
  495.8 1.0 copy-done.15
  497.1 4.6 collective-permute-done.26.refs_7_
  501.9 1.2 collective-permute-start.5
  503.2 3.3 collective-permute-done.15.refs_3_
  506.5 4.6 collective-permute-start.17
  511.1 76.9 %collective-permute-done.16.refs_4_ = f32[5,16,16,256]{3,2,1,0:T(8,128)} collective-permute-done((f32[5,16,16,256]{3,2,1,0:T(8,128)}, f32[5,16,16,256]{3,2,1,0:T(8,128)}, u32[]{:S(2)}, u32[]{:S(2)}) %collective-permute-start.16) | collective-permute-done | bytes 1310752 | tf_op jit(solution)/shard_map/ppermute | solution.py:342
  588.0 1.1 collective-permute-start.18
  589.1 55.0 %collective-permute-done.17.refs_5_ = f32[5,16,16,256]{3,2,1,0:T(8,128)} collective-permute-done((f32[5,16,16,256]{3,2,1,0:T(8,128)}, f32[5,16,16,256]{3,2,1,0:T(8,128)}, u32[]{:S(2)}, u32[]{:S(2)}) %collective-permute-start.17) | collective-permute-done | bytes 1310752 | tf_op jit(solution)/shard_map/ppermute | solution.py:342
  644.2 2.3 collective-permute-start.19
  646.5 13.8 %span_terms_1.1 = (f32[5,16,16,256]{3,2,1,0:T(8,128)}, f32[5,16,16,256]{3,2,1,0:T(8,128)}, f32[5,16,16,256]{3,2,1,0:T(8,128)}, f32[5,16,16,256]{3,2,1,0:T(8,128)...) custom-call(f32[16]{0:T(128)} %get-tuple-element.115.weights, ...), custom_call_target="tpu_custom_call" | custom-call | flops 4026531840 | bytes 21233664 | tf_op jit(solution)/shard_map/span_terms_1/pallas_call | solution.py:59
  660.3 41.9 %collective-permute-done.18.refs_6_ = f32[5,16,16,256]{3,2,1,0:T(8,128)} collective-permute-done((f32[5,16,16,256]{3,2,1,0:T(8,128)}, f32[5,16,16,256]{3,2,1,0:T(8,128)}, u32[]{:S(2)}, u32[]{:S(2)}) %collective-permute-start.18) | collective-permute-done | bytes 1310752 | tf_op jit(solution)/shard_map/ppermute | solution.py:342
  702.2 1.3 collective-permute-start.27
  703.6 26.9 %collective-permute-done.19.refs_7_ = f32[5,16,16,256]{3,2,1,0:T(8,128)} collective-permute-done((f32[5,16,16,256]{3,2,1,0:T(8,128)}, f32[5,16,16,256]{3,2,1,0:T(8,128)}, u32[]{:S(2)}, u32[]{:S(2)}) %collective-permute-start.19) | collective-permute-done | bytes 1310752 | tf_op jit(solution)/shard_map/ppermute | solution.py:342
  730.5 1.9 collective-permute-start.29
  732.4 28.5 %collective-permute-done.28.refs_2_ = f32[5,16,16,256]{3,2,1,0:T(8,128)S(1)} collective-permute-done((f32[5,16,16,256]{3,2,1,0:T(8,128)}, f32[5,16,16,256]{3,2,1,0:T(8,128)S(1)}, u32[]{:S(2)}, u32[]{:S(2)}) %collective-permute-start.28) | collective-permute-done | bytes 1310752 | tf_op jit(solution)/shard_map/ppermute | solution.py:342
  761.2 3.9 collective-permute-start.31
  765.4 49.4 %base_fields.1 = (f32[4096,256]{1,0:T(8,128)}, f32[3,4096,256]{2,1,0:T(8,128)}, f32[4096,256]{1,0:T(8,128)}) custom-call(s32[4]{0:T(128)} %pad_add_fusion.order, f32[4096,256]{1,0:T(8,128)} %bitcast.40, f32[3,4096,256]{2,1,0:T(8,128)} %bitcast.36, f32[4096,256]{1,0:T(8,128)} %bitcast.44, f32[5,4,256,256]{3,2,1,0:T(8,128)} %get-tuple-element.58.refs_0_, ...), custom_call_target="tpu_custom_call" | custom-call | bytes 62914560 | tf_op jit(solution)/shard_map/base_fields/pallas_call | solution.py:59
  814.8 13.3 %add_span_0.1 = (f32[8,32,16,256]{3,2,1,0:T(8,128)}, f32[3,8,32,16,256]{4,3,2,1,0:T(8,128)}, f32[8,32,16,256]{3,2,1,0:T(8,128)}) custom-call(s32[8]{0:T(128)} %stack.64.order, f32[8,32,16,256]{3,2,1,0:T(8,128)} %bitcast.47, f32[3,8,32,16,256]{4,3,2,1,0:T(8,128)} %bitcast.45, ...), custom_call_target="tpu_custom_call", output_to_operand_aliasing={{0}: (1, {}), {1}: (2, {}), {2}: (3, {})} | custom-call | bytes 52428800 | tf_op jit(solution)/shard_map/add_span_0/pallas_call | solution.py:59
  828.2 100.9 %collective-permute-done.31.refs_5_ = f32[5,16,16,256]{3,2,1,0:T(8,128)} collective-permute-done((f32[5,16,16,256]{3,2,1,0:T(8,128)}, f32[5,16,16,256]{3,2,1,0:T(8,128)}, u32[]{:S(2)}, u32[]{:S(2)}) %collective-permute-start.31) | collective-permute-done | bytes 1310752 | tf_op jit(solution)/shard_map/ppermute | solution.py:342
  929.0 30.1 %collective-permute-done.32.refs_6_ = f32[5,16,16,256]{3,2,1,0:T(8,128)} collective-permute-done((f32[5,16,16,256]{3,2,1,0:T(8,128)}, f32[5,16,16,256]{3,2,1,0:T(8,128)}, u32[]{:S(2)}, u32[]{:S(2)}) %collective-permute-start.32) | collective-permute-done | bytes 1310752 | tf_op jit(solution)/shard_map/ppermute | solution.py:342
  959.1 29.3 %collective-permute-done.33.refs_7_ = f32[5,16,16,256]{3,2,1,0:T(8,128)} collective-permute-done((f32[5,16,16,256]{3,2,1,0:T(8,128)}, f32[5,16,16,256]{3,2,1,0:T(8,128)}, u32[]{:S(2)}, u32[]{:S(2)}) %collective-permute-start.33) | collective-permute-done | bytes 1310752 | tf_op jit(solution)/shard_map/ppermute | solution.py:342
  988.4 13.3 %add_span_1.1 = (f32[8,32,16,256]{3,2,1,0:T(8,128)}, f32[3,8,32,16,256]{4,3,2,1,0:T(8,128)}, f32[8,32,16,256]{3,2,1,0:T(8,128)}) custom-call(s32[8]{0:T(128)} %stack.64.order, f32[8,32,16,256]{3,2,1,0:T(8,128)} %get-tuple-element.81.density, ...), custom_call_target="tpu_custom_call", output_to_operand_aliasing={{0}: (1, {}), {1}: (2, {}), {2}: (3, {})} | custom-call | bytes 52428800 | tf_op jit(solution)/shard_map/add_span_1/pallas_call | solution.py:59
  (99 shorter events, 12.7 us)
Async XLA Ops:
  11.9 5.1 collective-permute-start.6
  12.7 84.3 %collective-permute-start.7 = (f32[5,16,16,256]{3,2,1,0:T(8,128)}, f32[5,16,16,256]{3,2,1,0:T(8,128)S(1)}, u32[]{:S(2)}, u32[]{:S(2)}) collective-permute-start(f32[5,16,16,256]{3,2,1,0:T(8,128)} %get-tuple-element.67), channel_id=1, source_target_pairs={{0,2},{1,3},{2,0},{3,1},{4,6},{5,7},{6,4},{7,5},{8,10},{9,11},{10,... | collective-permute-start | bytes 3932168 | tf_op jit(solution)/shard_map/ppermute | solution.py:342
  12.8 112.2 %collective-permute-start.8 = (f32[5,16,16,256]{3,2,1,0:T(8,128)}, f32[5,16,16,256]{3,2,1,0:T(8,128)S(1)}, u32[]{:S(2)}, u32[]{:S(2)}) collective-permute-start(f32[5,16,16,256]{3,2,1,0:T(8,128)} %get-tuple-element.68), channel_id=1, source_target_pairs={{0,3},{1,2},{2,1},{3,0},{4,7},{5,6},{6,5},{7,4},{8,11},{9,10},{10,... | collective-permute-start | bytes 3932168 | tf_op jit(solution)/shard_map/ppermute | solution.py:342
  14.4 110.9 %collective-permute-start.9 = (f32[5,16,16,256]{3,2,1,0:T(8,128)}, f32[5,16,16,256]{3,2,1,0:T(8,128)}, u32[]{:S(2)}, u32[]{:S(2)}) collective-permute-start(f32[5,16,16,256]{3,2,1,0:T(8,128)} %get-tuple-element.69), channel_id=1, source_target_pairs={{0,4},{1,5},{2,6},{3,7},{4,0},{5,1},{6,2},{7,3},{8,12},{9,13},{10,... | collective-permute-start | bytes 3932168 | tf_op jit(solution)/shard_map/ppermute | solution.py:342
  16.7 140.7 %collective-permute-start.10 = (f32[5,16,16,256]{3,2,1,0:T(8,128)}, f32[5,16,16,256]{3,2,1,0:T(8,128)}, u32[]{:S(2)}, u32[]{:S(2)}) collective-permute-start(f32[5,16,16,256]{3,2,1,0:T(8,128)} %get-tuple-element.70), channel_id=1, source_target_pairs={{0,5},{1,4},{2,7},{3,6},{4,1},{5,0},{6,3},{7,2},{8,13},{9,12},{10,... | collective-permute-start | bytes 3932168 | tf_op jit(solution)/shard_map/ppermute | solution.py:342
  17.1 196.5 %collective-permute-start.11 = (f32[5,16,16,256]{3,2,1,0:T(8,128)}, f32[5,16,16,256]{3,2,1,0:T(8,128)}, u32[]{:S(2)}, u32[]{:S(2)}) collective-permute-start(f32[5,16,16,256]{3,2,1,0:T(8,128)} %get-tuple-element.71), channel_id=1, source_target_pairs={{0,6},{1,7},{2,4},{3,5},{4,2},{5,3},{6,0},{7,1},{8,14},{9,15},{10,... | collective-permute-start | bytes 3932168 | tf_op jit(solution)/shard_map/ppermute | solution.py:342
  96.9 29.5 %copy-start.9 = (f32[5,16,16,256]{3,2,1,0:T(8,128)}, f32[5,16,16,256]{3,2,1,0:T(8,128)S(1)}, u32[]{:S(2)}) copy-start(f32[5,16,16,256]{3,2,1,0:T(8,128)S(1)} %collective-permute-done.7.refs_2_) | copy-start | bytes 3932164
  96.9 320.9 %collective-permute-start = (f32[5,4,256,256]{3,2,1,0:T(8,128)}, f32[5,4,256,256]{3,2,1,0:T(8,128)}, u32[]{:S(2)}, u32[]{:S(2)}) collective-permute-start(f32[5,4,256,256]{3,2,1,0:T(8,128)} %get-tuple-element.55), channel_id=1, source_target_pairs={{0,8},{8,0},{16,24},{24,16},{1,9},{9,1},{17,25},{25,17},{2,10},{10... | collective-permute-start | bytes 15728648 | tf_op jit(solution)/shard_map/ppermute | solution.py:342
  125.0 12.1 %copy-start.10 = (f32[5,16,16,256]{3,2,1,0:T(8,128)}, f32[5,16,16,256]{3,2,1,0:T(8,128)S(1)}, u32[]{:S(2)}) copy-start(f32[5,16,16,256]{3,2,1,0:T(8,128)S(1)} %collective-permute-done.8.refs_3_) | copy-start | bytes 3932164
  125.0 292.8 %collective-permute-start.1 = (f32[5,4,256,256]{3,2,1,0:T(8,128)}, f32[5,4,256,256]{3,2,1,0:T(8,128)}, u32[]{:S(2)}, u32[]{:S(2)}) collective-permute-start(f32[5,4,256,256]{3,2,1,0:T(8,128)} %get-tuple-element.56), channel_id=1, source_target_pairs={{0,16},{8,24},{16,0},{24,8},{1,17},{9,25},{17,1},{25,9},{2,18},{10... | collective-permute-start | bytes 15728648 | tf_op jit(solution)/shard_map/ppermute | solution.py:342
  125.2 32.2 %copy-start.14 = (f32[5,16,16,256]{3,2,1,0:T(8,128)S(1)}, f32[5,16,16,256]{3,2,1,0:T(8,128)}, u32[]{:S(2)}) copy-start(f32[5,16,16,256]{3,2,1,0:T(8,128)} %get-tuple-element.72) | copy-start | bytes 3932164
  125.2 296.3 %collective-permute-start.2 = (f32[5,4,256,256]{3,2,1,0:T(8,128)}, f32[5,4,256,256]{3,2,1,0:T(8,128)}, u32[]{:S(2)}, u32[]{:S(2)}) collective-permute-start(f32[5,4,256,256]{3,2,1,0:T(8,128)} %get-tuple-element.57), channel_id=1, source_target_pairs={{0,24},{8,16},{16,8},{24,0},{1,25},{9,17},{17,9},{25,1},{2,26},{10... | collective-permute-start | bytes 15728648 | tf_op jit(solution)/shard_map/ppermute | solution.py:342
  137.1 78.6 %copy-start.6 = (s32[8]{0:T(128)S(1)}, s32[8]{0:T(128)}, u32[]{:S(2)}) copy-start(s32[8]{0:T(128)} %stack.64.order) | copy-start | bytes 100
  157.4 84.6 %collective-permute-start.12 = (f32[5,16,16,256]{3,2,1,0:T(8,128)S(1)}, f32[5,16,16,256]{3,2,1,0:T(8,128)S(1)}, u32[]{:S(2)}, u32[]{:S(2)}) collective-permute-start(f32[5,16,16,256]{3,2,1,0:T(8,128)S(1)} %copy-done.14), channel_id=1, source_target_pairs={{0,7},{1,6},{2,5},{3,4},{4,3},{5,2},{6,1},{7,0},{8,15},{9,14},{10,... | collective-permute-start | bytes 3932168 | tf_op jit(solution)/shard_map/ppermute | solution.py:342
  213.6 28.4 %collective-permute-start.20 = (f32[5,16,16,256]{3,2,1,0:T(8,128)}, f32[5,16,16,256]{3,2,1,0:T(8,128)S(1)}, u32[]{:S(2)}, u32[]{:S(2)}) collective-permute-start(f32[5,16,16,256]{3,2,1,0:T(8,128)} %get-tuple-element.85), channel_id=1, source_target_pairs={{0,1},{1,0},{2,3},{3,2},{4,5},{5,4},{6,7},{7,6},{8,9},{9,8},{10,11... | collective-permute-start | bytes 3932168 | tf_op jit(solution)/shard_map/ppermute | solution.py:342
  215.6 30.5 %copy-start.5 = (f32[128,128]{1,0:T(8,128)S(1)}, f32[128,128]{1,0:T(8,128)}, u32[]{:S(2)}) copy-start(f32[128,128]{1,0:T(8,128)} %param.14) | copy-start | bytes 196612
  242.0 3.2 copy-start.13
  242.0 30.1 %collective-permute-start.21 = (f32[5,16,16,256]{3,2,1,0:T(8,128)}, f32[5,16,16,256]{3,2,1,0:T(8,128)}, u32[]{:S(2)}, u32[]{:S(2)}) collective-permute-start(f32[5,16,16,256]{3,2,1,0:T(8,128)} %get-tuple-element.86), channel_id=1, source_target_pairs={{0,2},{1,3},{2,0},{3,1},{4,6},{5,7},{6,4},{7,5},{8,10},{9,11},{10,... | collective-permute-start | bytes 3932168 | tf_op jit(solution)/shard_map/ppermute | solution.py:342
  243.2 81.7 %collective-permute-start.22 = (f32[5,16,16,256]{3,2,1,0:T(8,128)}, f32[5,16,16,256]{3,2,1,0:T(8,128)}, u32[]{:S(2)}, u32[]{:S(2)}) collective-permute-start(f32[5,16,16,256]{3,2,1,0:T(8,128)} %get-tuple-element.87), channel_id=1, source_target_pairs={{0,3},{1,2},{2,1},{3,0},{4,7},{5,6},{6,5},{7,4},{8,11},{9,10},{10,... | collective-permute-start | bytes 3932168 | tf_op jit(solution)/shard_map/ppermute | solution.py:342
  249.4 75.5 %copy-start.12 = (f32[5,16,16,256]{3,2,1,0:T(8,128)S(1)}, f32[5,16,16,256]{3,2,1,0:T(8,128)}, u32[]{:S(2)}) copy-start(f32[5,16,16,256]{3,2,1,0:T(8,128)} %get-tuple-element.89) | copy-start | bytes 3932164
  249.4 78.4 %copy-start.7 = (f32[1024]{0:T(1024)S(1)}, f32[1024]{0:T(1024)}, u32[]{:S(2)}) copy-start(f32[1024]{0:T(1024)} %param.15) | copy-start | bytes 12292
  272.2 87.6 %collective-permute-start.23 = (f32[5,16,16,256]{3,2,1,0:T(8,128)}, f32[5,16,16,256]{3,2,1,0:T(8,128)}, u32[]{:S(2)}, u32[]{:S(2)}) collective-permute-start(f32[5,16,16,256]{3,2,1,0:T(8,128)} %get-tuple-element.88), channel_id=1, source_target_pairs={{0,4},{1,5},{2,6},{3,7},{4,0},{5,1},{6,2},{7,3},{8,12},{9,13},{10,... | collective-permute-start | bytes 3932168 | tf_op jit(solution)/shard_map/ppermute | solution.py:342
  324.9 91.0 %collective-permute-start.24 = (f32[5,16,16,256]{3,2,1,0:T(8,128)S(1)}, f32[5,16,16,256]{3,2,1,0:T(8,128)}, u32[]{:S(2)}, u32[]{:S(2)}) collective-permute-start(f32[5,16,16,256]{3,2,1,0:T(8,128)S(1)} %copy-done.12), channel_id=1, source_target_pairs={{0,5},{1,4},{2,7},{3,6},{4,1},{5,0},{6,3},{7,2},{8,13},{9,12},{10,... | collective-permute-start | bytes 3932168 | tf_op jit(solution)/shard_map/ppermute | solution.py:342
  335.8 24.1 %copy-start.11 = (f32[5,16,16,256]{3,2,1,0:T(8,128)S(1)}, f32[5,16,16,256]{3,2,1,0:T(8,128)}, u32[]{:S(2)}) copy-start(f32[5,16,16,256]{3,2,1,0:T(8,128)} %get-tuple-element.90) | copy-start | bytes 3932164
  359.8 135.9 %collective-permute-start.25 = (f32[5,16,16,256]{3,2,1,0:T(8,128)S(1)}, f32[5,16,16,256]{3,2,1,0:T(8,128)S(1)}, u32[]{:S(2)}, u32[]{:S(2)}) collective-permute-start(f32[5,16,16,256]{3,2,1,0:T(8,128)S(1)} %copy-done.11), channel_id=1, source_target_pairs={{0,6},{1,7},{2,4},{3,5},{4,2},{5,3},{6,0},{7,1},{8,14},{9,15},{10,... | collective-permute-start | bytes 3932168 | tf_op jit(solution)/shard_map/ppermute | solution.py:342
  415.9 85.8 %collective-permute-start.26 = (f32[5,16,16,256]{3,2,1,0:T(8,128)}, f32[5,16,16,256]{3,2,1,0:T(8,128)}, u32[]{:S(2)}, u32[]{:S(2)}) collective-permute-start(f32[5,16,16,256]{3,2,1,0:T(8,128)} %get-tuple-element.91), channel_id=1, source_target_pairs={{0,7},{1,6},{2,5},{3,4},{4,3},{5,2},{6,1},{7,0},{8,15},{9,14},{10,... | collective-permute-start | bytes 3932168 | tf_op jit(solution)/shard_map/ppermute | solution.py:342
  417.8 84.1 %collective-permute-start.13 = (f32[5,16,16,256]{3,2,1,0:T(8,128)}, f32[5,16,16,256]{3,2,1,0:T(8,128)S(1)}, u32[]{:S(2)}, u32[]{:S(2)}) collective-permute-start(f32[5,16,16,256]{3,2,1,0:T(8,128)} %get-tuple-element.74), channel_id=1, source_target_pairs={{0,1},{1,0},{2,3},{3,2},{4,5},{5,4},{6,7},{7,6},{8,9},{9,8},{10,11... | collective-permute-start | bytes 3932168 | tf_op jit(solution)/shard_map/ppermute | solution.py:342
  417.8 85.3 %collective-permute-start.14 = (f32[5,16,16,256]{3,2,1,0:T(8,128)}, f32[5,16,16,256]{3,2,1,0:T(8,128)S(1)}, u32[]{:S(2)}, u32[]{:S(2)}) collective-permute-start(f32[5,16,16,256]{3,2,1,0:T(8,128)} %get-tuple-element.75), channel_id=1, source_target_pairs={{0,2},{1,3},{2,0},{3,1},{4,6},{5,7},{6,4},{7,5},{8,10},{9,11},{10,... | collective-permute-start | bytes 3932168 | tf_op jit(solution)/shard_map/ppermute | solution.py:342
  421.6 84.9 %collective-permute-start.15 = (f32[5,16,16,256]{3,2,1,0:T(8,128)}, f32[5,16,16,256]{3,2,1,0:T(8,128)}, u32[]{:S(2)}, u32[]{:S(2)}) collective-permute-start(f32[5,16,16,256]{3,2,1,0:T(8,128)} %get-tuple-element.76), channel_id=1, source_target_pairs={{0,3},{1,2},{2,1},{3,0},{4,7},{5,6},{6,5},{7,4},{8,11},{9,10},{10,... | collective-permute-start | bytes 3932168 | tf_op jit(solution)/shard_map/ppermute | solution.py:342
  496.8 264.4 %collective-permute-start.3 = (f32[5,4,256,256]{3,2,1,0:T(8,128)}, f32[5,4,256,256]{3,2,1,0:T(8,128)S(1)}, u32[]{:S(2)}, u32[]{:S(2)}) collective-permute-start(f32[5,4,256,256]{3,2,1,0:T(8,128)} %get-tuple-element.59), channel_id=1, source_target_pairs={{0,8},{8,0},{16,24},{24,16},{1,9},{9,1},{17,25},{25,17},{2,10},{10... | collective-permute-start | bytes 15728648 | tf_op jit(solution)/shard_map/ppermute | solution.py:342
  501.7 263.4 %collective-permute-start.4 = (f32[5,4,256,256]{3,2,1,0:T(8,128)}, f32[5,4,256,256]{3,2,1,0:T(8,128)}, u32[]{:S(2)}, u32[]{:S(2)}) collective-permute-start(f32[5,4,256,256]{3,2,1,0:T(8,128)} %get-tuple-element.60), channel_id=1, source_target_pairs={{0,16},{8,24},{16,0},{24,8},{1,17},{9,25},{17,1},{25,9},{2,18},{10... | collective-permute-start | bytes 15728648 | tf_op jit(solution)/shard_map/ppermute | solution.py:342
  501.9 158.4 %copy-start.1 = (f32[5,16,16,256]{3,2,1,0:T(8,128)}, f32[5,16,16,256]{3,2,1,0:T(8,128)S(1)}, u32[]{:S(2)}) copy-start(f32[5,16,16,256]{3,2,1,0:T(8,128)S(1)} %collective-permute-done.13.refs_1_) | copy-start | bytes 3932164
  501.9 263.5 %collective-permute-start.5 = (f32[5,4,256,256]{3,2,1,0:T(8,128)}, f32[5,4,256,256]{3,2,1,0:T(8,128)}, u32[]{:S(2)}, u32[]{:S(2)}) collective-permute-start(f32[5,4,256,256]{3,2,1,0:T(8,128)} %get-tuple-element.61), channel_id=1, source_target_pairs={{0,24},{8,16},{16,8},{24,0},{1,25},{9,17},{17,9},{25,1},{2,26},{10... | collective-permute-start | bytes 15728648 | tf_op jit(solution)/shard_map/ppermute | solution.py:342
  503.1 157.2 %copy-start.2 = (f32[5,16,16,256]{3,2,1,0:T(8,128)}, f32[5,16,16,256]{3,2,1,0:T(8,128)S(1)}, u32[]{:S(2)}) copy-start(f32[5,16,16,256]{3,2,1,0:T(8,128)S(1)} %collective-permute-done.14.refs_2_) | copy-start | bytes 3932164
  503.2 84.8 %collective-permute-start.16 = (f32[5,16,16,256]{3,2,1,0:T(8,128)}, f32[5,16,16,256]{3,2,1,0:T(8,128)}, u32[]{:S(2)}, u32[]{:S(2)}) collective-permute-start(f32[5,16,16,256]{3,2,1,0:T(8,128)} %get-tuple-element.77), channel_id=1, source_target_pairs={{0,4},{1,5},{2,6},{3,7},{4,0},{5,1},{6,2},{7,3},{8,12},{9,13},{10,... | collective-permute-start | bytes 3932168 | tf_op jit(solution)/shard_map/ppermute | solution.py:342
  506.5 137.7 %collective-permute-start.17 = (f32[5,16,16,256]{3,2,1,0:T(8,128)}, f32[5,16,16,256]{3,2,1,0:T(8,128)}, u32[]{:S(2)}, u32[]{:S(2)}) collective-permute-start(f32[5,16,16,256]{3,2,1,0:T(8,128)} %get-tuple-element.78), channel_id=1, source_target_pairs={{0,5},{1,4},{2,7},{3,6},{4,1},{5,0},{6,3},{7,2},{8,13},{9,12},{10,... | collective-permute-start | bytes 3932168 | tf_op jit(solution)/shard_map/ppermute | solution.py:342
  588.0 114.2 %collective-permute-start.18 = (f32[5,16,16,256]{3,2,1,0:T(8,128)}, f32[5,16,16,256]{3,2,1,0:T(8,128)}, u32[]{:S(2)}, u32[]{:S(2)}) collective-permute-start(f32[5,16,16,256]{3,2,1,0:T(8,128)} %get-tuple-element.79), channel_id=1, source_target_pairs={{0,6},{1,7},{2,4},{3,5},{4,2},{5,3},{6,0},{7,1},{8,14},{9,15},{10,... | collective-permute-start | bytes 3932168 | tf_op jit(solution)/shard_map/ppermute | solution.py:342
  644.2 86.3 %collective-permute-start.19 = (f32[5,16,16,256]{3,2,1,0:T(8,128)}, f32[5,16,16,256]{3,2,1,0:T(8,128)}, u32[]{:S(2)}, u32[]{:S(2)}) collective-permute-start(f32[5,16,16,256]{3,2,1,0:T(8,128)} %get-tuple-element.80), channel_id=1, source_target_pairs={{0,7},{1,6},{2,5},{3,4},{4,3},{5,2},{6,1},{7,0},{8,15},{9,14},{10,... | collective-permute-start | bytes 3932168 | tf_op jit(solution)/shard_map/ppermute | solution.py:342
  702.2 28.3 %collective-permute-start.27 = (f32[5,16,16,256]{3,2,1,0:T(8,128)}, f32[5,16,16,256]{3,2,1,0:T(8,128)S(1)}, u32[]{:S(2)}, u32[]{:S(2)}) collective-permute-start(f32[5,16,16,256]{3,2,1,0:T(8,128)} %get-tuple-element.93), channel_id=1, source_target_pairs={{0,1},{1,0},{2,3},{3,2},{4,5},{5,4},{6,7},{7,6},{8,9},{9,8},{10,11... | collective-permute-start | bytes 3932168 | tf_op jit(solution)/shard_map/ppermute | solution.py:342
  730.5 30.3 %collective-permute-start.28 = (f32[5,16,16,256]{3,2,1,0:T(8,128)}, f32[5,16,16,256]{3,2,1,0:T(8,128)S(1)}, u32[]{:S(2)}, u32[]{:S(2)}) collective-permute-start(f32[5,16,16,256]{3,2,1,0:T(8,128)} %get-tuple-element.94), channel_id=1, source_target_pairs={{0,2},{1,3},{2,0},{3,1},{4,6},{5,7},{6,4},{7,5},{8,10},{9,11},{10,... | collective-permute-start | bytes 3932168 | tf_op jit(solution)/shard_map/ppermute | solution.py:342
  730.5 84.3 %copy-start.3 = (f32[5,16,16,256]{3,2,1,0:T(8,128)}, f32[5,16,16,256]{3,2,1,0:T(8,128)S(1)}, u32[]{:S(2)}) copy-start(f32[5,16,16,256]{3,2,1,0:T(8,128)S(1)} %collective-permute-done.27.refs_1_) | copy-start | bytes 3932164
  730.5 97.6 %collective-permute-start.29 = (f32[5,16,16,256]{3,2,1,0:T(8,128)}, f32[5,16,16,256]{3,2,1,0:T(8,128)}, u32[]{:S(2)}, u32[]{:S(2)}) collective-permute-start(f32[5,16,16,256]{3,2,1,0:T(8,128)} %get-tuple-element.95), channel_id=1, source_target_pairs={{0,3},{1,2},{2,1},{3,0},{4,7},{5,6},{6,5},{7,4},{8,11},{9,10},{10,... | collective-permute-start | bytes 3932168 | tf_op jit(solution)/shard_map/ppermute | solution.py:342
  760.8 54.0 %copy-start.4 = (f32[5,16,16,256]{3,2,1,0:T(8,128)}, f32[5,16,16,256]{3,2,1,0:T(8,128)S(1)}, u32[]{:S(2)}) copy-start(f32[5,16,16,256]{3,2,1,0:T(8,128)S(1)} %collective-permute-done.28.refs_2_) | copy-start | bytes 3932164
  760.8 67.3 %collective-permute-start.30 = (f32[5,16,16,256]{3,2,1,0:T(8,128)}, f32[5,16,16,256]{3,2,1,0:T(8,128)}, u32[]{:S(2)}, u32[]{:S(2)}) collective-permute-start(f32[5,16,16,256]{3,2,1,0:T(8,128)} %get-tuple-element.96), channel_id=1, source_target_pairs={{0,4},{1,5},{2,6},{3,7},{4,0},{5,1},{6,2},{7,3},{8,12},{9,13},{10,... | collective-permute-start | bytes 3932168 | tf_op jit(solution)/shard_map/ppermute | solution.py:342
  761.2 4.2 copy-start
  761.2 167.8 %collective-permute-start.31 = (f32[5,16,16,256]{3,2,1,0:T(8,128)}, f32[5,16,16,256]{3,2,1,0:T(8,128)}, u32[]{:S(2)}, u32[]{:S(2)}) collective-permute-start(f32[5,16,16,256]{3,2,1,0:T(8,128)} %get-tuple-element.97), channel_id=1, source_target_pairs={{0,5},{1,4},{2,7},{3,6},{4,1},{5,0},{6,3},{7,2},{8,13},{9,12},{10,... | collective-permute-start | bytes 3932168 | tf_op jit(solution)/shard_map/ppermute | solution.py:342
  765.1 194.0 %collective-permute-start.32 = (f32[5,16,16,256]{3,2,1,0:T(8,128)}, f32[5,16,16,256]{3,2,1,0:T(8,128)}, u32[]{:S(2)}, u32[]{:S(2)}) collective-permute-start(f32[5,16,16,256]{3,2,1,0:T(8,128)} %get-tuple-element.98), channel_id=1, source_target_pairs={{0,6},{1,7},{2,4},{3,5},{4,2},{5,3},{6,0},{7,1},{8,14},{9,15},{10,... | collective-permute-start | bytes 3932168 | tf_op jit(solution)/shard_map/ppermute | solution.py:342
  765.4 223.0 %collective-permute-start.33 = (f32[5,16,16,256]{3,2,1,0:T(8,128)}, f32[5,16,16,256]{3,2,1,0:T(8,128)}, u32[]{:S(2)}, u32[]{:S(2)}) collective-permute-start(f32[5,16,16,256]{3,2,1,0:T(8,128)} %get-tuple-element.99), channel_id=1, source_target_pairs={{0,7},{1,6},{2,5},{3,4},{4,3},{5,2},{6,1},{7,0},{8,15},{9,14},{10,... | collective-permute-start | bytes 3932168 | tf_op jit(solution)/shard_map/ppermute | solution.py:342
  (2 other events, 2.2 us)
